TPU v7x, 128 devices: a whole 4x4x4 slice. The times are simulated.
128 devices in a mesh: section: 2 (over x_lo), dp: 16 (over x_hi, z, core), tensor: 4 (over y).
Axes of the slice: x: 4 (x_hi: 2, x_lo: 2; x = x_hi * 2 + x_lo), y: 4, z: 4, core: 2. Of those that a mesh axis runs over, the one named last changes fastest.
Arguments:
- stream_in: bfloat16 [32, 640, 1024], P('dp', 'tensor'), may hold values from -6 to 6
- cotangent: bfloat16 [32, 640, 1024], P('dp', 'tensor'), may hold values from -6 to 6
- mixer_gain: bfloat16 [2, 1024], P('section'), may hold values from 0.5 to 1.5
- mamba_in: bfloat16 [2, 1024, 2, 1536], P('section', None, None, 'tensor'), may hold values from -0.1875 to 0.1875
- state_in: bfloat16 [2, 1024, 256], P('section'), may hold values from -0.1875 to 0.1875
- step_in: bfloat16 [2, 1024, 24], P('section', None, 'tensor'), may hold values from -0.1875 to 0.1875
- mamba_conv: bfloat16 [2, 4, 1536], P('section', None, 'tensor'), may hold values from -3 to 3
- state_conv: bfloat16 [2, 4, 256], P('section'), may hold values from -3 to 3
- step_bias: float32 [2, 24], P('section', 'tensor'), may hold values from -4 to -1.5
- decay_log: float32 [2, 24], P('section', 'tensor'), may hold values from -1 to 1
- skip_gain: float32 [2, 24], P('section', 'tensor'), may hold values from 0.5 to 1.5
- query_in: bfloat16 [2, 1024, 512], P('section', None, 'tensor'), may hold values from -0.1875 to 0.1875
- keyval_in: bfloat16 [2, 1024, 2, 128], P('section'), may hold values from -0.1875 to 0.1875
- mamba_out: bfloat16 [2, 1536, 1024], P('section', 'tensor'), may hold values from -0.0390625 to 0.0390625
- attention_out: bfloat16 [2, 512, 1024], P('section', 'tensor'), may hold values from -0.5 to 0.5
- feed_gain: bfloat16 [2, 1024], P('section'), may hold values from 0.5 to 1.5
- gate_up: bfloat16 [2, 1024, 2, 2048], P('section', None, None, 'tensor'), may hold values from -0.1875 to 0.1875
- down_weight: bfloat16 [2, 2048, 1024], P('section', 'tensor'), may hold values from -0.125 to 0.125
Outputs:
- section_output: float32 [2, 32, 640, 1024], P('section', 'dp', 'tensor')
- input_grad: float32 [2, 32, 640, 1024], P('section', 'dp', 'tensor')
- grad_mixer_gain: float32 [2, 1024], P('section', ('dp', 'tensor'))
- grad_mamba_in: float32 [2, 1024, 2, 1536], P('section', 'dp', None, 'tensor')
- grad_state_in: float32 [2, 1024, 256], P('section', ('dp', 'tensor'))
- grad_step_in: float32 [2, 1024, 24], P('section', 'dp', 'tensor')
- grad_mamba_conv: float32 [2, 4, 1536], P('section', None, 'tensor')
- grad_state_conv: float32 [2, 4, 256], P('section', None, ('dp', 'tensor'))
- grad_step_bias: float32 [2, 24], P('section', 'tensor')
- grad_decay_log: float32 [2, 24], P('section', 'tensor')
- grad_skip_gain: float32 [2, 24], P('section', 'tensor')
- grad_query_in: float32 [2, 1024, 512], P('section', 'dp', 'tensor')
- grad_keyval_in: float32 [2, 1024, 2, 128], P('section', ('dp', 'tensor'))
- grad_mamba_out: float32 [2, 1536, 1024], P('section', 'tensor', 'dp')
- grad_attention_out: float32 [2, 512, 1024], P('section', 'tensor', 'dp')
- grad_feed_gain: float32 [2, 1024], P('section', ('dp', 'tensor'))
- grad_gate_up: float32 [2, 1024, 2, 2048], P('section', 'dp', None, 'tensor')
- grad_down_weight: float32 [2, 2048, 1024], P('section', 'tensor', 'dp')
All inputs are finite; a program needn't handle non-finite values.
Results may differ from a plain program's by a relative error of at most 0.024.
Values may be sent and summed in bfloat16 or wider, within the bound.
A program may use at most 256 MiB of HBM per device.

v0:
```python
from functools import partial

import jax
import jax.numpy as jnp
from jax import lax
from jax.sharding import PartitionSpec as P

ATT_HEADS = 8
KV_HEADS = 2
HEAD_DIM = 64


rope_base = 100000000000.0
norm_eps = 1e-05


def passed_along(shard, axis, by):
    devices = lax.axis_size(axis)
    pairs = [(i, i + by) for i in range(devices) if 0 <= i + by < devices]
    return lax.ppermute(shard, axis, pairs)


def rms_norm(values, gain_vector):
    inverse_rms = lax.rsqrt(jnp.mean(values * values, axis=-1, keepdims=True) + norm_eps)
    return values * inverse_rms * gain_vector


def causal_conv(signal, kernel):
    kernel_size = kernel.shape[0]
    length = signal.shape[0]
    padded = jnp.pad(signal, ((kernel_size - 1, 0), (0, 0)))
    running = padded[0:length] * kernel[0]
    for offset in range(1, kernel_size):
        running = running + padded[offset : offset + length] * kernel[offset]
    return running


def rotate(values):
    length = values.shape[0]
    half_size = values.shape[-1] // 2
    exponents = jnp.arange(half_size, dtype=jnp.float32) * (-2.0 / values.shape[-1])
    frequency = jnp.power(rope_base, exponents)
    angles = jnp.arange(length, dtype=jnp.float32)[:, None] * frequency[None, :]
    cosine = jnp.cos(angles)[:, None, :]
    sine_part = jnp.sin(angles)[:, None, :]
    first_half = values[..., :half_size]
    second_half = values[..., half_size:]
    return jnp.concatenate(
        [
            first_half * cosine - second_half * sine_part,
            second_half * cosine + first_half * sine_part,
        ],
        axis=-1,
    )


def attention(queries, key_heads, value_heads):
    group_size = queries.shape[1] // key_heads.shape[1]
    keys_all = jnp.repeat(key_heads, group_size, axis=1)
    values_all = jnp.repeat(value_heads, group_size, axis=1)
    length = queries.shape[0]
    scores = jnp.einsum(
        "thd,shd->hts", queries, keys_all, precision=lax.Precision.HIGHEST
    ) * queries.shape[-1] ** (-0.5)
    causal = lax.broadcasted_iota(jnp.int32, (length, length), 0) >= lax.broadcasted_iota(
        jnp.int32, (length, length), 1
    )
    scores = jnp.where(causal[None], scores, -1e30)
    row_max = jnp.max(scores, axis=-1, keepdims=True)
    weights = jnp.exp(scores - row_max)
    weights = weights / jnp.sum(weights, axis=-1, keepdims=True)
    return jnp.einsum("hts,shd->thd", weights, values_all, precision=lax.Precision.HIGHEST)


def state_mix(inputs, state_inputs, state_reads, step_size, decay_log, skip_gain):
    length = inputs.shape[0]
    log_decay = -step_size * jnp.exp(decay_log)[None, :]
    running = jnp.cumsum(log_decay, axis=0)
    causal = lax.broadcasted_iota(jnp.int32, (length, length), 0) >= lax.broadcasted_iota(
        jnp.int32, (length, length), 1
    )
    decay_gap = running[:, None, :] - running[None, :, :]
    decays = jnp.exp(jnp.where(causal[:, :, None], decay_gap, -jnp.inf))
    intersection = jnp.dot(
        state_reads,
        state_inputs.T,
        precision=lax.Precision.HIGHEST,
        preferred_element_type=jnp.float32,
    )
    mixing = intersection[:, :, None] * decays * step_size[None, :, :]
    mixed = jnp.einsum("tsh,shp->thp", mixing, inputs, precision=lax.Precision.HIGHEST)
    return mixed + skip_gain[None, :, None] * inputs


def mixer_core(
    mamba_proj,
    state_proj,
    step_proj,
    query_proj,
    keyval_proj,
    mamba_conv,
    state_conv,
    step_bias,
    decay_log,
    skip_gain,
):
    length = mamba_proj.shape[0]
    head_count = step_proj.shape[1]
    gate_part = mamba_proj[:, 0]
    conv_input = jax.nn.silu(causal_conv(mamba_proj[:, 1], mamba_conv))
    conv_state = jax.nn.silu(causal_conv(state_proj, state_conv))
    state_size = state_proj.shape[1] // 2
    step_size = jax.nn.softplus(step_proj + step_bias)
    mixed = state_mix(
        conv_input.reshape(length, head_count, -1),
        conv_state[:, :state_size],
        conv_state[:, state_size:],
        step_size,
        decay_log,
        skip_gain,
    )
    gated_out = mixed.reshape(length, -1) * jax.nn.silu(gate_part)
    queries = rotate(query_proj.reshape(length, -1, HEAD_DIM))
    key_heads = rotate(keyval_proj[:, 0].reshape(length, -1, HEAD_DIM))
    value_heads = keyval_proj[:, 1].reshape(length, -1, HEAD_DIM)
    attended = jax.checkpoint(attention)(queries, key_heads, value_heads).reshape(length, -1)
    return (gated_out, attended)


def swiglu(gate_values):
    return jax.nn.silu(gate_values[:, 0]) * gate_values[:, 1]


def product(left, right, flipped):
    if flipped:
        return lax.dot_general(
            left, right, (((1,), (1,)), ((), ())), preferred_element_type=jnp.float32
        )
    return jnp.dot(left, right, preferred_element_type=jnp.float32)


def outer_sum(left, right):
    return lax.dot_general(
        left, right, (((0,), (0,)), ((), ())), preferred_element_type=jnp.float32
    )


def spread(shard):
    return lax.all_gather(shard, "tensor", axis=0, tiled=True)


def reduce_rows(terms):
    running = None
    for left, right, flipped in terms:
        value = product(left, right, flipped)
        running = value if running is None else running + value
    return lax.psum_scatter(running, "tensor", scatter_dimension=0, tiled=True)


def replica_sum(terms):
    return (
        lax.psum_scatter(terms[0], "dp", scatter_dimension=1, tiled=True),
        lax.psum_scatter(terms[1], "dp", scatter_dimension=1, tiled=True),
        lax.psum_scatter(terms[2], "dp", scatter_dimension=1, tiled=True),
        lax.psum_scatter(terms[3], "dp", scatter_dimension=2, tiled=True),
        lax.psum_scatter(terms[4], "dp", scatter_dimension=2, tiled=True),
        lax.psum_scatter(terms[5], "dp", scatter_dimension=1, tiled=True),
        lax.psum_scatter(terms[6], "dp", scatter_dimension=2, tiled=True),
    )


def replica_terms(products, model_width):
    return (
        products[0].reshape(model_width, 2, -1)[None],
        products[2][None],
        products[3][None],
        products[5][None],
        products[6][None],
        products[7].reshape(model_width, 2, -1)[None],
        products[8][None],
    )


def weight_products(operands):
    (
        normed_full,
        mamba_grad,
        state_grad,
        step_grad,
        query_grad,
        keyval_grad,
        gated_low,
        attended_low,
        branch_grad,
        normed_two_full,
        gate_grad,
        activated_low,
        feed_grad,
    ) = operands
    return (
        outer_sum(normed_full, mamba_grad),
        outer_sum(normed_full, state_grad),
        outer_sum(normed_full, step_grad),
        outer_sum(normed_full, query_grad),
        outer_sum(normed_full, keyval_grad),
        outer_sum(gated_low, branch_grad),
        outer_sum(attended_low, branch_grad),
        outer_sum(normed_two_full, gate_grad),
        outer_sum(activated_low, feed_grad),
    )


def accumulate(running, addition):
    if running is None:
        return addition
    return jax.tree.map(jnp.add, running, addition)


def per_device(
    stream_in,
    cotangent,
    mixer_gain,
    mamba_in,
    state_in,
    step_in,
    mamba_conv,
    state_conv,
    step_bias,
    decay_log,
    skip_gain,
    query_in,
    keyval_in,
    mamba_out,
    attention_out,
    feed_gain,
    gate_up,
    down_weight,
):
    is_first = lax.axis_index("section") == 0
    micro_count = stream_in.shape[0]
    shard_rows = stream_in.shape[1]
    model_width = stream_in.shape[2]
    heads_local = query_in.shape[2] // HEAD_DIM
    group_size = ATT_HEADS // KV_HEADS
    kv_index = lax.axis_index("tensor") * heads_local // group_size
    mixer_gain_f = mixer_gain[0].astype(jnp.float32)
    feed_gain_f = feed_gain[0].astype(jnp.float32)
    mamba_flat = mamba_in[0].reshape(model_width, -1)
    state_flat = state_in[0]
    step_flat = step_in[0]
    query_flat = query_in[0]
    keyval_local = lax.dynamic_slice_in_dim(keyval_in[0], kv_index * HEAD_DIM, HEAD_DIM, 2)
    keyval_flat = keyval_local.reshape(model_width, -1)
    mamba_back = mamba_out[0]
    attention_back = attention_out[0]
    gate_flat = gate_up[0].reshape(model_width, -1)
    down_flat = down_weight[0]
    conv_mamba_f = mamba_conv[0].astype(jnp.float32)
    conv_state_f = state_conv[0].astype(jnp.float32)
    bias_f = step_bias[0]
    decay_f = decay_log[0]
    skip_f = skip_gain[0]
    zero_rows = jnp.zeros((shard_rows, model_width), jnp.float32)
    received = zero_rows
    outputs = []
    records = []
    for tick_index in range(micro_count + 1):
        own_input = (
            stream_in[tick_index].astype(jnp.float32) if tick_index < micro_count else zero_rows
        )
        forward_hidden = jnp.where(is_first, own_input, received)
        normed = rms_norm(forward_hidden, mixer_gain_f).astype(jnp.bfloat16)
        forward_normed_full = spread(normed)
        forward_length = forward_normed_full.shape[0]
        mamba_proj = product(forward_normed_full, mamba_flat, False).reshape(forward_length, 2, -1)
        state_proj = product(forward_normed_full, state_flat, False)
        step_proj = product(forward_normed_full, step_flat, False)
        query_proj = product(forward_normed_full, query_flat, False)
        keyval_proj = product(forward_normed_full, keyval_flat, False).reshape(
            forward_length, 2, -1
        )
        core_values, forward_core_back = jax.vjp(
            mixer_core,
            mamba_proj,
            state_proj,
            step_proj,
            query_proj,
            keyval_proj,
            conv_mamba_f,
            conv_state_f,
            bias_f,
            decay_f,
            skip_f,
        )
        forward_gated_low = core_values[0].astype(jnp.bfloat16)
        forward_attended_low = core_values[1].astype(jnp.bfloat16)
        branch = reduce_rows(
            ((forward_gated_low, mamba_back, False), (forward_attended_low, attention_back, False))
        )
        forward_middle = forward_hidden + branch
        normed_two = rms_norm(forward_middle, feed_gain_f).astype(jnp.bfloat16)
        forward_normed_two_full = spread(normed_two)
        gate_values = product(forward_normed_two_full, gate_flat, False).reshape(
            forward_length, 2, -1
        )
        activated, forward_swiglu_back = jax.vjp(swiglu, gate_values)
        forward_activated_low = activated.astype(jnp.bfloat16)
        feed = reduce_rows(((forward_activated_low, down_flat, False),))
        forward_record = (
            forward_hidden,
            forward_middle,
            forward_normed_full,
            forward_core_back,
            forward_gated_low,
            forward_attended_low,
            forward_normed_two_full,
            forward_swiglu_back,
            forward_activated_low,
        )
        layer_output = forward_middle + feed
        outputs.append(layer_output)
        records.append(forward_record)
        if tick_index < micro_count:
            received = passed_along(layer_output, "section", 1)
    coming_back = zero_rows
    grads_in = []
    operand_list = []
    small_total = None
    product_total = None
    reduced_total = None
    for tick_index in range(micro_count + 1):
        item_index = micro_count - 1 - tick_index
        own_grad = cotangent[item_index].astype(jnp.float32) if item_index >= 0 else zero_rows
        grad_out = jnp.where(is_first, coming_back, own_grad)
        (
            hidden,
            middle,
            normed_full,
            core_back,
            gated_low,
            attended_low,
            normed_two_full,
            swiglu_back,
            activated_low,
        ) = records[micro_count - tick_index]
        length = normed_full.shape[0]
        feed_grad = spread(grad_out.astype(jnp.bfloat16))
        activated_grad = product(feed_grad, down_flat, True)
        gate_values_grad = swiglu_back(activated_grad)[0]
        gate_grad = gate_values_grad.reshape(length, -1).astype(jnp.bfloat16)
        normed_two_grad = reduce_rows(((gate_grad, gate_flat, True),))
        middle_value, middle_back = jax.vjp(rms_norm, middle, feed_gain_f)
        middle_part, feed_gain_grad = middle_back(normed_two_grad)
        middle_grad = grad_out + middle_part
        branch_grad = spread(middle_grad.astype(jnp.bfloat16))
        core_grads = core_back(
            (product(branch_grad, mamba_back, True), product(branch_grad, attention_back, True))
        )
        mamba_grad = core_grads[0].reshape(length, -1).astype(jnp.bfloat16)
        state_grad = core_grads[1].astype(jnp.bfloat16)
        step_grad = core_grads[2].astype(jnp.bfloat16)
        query_grad = core_grads[3].astype(jnp.bfloat16)
        keyval_grad = core_grads[4].reshape(length, -1).astype(jnp.bfloat16)
        normed_grad = reduce_rows(
            (
                (mamba_grad, mamba_flat, True),
                (state_grad, state_flat, True),
                (step_grad, step_flat, True),
                (query_grad, query_flat, True),
                (keyval_grad, keyval_flat, True),
            )
        )
        hidden_value, hidden_back = jax.vjp(rms_norm, hidden, mixer_gain_f)
        hidden_part, mixer_gain_grad = hidden_back(normed_grad)
        operands = (
            normed_full,
            mamba_grad,
            state_grad,
            step_grad,
            query_grad,
            keyval_grad,
            gated_low,
            attended_low,
            branch_grad,
            normed_two_full,
            gate_grad,
            activated_low,
            feed_grad,
        )
        small_grads = (
            mixer_gain_grad,
            feed_gain_grad,
            core_grads[5],
            core_grads[6],
            core_grads[7],
            core_grads[8],
            core_grads[9],
        )
        grad_in, operands, small_grads = (middle_grad + hidden_part, operands, small_grads)
        small_total = accumulate(small_total, small_grads)
        operand_list.append(operands)
        grads_in.append(grad_in)
        if tick_index < micro_count:
            coming_back = passed_along(grad_in, "section", -1)
    for item_index in range(micro_count):
        chosen = jax.tree.map(
            partial(jnp.where, is_first), operand_list[item_index + 1], operand_list[item_index]
        )
        product_total = accumulate(product_total, weight_products(chosen))
    reduced_total = replica_sum(replica_terms(product_total, model_width))
    keyval_part = product_total[4].reshape(model_width, 2, HEAD_DIM)
    keyval_full = lax.dynamic_update_slice_in_dim(
        jnp.zeros(keyval_in.shape[1:], jnp.float32), keyval_part, kv_index * HEAD_DIM, 2
    )
    shared = (
        lax.psum_scatter(small_total[0][None], ("dp", "tensor"), scatter_dimension=1, tiled=True),
        lax.psum_scatter(product_total[1][None], ("dp", "tensor"), scatter_dimension=1, tiled=True),
        lax.psum_scatter(keyval_full[None], ("dp", "tensor"), scatter_dimension=1, tiled=True),
        lax.psum_scatter(small_total[3][None], ("dp", "tensor"), scatter_dimension=2, tiled=True),
        lax.psum_scatter(small_total[1][None], ("dp", "tensor"), scatter_dimension=1, tiled=True),
    )
    small = lax.psum(
        (small_total[2][None], small_total[4][None], small_total[5][None], small_total[6][None]),
        "dp",
    )
    section_output = jnp.stack(
        [
            jnp.where(is_first, outputs[item_index], outputs[item_index + 1])
            for item_index in range(micro_count)
        ]
    )[None]
    input_grad = jnp.stack(
        [
            jnp.where(
                is_first, grads_in[micro_count - item_index], grads_in[micro_count - 1 - item_index]
            )
            for item_index in range(micro_count)
        ]
    )[None]
    return (
        section_output,
        input_grad,
        shared[0],
        reduced_total[0],
        shared[1],
        reduced_total[1],
        small[0],
        shared[3],
        small[1],
        small[2],
        small[3],
        reduced_total[2],
        shared[2],
        reduced_total[3],
        reduced_total[4],
        shared[4],
        reduced_total[5],
        reduced_total[6],
    )


def solution(mesh):
    in_specs = (
        P("dp", "tensor", None),
        P("dp", "tensor", None),
        P("section", None),
        P("section", None, None, "tensor"),
        P("section", None, None),
        P("section", None, "tensor"),
        P("section", None, "tensor"),
        P("section", None, None),
        P("section", "tensor"),
        P("section", "tensor"),
        P("section", "tensor"),
        P("section", None, "tensor"),
        P("section", None, None, None),
        P("section", "tensor", None),
        P("section", "tensor", None),
        P("section", None),
        P("section", None, None, "tensor"),
        P("section", "tensor", None),
    )
    out_specs = (
        P("section", "dp", "tensor", None),
        P("section", "dp", "tensor", None),
        P("section", ("dp", "tensor")),
        P("section", "dp", None, "tensor"),
        P("section", ("dp", "tensor"), None),
        P("section", "dp", "tensor"),
        P("section", None, "tensor"),
        P("section", None, ("dp", "tensor")),
        P("section", "tensor"),
        P("section", "tensor"),
        P("section", "tensor"),
        P("section", "dp", "tensor"),
        P("section", ("dp", "tensor"), None, None),
        P("section", "tensor", "dp"),
        P("section", "tensor", "dp"),
        P("section", ("dp", "tensor")),
        P("section", "dp", None, "tensor"),
        P("section", "tensor", "dp"),
    )
    return jax.shard_map(
        per_device, mesh=mesh, in_specs=in_specs, out_specs=out_specs, check_vma=False
    )
```

profile of v0, /device:TPU:0, one launch (start us, length us, event | category | flops | bytes accessed | tf_op | source)
XLA Modules:
  0.0 3252.1 jit_solution(5692981392820103290)
XLA Ops:
  27.6 12.2 all-gather.13.cloned.1.call-done
  74.9 26.4 multiply_convert_fusion.8
  113.4 33.4 %reduce-scatter.38.cloned.1.call-done = f32[160,1024]{1,0:T(8,128)} async-done(((f32[640,1024]{1,0:T(8,128)}), f32[160,1024]{1,0:T(8,128)}) %reduce-scatter.38.cloned.1.call-update) | async-done | bytes 655376 | tf_op jit(solution)/shard_map/reduce_scatter | solution.py:157
  158.3 17.3 all-gather.15.cloned.1.call-done
  183.4 34.6 %reduce-scatter.40.cloned.1.call-done = f32[160,1024]{1,0:T(8,128)} async-done(((f32[640,1024]{1,0:T(8,128)}), f32[160,1024]{1,0:T(8,128)}) %reduce-scatter.40.cloned.1.call-update) | async-done | bytes 655376 | tf_op jit(solution)/shard_map/reduce_scatter | solution.py:157
  223.1 13.6 collective-permute-done
  238.3 25.4 all-gather.17.cloned.1.call-done
  298.0 14.8 multiply_convert_fusion.7
  324.2 34.7 %reduce-scatter.42.cloned.1.call-done = f32[160,1024]{1,0:T(8,128)} async-done(((f32[640,1024]{1,0:T(8,128)}), f32[160,1024]{1,0:T(8,128)}) %reduce-scatter.42.cloned.1.call-update) | async-done | bytes 655376 | tf_op jit(solution)/shard_map/reduce_scatter | solution.py:157
  362.2 24.7 all-gather.19.cloned.1.call-done
  394.7 34.6 %reduce-scatter.44.cloned.1.call-done = f32[160,1024]{1,0:T(8,128)} async-done(((f32[640,1024]{1,0:T(8,128)}), f32[160,1024]{1,0:T(8,128)}) %reduce-scatter.44.cloned.1.call-update) | async-done | bytes 655376 | tf_op jit(solution)/shard_map/reduce_scatter | solution.py:157
  434.9 14.0 collective-permute-done.1
  450.1 25.4 all-gather.21.cloned.1.call-done
  510.0 15.0 multiply_convert_fusion.6
  536.6 34.7 %reduce-scatter.46.cloned.1.call-done = f32[160,1024]{1,0:T(8,128)} async-done(((f32[640,1024]{1,0:T(8,128)}), f32[160,1024]{1,0:T(8,128)}) %reduce-scatter.46.cloned.1.call-update) | async-done | bytes 655376 | tf_op jit(solution)/shard_map/reduce_scatter | solution.py:157
  577.1 22.9 all-gather.23.cloned.1.call-done
  600.0 5.3 fusion.199
  605.3 22.3 all-gather.25.cloned.1.call-done
  636.7 34.7 %reduce-scatter.50.cloned.1.call-done = f32[160,1024]{1,0:T(8,128)} async-done(((f32[640,1024]{1,0:T(8,128)}), f32[160,1024]{1,0:T(8,128)}) %reduce-scatter.50.cloned.1.call-update) | async-done | bytes 655376 | tf_op jit(solution)/shard_map/reduce_scatter | solution.py:157
  681.1 20.3 all-gather.27.cloned.1.call-done
  701.4 5.6 multiply_reduce_fusion.8
  709.5 16.6 fusion.22
  741.0 4.9 convert_reduce_fusion.2
  755.4 9.6 fusion.154
  767.5 5.2 multiply_reduce_fusion.19
  773.3 8.9 reduce-window.50
  814.7 30.4 reduce-scatter.52.cloned.1.call-done
  848.2 32.9 %reduce-scatter.48.cloned.1.call-done = f32[160,1024]{1,0:T(8,128)} async-done(((f32[640,1024]{1,0:T(8,128)}), f32[160,1024]{1,0:T(8,128)}) %reduce-scatter.48.cloned.1.call-update) | async-done | bytes 655376 | tf_op jit(solution)/shard_map/reduce_scatter | solution.py:157
  885.5 17.1 collective-permute-done.2
  903.6 24.7 all-gather.29.cloned.1.call-done
  940.1 34.6 %reduce-scatter.54.cloned.1.call-done = f32[160,1024]{1,0:T(8,128)} async-done(((f32[640,1024]{1,0:T(8,128)}), f32[160,1024]{1,0:T(8,128)}) %reduce-scatter.54.cloned.1.call-update) | async-done | bytes 655376 | tf_op jit(solution)/shard_map/reduce_scatter | solution.py:157
  984.5 20.1 all-gather.31.cloned.1.call-done
  1004.6 5.7 multiply_convert_fusion.5
  1012.7 16.3 fusion.24
  1058.1 9.7 fusion.160
  1074.6 7.6 reduce-window.54
  1106.1 34.6 %reduce-scatter.56.cloned.1.call-done = f32[160,1024]{1,0:T(8,128)} async-done(((f32[640,1024]{1,0:T(8,128)}), f32[160,1024]{1,0:T(8,128)}) %reduce-scatter.56.cloned.1.call-update) | async-done | bytes 655376 | tf_op jit(solution)/shard_map/reduce_scatter | solution.py:157
  1146.2 17.1 collective-permute-done.3
  1164.4 24.7 all-gather.33.cloned.1.call-done
  1197.7 34.6 %reduce-scatter.58.cloned.1.call-done = f32[160,1024]{1,0:T(8,128)} async-done(((f32[640,1024]{1,0:T(8,128)}), f32[160,1024]{1,0:T(8,128)}) %reduce-scatter.58.cloned.1.call-update) | async-done | bytes 655376 | tf_op jit(solution)/shard_map/reduce_scatter | solution.py:157
  1241.0 21.0 all-gather.35.cloned.1.call-done
  1261.9 5.4 multiply_reduce_fusion.6
  1269.8 16.6 fusion.26
  1315.5 9.5 fusion.166
  1331.9 7.8 reduce-window.56
  1362.0 5.6 fusion.227
  1368.8 6.4 convolution_add_fusion
  1375.2 7.3 copy.322
  1382.4 5.2 copy.338
  1396.5 32.9 %dynamic_update_slice.4 = f32[1,1024,2,128]{3,2,1,0:T(2,128)} dynamic-update-slice(f32[1,1024,2,128]{3,2,1,0:T(2,128)} %broadcast_in_dim.392, f32[1,1024,2,64]{3,2,1,0:T(2,128)S(1)} %copy.282, s32[]{:T(128)} %constant.99.clone.1, s32[]{:T(128)} %constant.99.clone.1, s32[]{:T(128)} %constant.99.clone.1, s32[]{:T(128)S(6)} %select_n.298) | dynamic-update-slice | bytes 1048580 | tf_op jit(solution)/shard_map/dynamic_update_slice | solution.py:412
  1440.6 6.1 copy.289
  1464.4 4.9 convolution_add_fusion.1
  1469.4 5.9 copy.312
  1501.3 231.0 %reduce-scatter.76.cloned.1.call-done = f32[16,1]{1,0:T(8,128)} async-done(((f32[1024,1]{1,0:T(8,128)}), f32[16,1]{1,0:T(8,128)}) %reduce-scatter.76.cloned.1.call-update) | async-done | bytes 80
  1733.6 78.4 %reduce-scatter.78.cloned.1.call-done = f32[64,1024]{1,0:T(8,128)} async-done(((f32[1024,1024]{1,0:T(8,128)}), f32[64,1024]{1,0:T(8,128)}) %reduce-scatter.78.cloned.1.call-update) | async-done | bytes 262160
  1814.3 164.8 %all-reduce.90 = f32[1,4,256]{2,1,0:T(4,128)S(1)} all-reduce(f32[1,4,256]{2,1,0:T(4,128)S(1)} %add_bitcast_fusion.12), channel_id=18, replica_groups=mesh['section'=2,'dp'=16,'tensor'=4] {'dp','tensor'}, use_global_device_ids=true, to_apply=%region_101.103.clone | all-reduce | flops 1024 | bytes 8192
  1979.3 34.2 %all-reduce.93 = (f32[1,4,384]{2,1,0:T(4,128)}, f32[1,6]{1,0:T(1,128)}, f32[1,6]{1,0:T(1,128)}, f32[1,6]{1,0:T(1,128)}) all-reduce(f32[1,4,384]{2,1,0:T(4,128)S(1)} %add_bitcast_fusion.11, f32[1,6]{1,0:T(1,128)S(1)} %add_bitcast_fusion.14, ...), channel_id=1, replica_groups=mesh['section'=2,'dp'=16,'tensor'=4] {'dp'}, use_global_device_ids=true, to_apply=%region_88.90 | all-reduce | flops 1554 | bytes 12432 | tf_op jit(solution)/shard_map/psum | solution.py:422
  2015.6 199.7 %reduce-scatter.74.cloned.1.call-done = f32[16,256]{1,0:T(8,128)} async-done(((f32[1024,256]{1,0:T(8,128)}), f32[16,256]{1,0:T(8,128)}) %reduce-scatter.74.cloned.1.call-update) | async-done | bytes 16400
  2216.6 144.7 %all-reduce.97.cloned.1.call-done = (f32[1,384,1024]{1,0,2:T(1,128)}, f32[1,512,1024]{1,0,2:T(1,128)}) async-done(((f32[1,384,1024]{1,0,2:T(1,128)}, f32[1,512,1024]{1,0,2:T(1,128)}), (f32[1,384,1024]{1,0,2:T(1,128)}, f32[1,512,1024]{1,0,2:T(1,128)})) %all-reduce.97.cloned.1.call-update) | async-done | bytes 3670032
  2364.5 76.9 %reduce-scatter.70.cloned.1.call-done = f32[64,768]{1,0:T(8,128)} async-done(((f32[1024,768]{1,0:T(8,128)}), f32[64,768]{1,0:T(8,128)}) %reduce-scatter.70.cloned.1.call-update) | async-done | bytes 196624
  2445.6 330.4 %reduce-scatter.68.cloned.1.call-done = f32[16,1]{1,0:T(8,128)} async-done(((f32[1024,1]{1,0:T(8,128)}), f32[16,1]{1,0:T(8,128)}) %reduce-scatter.68.cloned.1.call-update) | async-done | bytes 80
  2777.3 63.2 %reduce-scatter.66.cloned.1.call-done = f32[1,128,64]{1,0,2:T(1,128)} async-done(((f32[1,128,1024]{1,0,2:T(1,128)}), f32[1,128,64]{1,0,2:T(1,128)}) %reduce-scatter.66.cloned.1.call-update) | async-done | bytes 32784 | tf_op jit(solution)/shard_map/reduce_scatter | solution.py:166
  2840.5 68.7 %reduce-scatter.64.cloned.1.call-done = f32[1,64,128]{2,1,0:T(8,128)} async-done(((f32[1,1024,128]{2,1,0:T(8,128)}), f32[1,64,128]{2,1,0:T(8,128)}) %reduce-scatter.64.cloned.1.call-update) | async-done | bytes 32784 | tf_op jit(solution)/shard_map/reduce_scatter | solution.py:164
  2909.2 335.9 %reduce-scatter.62.cloned.1.call-done = f32[1,16,256]{2,1,0:T(8,128)} async-done(((f32[1,1024,256]{2,1,0:T(8,128)}), f32[1,16,256]{2,1,0:T(8,128)}) %reduce-scatter.62.cloned.1.call-update) | async-done | bytes 16400 | tf_op jit(solution)/shard_map/reduce_scatter | solution.py:417
  (1075 shorter events, 542.8 us)
Async XLA Ops:
  7.2 32.6 %all-gather.13.cloned.1.call-start = ((), (), s32[]{:S(2)}) async-start(), calls=%async_computation.21 | async-start | bytes 1638400 | tf_op jit(solution)/shard_map/all_gather | solution.py:149
  12.3 134.5 %reduce-scatter.38.cloned.1.call-start = ((), (), s32[]{:S(2)}) async-start(), calls=%async_computation.22 | async-start | bytes 3276800 | tf_op jit(solution)/shard_map/reduce_scatter | solution.py:157
  112.1 63.5 %all-gather.15.cloned.1.call-start = ((), (), s32[]{:S(2)}) async-start(), calls=%async_computation.23 | async-start | bytes 1638400 | tf_op jit(solution)/shard_map/all_gather | solution.py:149
  150.8 67.3 %reduce-scatter.40.cloned.1.call-start = ((), (), s32[]{:S(2)}) async-start(), calls=%async_computation.24 | async-start | bytes 3276800 | tf_op jit(solution)/shard_map/reduce_scatter | solution.py:157
  183.4 80.4 %all-gather.17.cloned.1.call-start = ((), (), s32[]{:S(2)}) async-start(), calls=%async_computation.25 | async-start | bytes 1638400 | tf_op jit(solution)/shard_map/all_gather | solution.py:149
  219.3 17.4 collective-permute-start
  238.3 120.6 %reduce-scatter.42.cloned.1.call-start = ((), (), s32[]{:S(2)}) async-start(), calls=%async_computation.26 | async-start | bytes 3276800 | tf_op jit(solution)/shard_map/reduce_scatter | solution.py:157
  324.1 62.8 %all-gather.19.cloned.1.call-start = ((), (), s32[]{:S(2)}) async-start(), calls=%async_computation.27 | async-start | bytes 1638400 | tf_op jit(solution)/shard_map/all_gather | solution.py:149
  362.1 67.2 %reduce-scatter.44.cloned.1.call-start = ((), (), s32[]{:S(2)}) async-start(), calls=%async_computation.28 | async-start | bytes 3276800 | tf_op jit(solution)/shard_map/reduce_scatter | solution.py:157
  394.7 80.8 %all-gather.21.cloned.1.call-start = ((), (), s32[]{:S(2)}) async-start(), calls=%async_computation.29 | async-start | bytes 1638400 | tf_op jit(solution)/shard_map/all_gather | solution.py:149
  431.5 17.4 collective-permute-start.1
  450.0 121.3 %reduce-scatter.46.cloned.1.call-start = ((), (), s32[]{:S(2)}) async-start(), calls=%async_computation.30 | async-start | bytes 3276800 | tf_op jit(solution)/shard_map/reduce_scatter | solution.py:157
  536.6 63.4 %all-gather.23.cloned.1.call-start = ((), (), s32[]{:S(2)}) async-start(), calls=%async_computation.31 | async-start | bytes 1638400 | tf_op jit(solution)/shard_map/all_gather | solution.py:149
  575.2 52.4 %all-gather.25.cloned.1.call-start = ((), (), s32[]{:S(2)}) async-start(), calls=%async_computation.33 | async-start | bytes 1638400 | tf_op jit(solution)/shard_map/all_gather | solution.py:149
  577.0 94.3 %reduce-scatter.50.cloned.1.call-start = ((), (), s32[]{:S(2)}) async-start(), calls=%async_computation.34 | async-start | bytes 3276800 | tf_op jit(solution)/shard_map/reduce_scatter | solution.py:157
  636.6 64.8 %all-gather.27.cloned.1.call-start = ((), (), s32[]{:S(2)}) async-start(), calls=%async_computation.35 | async-start | bytes 1638400 | tf_op jit(solution)/shard_map/all_gather | solution.py:149
  676.6 168.5 %reduce-scatter.52.cloned.1.call-start = ((), (), s32[]{:S(2)}) async-start(), calls=%async_computation.36 | async-start | bytes 3276800 | tf_op jit(solution)/shard_map/reduce_scatter | solution.py:157
  810.4 70.7 %reduce-scatter.48.cloned.1.call-start = ((), (), s32[]{:S(2)}) async-start(), calls=%async_computation.32 | async-start | bytes 3276800 | tf_op jit(solution)/shard_map/reduce_scatter | solution.py:157
  814.7 113.7 %all-gather.29.cloned.1.call-start = ((), (), s32[]{:S(2)}) async-start(), calls=%async_computation.37 | async-start | bytes 1638400 | tf_op jit(solution)/shard_map/all_gather | solution.py:149
  884.2 18.4 collective-permute-start.2
  903.6 71.2 %reduce-scatter.54.cloned.1.call-start = ((), (), s32[]{:S(2)}) async-start(), calls=%async_computation.38 | async-start | bytes 3276800 | tf_op jit(solution)/shard_map/reduce_scatter | solution.py:157
  940.1 64.5 %all-gather.31.cloned.1.call-start = ((), (), s32[]{:S(2)}) async-start(), calls=%async_computation.39 | async-start | bytes 1638400 | tf_op jit(solution)/shard_map/all_gather | solution.py:149
  979.8 160.9 %reduce-scatter.56.cloned.1.call-start = ((), (), s32[]{:S(2)}) async-start(), calls=%async_computation.40 | async-start | bytes 3276800 | tf_op jit(solution)/shard_map/reduce_scatter | solution.py:157
  1106.0 83.1 %all-gather.33.cloned.1.call-start = ((), (), s32[]{:S(2)}) async-start(), calls=%async_computation.41 | async-start | bytes 1638400 | tf_op jit(solution)/shard_map/all_gather | solution.py:149
  1144.9 18.4 collective-permute-start.3
  1164.4 67.9 %reduce-scatter.58.cloned.1.call-start = ((), (), s32[]{:S(2)}) async-start(), calls=%async_computation.42 | async-start | bytes 3276800 | tf_op jit(solution)/shard_map/reduce_scatter | solution.py:157
  1197.6 64.3 %all-gather.35.cloned.1.call-start = ((), (), s32[]{:S(2)}) async-start(), calls=%async_computation.43 | async-start | bytes 1638400 | tf_op jit(solution)/shard_map/all_gather | solution.py:149
  1237.1 245.3 %reduce-scatter.60.cloned.1.call-start = ((), (), s32[]{:S(2)}) async-start(), calls=%async_computation.44 | async-start | bytes 3276800 | tf_op jit(solution)/shard_map/reduce_scatter | solution.py:157
  1362.0 370.4 %reduce-scatter.76.cloned.1.call-start = ((), (), s32[]{:S(2)}) async-start(), calls=%async_computation.52 | async-start | bytes 532480
  1368.7 443.3 %reduce-scatter.78.cloned.1.call-start = ((), (), s32[]{:S(2)}) async-start(), calls=%async_computation.53 | async-start | bytes 4456448
  1387.6 626.5 %reduce-scatter.72.cloned.1.call-start = ((), (), s32[]{:S(2)}) async-start(), calls=%async_computation.50 | async-start | bytes 557056
  1392.5 822.8 %reduce-scatter.74.cloned.1.call-start = ((), (), s32[]{:S(2)}) async-start(), calls=%async_computation.51 | async-start | bytes 1064960
  1431.8 929.5 %all-reduce.97.cloned.1.call-start = ((), (), s32[]{:S(2)}) async-start(), calls=%async_computation.54 | async-start | bytes 7340032
  1455.7 985.7 %reduce-scatter.70.cloned.1.call-start = ((), (), s32[]{:S(2)}) async-start(), calls=%async_computation.49 | async-start | bytes 3342336
  1479.0 1297.0 %reduce-scatter.68.cloned.1.call-start = ((), (), s32[]{:S(2)}) async-start(), calls=%async_computation.48 | async-start | bytes 532480
  1484.9 1355.6 %reduce-scatter.66.cloned.1.call-start = ((), (), s32[]{:S(2)}) async-start(), calls=%async_computation.47 | async-start | bytes 557056 | tf_op jit(solution)/shard_map/reduce_scatter | solution.py:166
  1488.0 1421.2 %reduce-scatter.64.cloned.1.call-start = ((), (), s32[]{:S(2)}) async-start(), calls=%async_computation.46 | async-start | bytes 557056 | tf_op jit(solution)/shard_map/reduce_scatter | solution.py:164
  1491.4 1753.7 %reduce-scatter.62.cloned.1.call-start = ((), (), s32[]{:S(2)}) async-start(), calls=%async_computation.45 | async-start | bytes 1064960 | tf_op jit(solution)/shard_map/reduce_scatter | solution.py:417
  1495.5 318.4 %copy-start.312 = (f32[384]{0:T(512)S(1)}, f32[384]{0:T(512)}, u32[]{:S(2)}) copy-start(f32[384]{0:T(512)} %get-tuple-element.203) | copy-start | bytes 4612
  1495.5 318.6 %copy-start.291 = (f32[384]{0:T(512)S(1)}, f32[384]{0:T(512)}, u32[]{:S(2)}) copy-start(f32[384]{0:T(512)} %get-tuple-element.144) | copy-start | bytes 4612
  1495.5 318.6 %copy-start.290 = (f32[384]{0:T(512)S(1)}, f32[384]{0:T(512)}, u32[]{:S(2)}) copy-start(f32[384]{0:T(512)} %get-tuple-element.145) | copy-start | bytes 4612
  1495.5 318.6 %copy-start.289 = (f32[384]{0:T(512)S(1)}, f32[384]{0:T(512)}, u32[]{:S(2)}) copy-start(f32[384]{0:T(512)} %get-tuple-element.146) | copy-start | bytes 4612
  1495.5 318.6 %copy-start.288 = (f32[384]{0:T(512)S(1)}, f32[384]{0:T(512)}, u32[]{:S(2)}) copy-start(f32[384]{0:T(512)} %get-tuple-element.173) | copy-start | bytes 4612
  1495.5 318.7 %copy-start.292 = (f32[256]{0:T(256)S(1)}, f32[256]{0:T(256)}, u32[]{:S(2)}) copy-start(f32[256]{0:T(256)} %get-tuple-element.153) | copy-start | bytes 3076
  1495.5 318.7 %copy-start.293 = (f32[256]{0:T(256)S(1)}, f32[256]{0:T(256)}, u32[]{:S(2)}) copy-start(f32[256]{0:T(256)} %get-tuple-element.154) | copy-start | bytes 3076
  1495.5 318.7 %copy-start.294 = (f32[256]{0:T(256)S(1)}, f32[256]{0:T(256)}, u32[]{:S(2)}) copy-start(f32[256]{0:T(256)} %get-tuple-element.155) | copy-start | bytes 3076
  1495.5 318.7 %copy-start.295 = (f32[256]{0:T(256)S(1)}, f32[256]{0:T(256)}, u32[]{:S(2)}) copy-start(f32[256]{0:T(256)} %get-tuple-element.156) | copy-start | bytes 3076
  1495.6 318.7 %copy-start.296 = (f32[256]{0:T(256)S(1)}, f32[256]{0:T(256)}, u32[]{:S(2)}) copy-start(f32[256]{0:T(256)} %get-tuple-element.157) | copy-start | bytes 3076
  1495.6 318.7 %copy-start.297 = (f32[256]{0:T(256)S(1)}, f32[256]{0:T(256)}, u32[]{:S(2)}) copy-start(f32[256]{0:T(256)} %get-tuple-element.158) | copy-start | bytes 3076
  1495.6 318.7 %copy-start.298 = (f32[256]{0:T(256)S(1)}, f32[256]{0:T(256)}, u32[]{:S(2)}) copy-start(f32[256]{0:T(256)} %get-tuple-element.159) | copy-start | bytes 3076
  1495.6 318.7 %copy-start.299 = (f32[256]{0:T(256)S(1)}, f32[256]{0:T(256)}, u32[]{:S(2)}) copy-start(f32[256]{0:T(256)} %get-tuple-element.160) | copy-start | bytes 3076
  1495.6 318.7 %copy-start.300 = (f32[256]{0:T(256)S(1)}, f32[256]{0:T(256)}, u32[]{:S(2)}) copy-start(f32[256]{0:T(256)} %get-tuple-element.161) | copy-start | bytes 3076
  1495.6 318.7 %copy-start.301 = (f32[256]{0:T(256)S(1)}, f32[256]{0:T(256)}, u32[]{:S(2)}) copy-start(f32[256]{0:T(256)} %get-tuple-element.162) | copy-start | bytes 3076
  1495.6 318.7 %copy-start.302 = (f32[256]{0:T(256)S(1)}, f32[256]{0:T(256)}, u32[]{:S(2)}) copy-start(f32[256]{0:T(256)} %get-tuple-element.163) | copy-start | bytes 3076
  1495.6 318.7 %copy-start.303 = (f32[256]{0:T(256)S(1)}, f32[256]{0:T(256)}, u32[]{:S(2)}) copy-start(f32[256]{0:T(256)} %get-tuple-element.164) | copy-start | bytes 3076
  1495.6 483.5 %copy-start.307 = (f32[6]{0:T(128)S(1)}, f32[6]{0:T(128)}, u32[]{:S(2)}) copy-start(f32[6]{0:T(128)} %get-tuple-element.207) | copy-start | bytes 76
  1495.7 483.5 %copy-start.308 = (f32[6]{0:T(128)S(1)}, f32[6]{0:T(128)}, u32[]{:S(2)}) copy-start(f32[6]{0:T(128)} %get-tuple-element.205) | copy-start | bytes 76
  1495.7 483.5 %copy-start.309 = (f32[6]{0:T(128)S(1)}, f32[6]{0:T(128)}, u32[]{:S(2)}) copy-start(f32[6]{0:T(128)} %get-tuple-element.209) | copy-start | bytes 76
  1495.7 483.6 %copy-start.305 = (f32[6]{0:T(128)S(1)}, f32[6]{0:T(128)}, u32[]{:S(2)}) copy-start(f32[6]{0:T(128)} %get-tuple-element.347) | copy-start | bytes 76
  1495.7 483.5 %copy-start.306 = (f32[6]{0:T(128)S(1)}, f32[6]{0:T(128)}, u32[]{:S(2)}) copy-start(f32[6]{0:T(128)} %get-tuple-element.346) | copy-start | bytes 76
  1495.7 483.5 %copy-start.313 = (f32[1,6]{1,0:T(1,128)S(1)}, f32[1,6]{1,0:T(1,128)}, u32[]{:S(2)}) copy-start(f32[1,6]{1,0:T(1,128)} %param.28) | copy-start | bytes 76
  1495.7 947.4 %copy-start.273 = (f32[160]{0:T(256)S(1)}, f32[160]{0:T(256)}, u32[]{:S(2)}) copy-start(f32[160]{0:T(256)} %copy-done.272) | copy-start | bytes 1924
  1495.7 947.4 %copy-start.95 = (f32[160,1024]{1,0:T(8,128)S(1)}, f32[160,1024]{1,0:T(8,128)}, u32[]{:S(2)}) copy-start(f32[160,1024]{1,0:T(8,128)} %reduce-scatter.60.cloned.1.call-done) | copy-start | bytes 1966084
  1501.0 943.4 %copy-start.94 = (f32[1,160,1024]{2,1,0:T(8,128)S(1)}, f32[1,160,1024]{2,1,0:T(8,128)}, u32[]{:S(2)}) copy-start(f32[1,160,1024]{2,1,0:T(8,128)} %get-tuple-element.224) | copy-start | bytes 1966084
  (303 other events, 2105.8 us)
Sparse Core Ops, SparseCore 0:
  12.4 27.3 all-gather.12
  112.2 34.5 reduce-scatter.37
  150.9 24.6 all-gather.14
  183.5 34.5 reduce-scatter.39
  238.4 25.3 all-gather.16
  324.2 34.5 reduce-scatter.41
  362.3 24.6 all-gather.18
  394.8 34.5 reduce-scatter.43
  450.1 25.3 all-gather.20
  536.7 34.5 reduce-scatter.45
  575.3 24.6 all-gather.22
  602.0 25.4 all-gather.24
  636.7 34.5 reduce-scatter.49
  676.7 24.6 all-gather.26
  810.6 34.5 reduce-scatter.51
  847.4 33.6 reduce-scatter.47
  903.7 24.6 all-gather.28
  940.2 34.5 reduce-scatter.53
  979.9 24.6 all-gather.30
  1106.2 34.5 reduce-scatter.55
  1164.5 24.6 all-gather.32
  1197.8 34.5 reduce-scatter.57
  1237.3 24.6 all-gather.34
  1362.1 34.5 reduce-scatter.59
  1399.0 333.2 reduce-scatter.75
  1736.7 75.2 reduce-scatter.77
  1815.6 64.2 reduce-scatter.71
  1882.3 332.8 reduce-scatter.73
  2217.8 143.4 all-reduce.96
  2365.2 76.1 reduce-scatter.69
  2443.7 332.2 reduce-scatter.67
  2780.7 59.7 reduce-scatter.65
  2844.6 64.5 reduce-scatter.63
  2912.2 332.7 reduce-scatter.61
where the time goes:
time: 3260 us; the launch traced here: 3250 us
  waiting for transfers between devices  2230 us (68%)
  matrix products  405 us (12%)
  local copies, waits for them, and re-layouts  201 us (6%)
  blocking collectives  199 us (6%)
  other arithmetic  189 us (6%)
    unnamed x41, waiting for transfers between devices  1060 us
    reduce_scatter x12, waiting for transfers between devices, reduce_rows(): return lax.psum_scatter(running, 'tensor', scatter_dimension=0, tiled=True)  374 us
    reduce_scatter x1, waiting for transfers between devices, per_device(): lax.psum_scatter(product_total[1][None], ('dp', 'tensor'), scatter_dimens...  336 us
    all_gather x12, waiting for transfers between devices, spread(): return lax.all_gather(shard, 'tensor', axis=0, tiled=True)  261 us
    unnamed x1, blocking collectives  165 us
    dot_general x9, matrix products, state_mix(): jnp.einsum('tsh,shp->thp', mixing, inputs, precision=lax.Precision.HIGHEST)  134 us
    unnamed x686, local copies, waits for them, and re-layouts  79.7 us
    reduce_scatter x1, waiting for transfers between devices, replica_sum(): lax.psum_scatter(terms[2], 'dp', scatter_dimension=1, tiled=True)  68.7 us
  transfers between devices with their start and end apart: 38, of which 36 were waited for; matrix products, arithmetic and copies ran while one was open for 6% of the time, Pallas kernels for 0%

commit v1 on v0

v1 whole, which is shorter than its diff:
```python
import jax
import jax.numpy as jnp
from jax import lax
from jax.experimental import pallas as pl
from jax.experimental.pallas import tpu as pltpu
from jax.sharding import PartitionSpec as P

ATT_HEADS = 8
KV_HEADS = 2
HEAD_DIM = 64
ROWS_IN = 464
ROWS_MIX = 720
ROWS_FEED = 768
ROWS_OWN = ROWS_MIX + ROWS_FEED
ROWS_SHARED = 128
ROWS_ALL = ROWS_OWN + ROWS_SHARED

MESH = pl.DeviceIdType.MESH
DMA = pltpu.SemaphoreType.DMA
bf16 = jnp.bfloat16
f32 = jnp.float32
VMEM = pltpu.VMEM

rope_base = 100000000000.0
norm_eps = 1e-05


def place():
    section = lax.axis_index("section")
    dp = lax.axis_index("dp")
    y = lax.axis_index("tensor")
    return section, dp // 8, (dp // 2) % 4, dp % 2, y


def at_y(y):
    return {"tensor": y}


def at_z(x_hi, z, core):
    return {"dp": x_hi * 8 + z * 2 + core}


def greet(partners):
    barrier = pltpu.get_barrier_semaphore()
    for partner in partners:
        pl.semaphore_signal(barrier, inc=1, device_id=partner, device_id_type=MESH)
    pl.semaphore_wait(barrier, len(partners))


def remote(src, dst, send_sem, recv_sem, partner):
    return pltpu.make_async_remote_copy(
        src_ref=src,
        dst_ref=dst,
        send_sem=send_sem,
        recv_sem=recv_sem,
        device_id=partner,
        device_id_type=MESH,
    )


def kernel_call(body, name, collective, out_shape, args, scratch, in_spaces=None, out_spaces=None):
    in_spaces = in_spaces or [VMEM] * len(args)
    outs = out_shape if isinstance(out_shape, (list, tuple)) else [out_shape]
    out_spaces = out_spaces or [VMEM] * len(outs)
    out_specs = [pl.BlockSpec(memory_space=space) for space in out_spaces]
    return pl.pallas_call(
        body,
        name=name,
        out_shape=out_shape,
        in_specs=[pl.BlockSpec(memory_space=space) for space in in_spaces],
        out_specs=out_specs if isinstance(out_shape, (list, tuple)) else out_specs[0],
        scratch_shapes=scratch,
        compiler_params=pltpu.CompilerParams(
            collective_id=collective, has_side_effects=True, vmem_limit_bytes=56 * 2**20
        ),
    )(*args)


def shape(dims, kind):
    return jax.ShapeDtypeStruct(dims, kind)


def to_chips_body(x_ref, out_ref, send_sem, recv_sem, local_sem):
    _, x_hi, z, core, y = place()
    mine = y // 2
    bit = y % 2
    own = mine == core
    barrier = pltpu.get_barrier_semaphore()
    for b in (0, 1):
        source = {"tensor": 2 * core + b, "dp": x_hi * 8 + z * 2 + mine}
        is_self = jnp.logical_and(own, bit == b)

        @pl.when(jnp.logical_not(is_self))
        def _():
            pl.semaphore_signal(barrier, inc=1, device_id=source, device_id_type=MESH)

    @pl.when(own)
    def _():
        pl.semaphore_wait(barrier, 1)

    @pl.when(jnp.logical_not(own))
    def _():
        pl.semaphore_wait(barrier, 2)

    rows = x_ref.shape[1]
    for j in (0, 1):
        target = {"tensor": 2 * core + j, "dp": x_hi * 8 + z * 2 + mine}
        is_self = jnp.logical_and(own, bit == j)
        slot = out_ref.at[pl.ds(pl.multiple_of(bit * rows, rows), rows)]

        @pl.when(is_self)
        def _():
            pltpu.make_async_copy(x_ref.at[j], slot, local_sem.at[0]).start()

        @pl.when(jnp.logical_not(is_self))
        def _():
            remote(x_ref.at[j], slot, send_sem.at[j], recv_sem.at[bit], target).start()

    for j in (0, 1):
        is_self = jnp.logical_and(own, bit == j)
        slot = out_ref.at[pl.ds(j * rows, rows)]
        target = {"tensor": 2 * core + j, "dp": x_hi * 8 + z * 2 + mine}

        @pl.when(is_self)
        def _():
            pltpu.make_async_copy(x_ref.at[j], slot, local_sem.at[0]).wait()

        @pl.when(jnp.logical_not(is_self))
        def _():
            copy = remote(x_ref.at[j], slot, send_sem.at[j], recv_sem.at[j], target)
            copy.wait_send()
            copy.wait_recv()


def to_chips(x):
    return kernel_call(
        to_chips_body,
        "to_chips",
        1,
        shape((2 * x.shape[1], x.shape[2]), x.dtype),
        (x,),
        [DMA((2,)), DMA((2,)), DMA((1,))],
    )


def from_chips_body(x_ref, out_ref, send_sem, recv_sem, local_sem):
    _, x_hi, z, core, y = place()
    mine = y // 2
    bit = y % 2
    own = mine == core
    barrier = pltpu.get_barrier_semaphore()
    for b in (0, 1):
        source = {"tensor": 2 * core + b, "dp": x_hi * 8 + z * 2 + mine}
        is_self = jnp.logical_and(own, bit == b)

        @pl.when(jnp.logical_not(is_self))
        def _():
            pl.semaphore_signal(barrier, inc=1, device_id=source, device_id_type=MESH)

    @pl.when(own)
    def _():
        pl.semaphore_wait(barrier, 1)

    @pl.when(jnp.logical_not(own))
    def _():
        pl.semaphore_wait(barrier, 2)

    rows = x_ref.shape[0] // 2
    for b in (0, 1):
        target = {"tensor": 2 * core + b, "dp": x_hi * 8 + z * 2 + mine}
        is_self = jnp.logical_and(own, bit == b)
        block = x_ref.at[pl.ds(b * rows, rows)]

        @pl.when(is_self)
        def _():
            pltpu.make_async_copy(block, out_ref.at[bit], local_sem.at[0]).start()

        @pl.when(jnp.logical_not(is_self))
        def _():
            remote(block, out_ref.at[bit], send_sem.at[b], recv_sem.at[bit], target).start()

    for b in (0, 1):
        target = {"tensor": 2 * core + b, "dp": x_hi * 8 + z * 2 + mine}
        is_self = jnp.logical_and(own, bit == b)
        block = x_ref.at[pl.ds(b * rows, rows)]

        @pl.when(is_self)
        def _():
            pltpu.make_async_copy(block, out_ref.at[b], local_sem.at[0]).wait()

        @pl.when(jnp.logical_not(is_self))
        def _():
            copy = remote(block, out_ref.at[b], send_sem.at[b], recv_sem.at[b], target)
            copy.wait_send()
            copy.wait_recv()


def from_chips(x, collective):
    return kernel_call(
        from_chips_body,
        "from_chips",
        collective,
        shape((2, x.shape[0] // 2, x.shape[1]), x.dtype),
        (x,),
        [DMA((2,)), DMA((2,)), DMA((1,))],
    )


def gather_body(mix_ref, feed_ref, small_ref, mix_out, feed_out, small_out, send, recv, local):
    _, x_hi, z, core, y = place()
    right, left, across = (y + 1) % 4, (y + 3) % 4, (y + 2) % 4
    z_right, z_left = at_z(x_hi, (z + 1) % 4, core), at_z(x_hi, (z + 3) % 4, core)
    greet([at_y(right), at_y(left), at_y(across), z_right, z_left])
    counter = [0]

    def go(src, dst, partner):
        n = counter[0]
        counter[0] += 1
        copy = remote(src, dst, send.at[n], recv.at[n], partner)
        copy.start()
        return copy

    def aligned(start, by):
        return pl.multiple_of(start, by)

    feed_at = aligned(z * 192, 192)
    mix_at = aligned(ROWS_IN + z * 64, 16)

    own = []
    for n, (src, dst) in enumerate(
        ((mix_ref, mix_out.at[y]), (feed_ref, feed_out.at[y]), (small_ref, small_out.at[y]))
    ):
        copy = pltpu.make_async_copy(src, dst, local.at[n])
        copy.start()
        own.append(copy)

    helped = (
        (feed_ref, feed_out, feed_at, 0, 192, 96),
        (mix_ref, mix_out, mix_at, 0, 64, 32),
    )
    straight = ((mix_ref, mix_out, 0, 0, ROWS_IN, 240),)
    small = [
        go(small_ref, small_out.at[y], at_y(other)) for other in (right, left, across)
    ]

    def first(group):
        sent = []
        for src, out, start, _, rows, _ in group:
            piece = src.at[pl.ds(start, rows)]
            dst = out.at[y, pl.ds(start, rows)]
            sent.append((go(piece, dst, at_y(right)), go(piece, dst, at_y(left))))
        return sent

    def second(group, sent):
        more = []
        for (src, out, start, _, rows, cut), (to_right, to_left) in zip(group, sent):
            to_right.wait_recv()
            piece = out.at[left, pl.ds(start, cut)]
            a = go(piece, piece, at_y(right))
            to_left.wait_recv()
            piece = out.at[right, pl.ds(start + cut, rows - cut)]
            b = go(piece, piece, at_y(left))
            more.append((a, b))
        return more

    waits = []
    helped_one = first(helped)
    straight_one = first(straight)
    helped_two = second(helped, helped_one)

    def z_first(source_y):
        sent = []
        for src, out, start, _, rows, cut in helped:
            piece = out.at[source_y, pl.ds(start, rows)]
            sent.append((go(piece, piece, z_right), go(piece, piece, z_left)))
        return sent

    def z_second(source_y, sent):
        more = []
        for (src, out, start, _, rows, cut), (to_right, to_left) in zip(helped, sent):
            step = rows
            base = start - z * rows
            from_left = base + ((z + 3) % 4) * rows
            from_right = base + ((z + 1) % 4) * rows
            to_right.wait_recv()
            piece = out.at[source_y, pl.ds(aligned(from_left, 16), cut)]
            a = go(piece, piece, z_right)
            to_left.wait_recv()
            piece = out.at[source_y, pl.ds(aligned(from_right + cut, 16), rows - cut)]
            b = go(piece, piece, z_left)
            more.append((a, b))
        return more

    z_one_left = z_first(left)
    z_one_right = z_first(right)
    straight_two = second(straight, straight_one)
    z_two_left = z_second(left, z_one_left)
    z_two_right = z_second(right, z_one_right)
    for a, b in helped_two:
        a.wait_recv()
        b.wait_recv()
    z_one_across = z_first(across)
    z_two_across = z_second(across, z_one_across)
    for a, b in straight_two:
        a.wait_recv()
        b.wait_recv()
    for group in (z_two_left, z_two_right, z_two_across):
        for a, b in group:
            a.wait_recv()
            b.wait_recv()
    for group in (
        helped_one,
        straight_one,
        helped_two,
        straight_two,
        z_one_left,
        z_one_right,
        z_one_across,
        z_two_left,
        z_two_right,
        z_two_across,
    ):
        for a, b in group:
            a.wait_send()
            b.wait_send()
    for copy in small:
        copy.wait()
    for copy in own:
        copy.wait()


def gather_weights(mix, feed, small):
    any_space = pl.ANY
    return kernel_call(
        gather_body,
        "gather_weights",
        2,
        [
            shape((4,) + mix.shape, mix.dtype),
            shape((4,) + feed.shape, feed.dtype),
            shape((4,) + small.shape, small.dtype),
        ],
        (mix, feed, small),
        [DMA((40,)), DMA((40,)), DMA((3,))],
        [any_space] * 3,
        [any_space] * 3,
    )


def other_core(x_hi, z, core):
    return at_z(x_hi, z, 1 - core)


def inverse_rms(values):
    return lax.rsqrt(jnp.mean(values * values, axis=-1, keepdims=True) + norm_eps)


def my_rows(core, rows):
    return pl.ds(pl.multiple_of(core * rows, rows), rows)


def norm_gather_body(hidden_ref, gain_ref, out_ref, send, recv):
    _, x_hi, z, core, _ = place()
    rows = hidden_ref.shape[0]
    partner = other_core(x_hi, z, core)
    greet([partner])
    hidden = hidden_ref[...]
    out_ref[my_rows(core, rows)] = (hidden * inverse_rms(hidden) * gain_ref[...]).astype(bf16)
    mine = out_ref.at[my_rows(core, rows)]
    copy = remote(mine, mine, send.at[0], recv.at[0], partner)
    copy.start()
    copy.wait()


def norm_gather(hidden, gain, collective):
    return kernel_call(
        norm_gather_body,
        "norm_gather",
        collective,
        shape((2 * hidden.shape[0], hidden.shape[1]), bf16),
        (hidden, gain),
        [DMA((1,)), DMA((1,))],
    )


def cast_gather_body(grad_ref, out_ref, send, recv):
    _, x_hi, z, core, _ = place()
    rows = grad_ref.shape[0]
    partner = other_core(x_hi, z, core)
    greet([partner])
    out_ref[my_rows(core, rows)] = grad_ref[...].astype(bf16)
    mine = out_ref.at[my_rows(core, rows)]
    copy = remote(mine, mine, send.at[0], recv.at[0], partner)
    copy.start()
    copy.wait()


def cast_gather(grad, collective):
    return kernel_call(
        cast_gather_body,
        "cast_gather",
        collective,
        shape((2 * grad.shape[0], grad.shape[1]), bf16),
        (grad,),
        [DMA((1,)), DMA((1,))],
    )


def swap_halves(part_ref, land, send, recv, partner, core):
    rows = land.shape[0]
    copy = remote(part_ref.at[my_rows(1 - core, rows)], land, send, recv, partner)
    copy.start()
    copy.wait()
    return part_ref[my_rows(core, rows)].astype(f32) + land[...].astype(f32)


def middle_body(part_ref, hidden_ref, gain_ref, middle_ref, out_ref, land, send, recv):
    _, x_hi, z, core, _ = place()
    rows = hidden_ref.shape[0]
    partner = other_core(x_hi, z, core)
    greet([partner])
    branch = swap_halves(part_ref, land, send.at[0], recv.at[0], partner, core)
    middle = hidden_ref[...] + branch
    middle_ref[...] = middle
    out_ref[my_rows(core, rows)] = (middle * inverse_rms(middle) * gain_ref[...]).astype(bf16)
    mine = out_ref.at[my_rows(core, rows)]
    copy = remote(mine, mine, send.at[1], recv.at[1], partner)
    copy.start()
    copy.wait()


def middle_step(part, hidden, gain, collective):
    rows, width = hidden.shape
    return kernel_call(
        middle_body,
        "middle_step",
        collective,
        [shape((rows, width), f32), shape((2 * rows, width), bf16)],
        (part, hidden, gain),
        [VMEM((rows, width), bf16), DMA((2,)), DMA((2,))],
    )


def output_body(part_ref, middle_ref, out_ref, received_ref, land, low, send, recv):
    section, x_hi, z, core, _ = place()
    partner = other_core(x_hi, z, core)
    beyond = {"section": 1 - section}
    greet([partner, beyond])
    out = middle_ref[...] + swap_halves(part_ref, land, send.at[0], recv.at[0], partner, core)
    out_ref[...] = out
    low[...] = out.astype(bf16)
    copy = remote(low, received_ref, send.at[1], recv.at[1], beyond)
    copy.start()
    copy.wait()


def output_step(part, middle, collective):
    rows, width = middle.shape
    return kernel_call(
        output_body,
        "output_step",
        collective,
        [shape((rows, width), f32), shape((rows, width), bf16)],
        (part, middle),
        [VMEM((rows, width), bf16), VMEM((rows, width), bf16), DMA((2,)), DMA((2,))],
    )


def rms_back(values, gain, grad):
    scale = inverse_rms(values)
    weighted = grad * gain
    unit = values * scale
    inner = jnp.mean(weighted * unit, axis=-1, keepdims=True)
    return scale * (weighted - unit * inner), jnp.sum(grad * unit, axis=0, keepdims=True)


def middle_back_body(
    part_ref, middle_ref, gain_ref, grad_ref, out_ref, full_ref, gain_grad_ref, land, send, recv
):
    _, x_hi, z, core, _ = place()
    rows = middle_ref.shape[0]
    partner = other_core(x_hi, z, core)
    greet([partner])
    normed_grad = swap_halves(part_ref, land, send.at[0], recv.at[0], partner, core)
    back, gain_grad = rms_back(middle_ref[...], gain_ref[...], normed_grad)
    gain_grad_ref[...] = gain_grad
    grad = grad_ref[...] + back
    out_ref[...] = grad
    full_ref[my_rows(core, rows)] = grad.astype(bf16)
    mine = full_ref.at[my_rows(core, rows)]
    copy = remote(mine, mine, send.at[1], recv.at[1], partner)
    copy.start()
    copy.wait()


def middle_back(part, middle, gain, grad, collective):
    rows, width = middle.shape
    return kernel_call(
        middle_back_body,
        "middle_back",
        collective,
        [shape((rows, width), f32), shape((2 * rows, width), bf16), shape((1, width), f32)],
        (part, middle, gain, grad),
        [VMEM((rows, width), bf16), DMA((2,)), DMA((2,))],
    )


def input_back_body(
    part_ref, hidden_ref, gain_ref, grad_ref, out_ref, received_ref, gain_grad_ref, land, low, send, recv
):
    section, x_hi, z, core, _ = place()
    partner = other_core(x_hi, z, core)
    beyond = {"section": 1 - section}
    greet([partner, beyond])
    normed_grad = swap_halves(part_ref, land, send.at[0], recv.at[0], partner, core)
    back, gain_grad = rms_back(hidden_ref[...], gain_ref[...], normed_grad)
    gain_grad_ref[...] = gain_grad
    grad = grad_ref[...] + back
    out_ref[...] = grad
    low[...] = grad.astype(bf16)
    copy = remote(low, received_ref, send.at[1], recv.at[1], beyond)
    copy.start()
    copy.wait()


def input_back(part, hidden, gain, grad, collective):
    rows, width = hidden.shape
    return kernel_call(
        input_back_body,
        "input_back",
        collective,
        [shape((rows, width), f32), shape((rows, width), bf16), shape((1, width), f32)],
        (part, hidden, gain, grad),
        [VMEM((rows, width), bf16), VMEM((rows, width), bf16), DMA((2,)), DMA((2,))],
    )


CUT_ONE = 816
CUT_HALF = 416


def add_into(dst, sources, rows, strip):
    def step(n, carry):
        at = pl.ds(pl.multiple_of(n * strip, 16), strip)
        total = sources[0][at].astype(f32)
        for source in sources[1:]:
            total = total + source[at].astype(f32)
        dst[at] = total.astype(dst.dtype)
        return carry

    lax.fori_loop(0, rows // strip, step, 0)


def reduce_body(
    grads,
    small_ref,
    out_ref,
    shared_ref,
    small_out,
    land_y,
    land_z,
    sum_y,
    sum_z,
    land_yz,
    land_zy,
    both,
    land_x,
    small_y,
    small_z,
    small_x,
    small_sum,
    send,
    recv,
):
    _, x_hi, z, core, y = place()
    right, left, across = (y + 1) % 4, (y + 3) % 4, (y + 2) % 4
    y_right, y_left, y_across = at_y(right), at_y(left), at_y(across)
    z_r, z_l, z_a = (z + 1) % 4, (z + 3) % 4, (z + 2) % 4
    z_right, z_left, z_across = (at_z(x_hi, k, core) for k in (z_r, z_l, z_a))
    x_other = at_z(1 - x_hi, z, core)
    partner = other_core(x_hi, z, core)
    greet([y_right, y_left, y_across, z_right, z_left, z_across, x_other, partner])
    counter = [0]
    started = []

    def go(src, dst, to):
        n = counter[0]
        counter[0] += 1
        copy = remote(src, dst, send.at[n], recv.at[n], to)
        copy.start()
        started.append(copy)
        return copy

    top = (0, CUT_HALF)
    low = (CUT_HALF, CUT_ONE - CUT_HALF)
    rest = ROWS_ALL - CUT_ONE
    rest_half = rest // 2

    def lanes(k):
        return pl.ds(pl.multiple_of(k * 256, 256), 256)

    def one(k, piece):
        return grads.at[k, pl.ds(*piece)]

    a1 = go(one(across, top), land_y.at[0, pl.ds(*top)], y_right)
    b1 = go(one(across, low), land_y.at[0, pl.ds(*low)], y_left)

    def two(k, pair):
        return grads.at[pl.ds(pair, 2), pl.ds(CUT_ONE, rest), lanes(k)]

    a2 = go(two(z_a, 0), land_z.at[0, pl.ds(0, 2)], z_right)
    b2 = go(two(z_a, 2), land_z.at[0, pl.ds(2, 2)], z_left)
    e1 = go(one(right, low), land_y.at[1, pl.ds(*low)], y_right)
    f1 = go(one(left, top), land_y.at[2, pl.ds(*top)], y_left)
    e2 = go(two(z_r, 2), land_z.at[1, pl.ds(2, 2)], z_right)
    f2 = go(two(z_l, 0), land_z.at[2, pl.ds(0, 2)], z_left)

    s_y = [go(small_ref, small_y.at[n], to) for n, to in enumerate((y_right, y_left, y_across))]
    for copy in s_y:
        copy.wait_recv()
    small_sum[0] = small_ref[...] + small_y[0] + small_y[1] + small_y[2]
    s_z = [go(small_sum.at[0], small_z.at[n], to) for n, to in enumerate((z_right, z_left, z_across))]

    a1.wait_recv()
    add_into(land_y.at[0, pl.ds(*top)], (one(right, top), land_y.at[0, pl.ds(*top)]), top[1], 32)
    c1 = go(land_y.at[0, pl.ds(*top)], land_y.at[1, pl.ds(*top)], y_right)
    b1.wait_recv()
    add_into(land_y.at[0, pl.ds(*low)], (one(left, low), land_y.at[0, pl.ds(*low)]), low[1], 80)
    d1 = go(land_y.at[0, pl.ds(*low)], land_y.at[2, pl.ds(*low)], y_left)
    a2.wait_recv()
    for k in (0, 1):
        mine = grads.at[k, pl.ds(CUT_ONE, rest), lanes(z_r)]
        add_into(land_z.at[0, k], (mine, land_z.at[0, k]), rest, 80)
    c2 = go(land_z.at[0, pl.ds(0, 2)], land_z.at[1, pl.ds(0, 2)], z_right)
    b2.wait_recv()
    for k in (2, 3):
        mine = grads.at[k, pl.ds(CUT_ONE, rest), lanes(z_l)]
        add_into(land_z.at[0, k], (mine, land_z.at[0, k]), rest, 80)
    d2 = go(land_z.at[0, pl.ds(2, 2)], land_z.at[2, pl.ds(2, 2)], z_left)

    for copy in s_z:
        copy.wait_recv()
    small_sum[1] = small_sum[0] + small_z[0] + small_z[1] + small_z[2]
    s_x = go(small_sum.at[1], small_x.at[0], x_other)

    for copy in (e1, f1, c1, d1):
        copy.wait_recv()
    add_into(sum_y, (grads.at[y, pl.ds(0, CUT_ONE)], land_y.at[1], land_y.at[2]), CUT_ONE, 48)

    def one_z(k, piece):
        return sum_y.at[pl.ds(*piece), lanes(k)]

    a3 = go(one_z(z_a, top), land_yz.at[0, pl.ds(*top)], z_right)
    b3 = go(one_z(z_a, low), land_yz.at[0, pl.ds(*low)], z_left)
    e3 = go(one_z(z_r, low), land_yz.at[1, pl.ds(*low)], z_right)
    f3 = go(one_z(z_l, top), land_yz.at[2, pl.ds(*top)], z_left)

    for copy in (e2, f2, c2, d2):
        copy.wait_recv()
    for k in range(4):
        mine = grads.at[k, pl.ds(CUT_ONE, rest), lanes(z)]
        add_into(sum_z.at[k], (mine, land_z.at[1, k], land_z.at[2, k]), rest, 80)

    def two_y(k, start):
        return sum_z.at[k, pl.ds(start, rest_half)]

    a4 = go(two_y(across, 0), land_zy.at[0, pl.ds(0, rest_half)], y_right)
    b4 = go(two_y(across, rest_half), land_zy.at[0, pl.ds(rest_half, rest_half)], y_left)
    e4 = go(two_y(right, rest_half), land_zy.at[1, pl.ds(rest_half, rest_half)], y_right)
    f4 = go(two_y(left, 0), land_zy.at[2, pl.ds(0, rest_half)], y_left)

    s_x.wait_recv()
    small_sum[2] = small_sum[1] + small_x[0]
    s_c = go(small_sum.at[2], small_out.at[core], partner)
    small_out[core] = small_sum[2]

    a3.wait_recv()
    add_into(land_yz.at[0, pl.ds(*top)], (one_z(z_r, top), land_yz.at[0, pl.ds(*top)]), top[1], 32)
    c3 = go(land_yz.at[0, pl.ds(*top)], land_yz.at[1, pl.ds(*top)], z_right)
    b3.wait_recv()
    add_into(land_yz.at[0, pl.ds(*low)], (one_z(z_l, low), land_yz.at[0, pl.ds(*low)]), low[1], 80)
    d3 = go(land_yz.at[0, pl.ds(*low)], land_yz.at[2, pl.ds(*low)], z_left)
    a4.wait_recv()
    first = pl.ds(0, rest_half)
    second = pl.ds(rest_half, rest_half)
    add_into(land_zy.at[0, first], (two_y(right, 0), land_zy.at[0, first]), rest_half, 80)
    c4 = go(land_zy.at[0, first], land_zy.at[1, first], y_right)
    b4.wait_recv()
    add_into(land_zy.at[0, second], (two_y(left, rest_half), land_zy.at[0, second]), rest_half, 80)
    d4 = go(land_zy.at[0, second], land_zy.at[2, second], y_left)

    for copy in (e3, f3, c3, d3):
        copy.wait_recv()
    add_into(
        both.at[pl.ds(0, CUT_ONE)],
        (sum_y.at[:, lanes(z)], land_yz.at[1], land_yz.at[2]),
        CUT_ONE,
        48,
    )

    def half(k):
        return pl.ds(pl.multiple_of(k * 128, 128), 128)

    part_one = pl.ds(0, CUT_ONE)
    part_two = pl.ds(CUT_ONE, rest)
    x1 = go(both.at[part_one, half(1 - x_hi)], land_x.at[part_one], x_other)
    for copy in (e4, f4, c4, d4):
        copy.wait_recv()
    add_into(both.at[part_two], (sum_z.at[y], land_zy.at[1], land_zy.at[2]), rest, 80)
    x2 = go(both.at[part_two, half(1 - x_hi)], land_x.at[part_two], x_other)
    x1.wait_recv()
    add_into(
        out_ref.at[core, part_one], (both.at[part_one, half(x_hi)], land_x.at[part_one]), CUT_ONE, 48
    )
    k1 = go(out_ref.at[core, part_one], out_ref.at[core, part_one], partner)
    x2.wait_recv()
    add_into(
        out_ref.at[core, part_two], (both.at[part_two, half(x_hi)], land_x.at[part_two]), rest, 80
    )
    k2 = go(out_ref.at[core, part_two], out_ref.at[core, part_two], partner)
    k1.wait_recv()
    k2.wait_recv()
    shared_at = pl.ds(ROWS_OWN, ROWS_SHARED)
    shared_ref[y] = out_ref[0, shared_at] + out_ref[1, shared_at]
    ends = [go(shared_ref.at[y], shared_ref.at[y], to) for to in (y_right, y_left, y_across)]
    s_c.wait_recv()
    for copy in ends:
        copy.wait_recv()
    for copy in started:
        copy.wait_send()


def reduce_grads(grads, small, collective):
    rest = ROWS_ALL - CUT_ONE
    return kernel_call(
        reduce_body,
        "reduce_grads",
        collective,
        [
            shape((2, ROWS_ALL, 128), f32),
            shape((4, ROWS_SHARED, 128), f32),
            shape((2,) + small.shape, f32),
        ],
        (grads, small),
        [
            VMEM((3, CUT_ONE, 1024), bf16),
            VMEM((3, 4, rest, 256), bf16),
            VMEM((CUT_ONE, 1024), bf16),
            VMEM((4, rest, 256), bf16),
            VMEM((3, CUT_ONE, 256), bf16),
            VMEM((3, rest, 256), bf16),
            VMEM((ROWS_ALL, 256), bf16),
            VMEM((ROWS_ALL, 128), bf16),
            VMEM((3,) + small.shape, f32),
            VMEM((3,) + small.shape, f32),
            VMEM((1,) + small.shape, f32),
            VMEM((3,) + small.shape, f32),
            DMA((40,)),
            DMA((40,)),
        ],
    )


def causal_conv(signal, kernel):
    kernel_size = kernel.shape[0]
    length = signal.shape[0]
    padded = jnp.pad(signal, ((kernel_size - 1, 0), (0, 0)))
    running = padded[0:length] * kernel[0]
    for offset in range(1, kernel_size):
        running = running + padded[offset : offset + length] * kernel[offset]
    return running


def rotate(values):
    length = values.shape[0]
    half_size = values.shape[-1] // 2
    exponents = jnp.arange(half_size, dtype=jnp.float32) * (-2.0 / values.shape[-1])
    frequency = jnp.power(rope_base, exponents)
    angles = jnp.arange(length, dtype=jnp.float32)[:, None] * frequency[None, :]
    cosine = jnp.cos(angles)[:, None, :]
    sine_part = jnp.sin(angles)[:, None, :]
    first_half = values[..., :half_size]
    second_half = values[..., half_size:]
    return jnp.concatenate(
        [
            first_half * cosine - second_half * sine_part,
            second_half * cosine + first_half * sine_part,
        ],
        axis=-1,
    )


def attention(queries, key_heads, value_heads):
    group_size = queries.shape[1] // key_heads.shape[1]
    keys_all = jnp.repeat(key_heads, group_size, axis=1)
    values_all = jnp.repeat(value_heads, group_size, axis=1)
    length = queries.shape[0]
    scores = jnp.einsum(
        "thd,shd->hts", queries, keys_all
    ) * queries.shape[-1] ** (-0.5)
    causal = lax.broadcasted_iota(jnp.int32, (length, length), 0) >= lax.broadcasted_iota(
        jnp.int32, (length, length), 1
    )
    scores = jnp.where(causal[None], scores, -1e30)
    row_max = jnp.max(scores, axis=-1, keepdims=True)
    weights = jnp.exp(scores - row_max)
    weights = weights / jnp.sum(weights, axis=-1, keepdims=True)
    return jnp.einsum("hts,shd->thd", weights, values_all)


def state_mix(inputs, state_inputs, state_reads, step_size, decay_log, skip_gain):
    length = inputs.shape[0]
    log_decay = -step_size * jnp.exp(decay_log)[None, :]
    running = jnp.cumsum(log_decay, axis=0)
    causal = lax.broadcasted_iota(jnp.int32, (length, length), 0) >= lax.broadcasted_iota(
        jnp.int32, (length, length), 1
    )
    decay_gap = running[:, None, :] - running[None, :, :]
    decays = jnp.exp(jnp.where(causal[:, :, None], decay_gap, -jnp.inf))
    intersection = jnp.dot(state_reads, state_inputs.T, preferred_element_type=jnp.float32)
    mixing = intersection[:, :, None] * decays * step_size[None, :, :]
    mixed = jnp.einsum("tsh,shp->thp", mixing, inputs)
    return mixed + skip_gain[None, :, None] * inputs


def mixer_core(
    mamba_proj,
    state_proj,
    step_proj,
    query_proj,
    keyval_proj,
    mamba_conv,
    state_conv,
    step_bias,
    decay_log,
    skip_gain,
):
    length = mamba_proj.shape[0]
    head_count = step_proj.shape[1]
    gate_part = mamba_proj[:, 0]
    conv_input = jax.nn.silu(causal_conv(mamba_proj[:, 1], mamba_conv))
    conv_state = jax.nn.silu(causal_conv(state_proj, state_conv))
    state_size = state_proj.shape[1] // 2
    step_size = jax.nn.softplus(step_proj + step_bias)
    mixed = state_mix(
        conv_input.reshape(length, head_count, -1),
        conv_state[:, :state_size],
        conv_state[:, state_size:],
        step_size,
        decay_log,
        skip_gain,
    )
    gated_out = mixed.reshape(length, -1) * jax.nn.silu(gate_part)
    queries = rotate(query_proj.reshape(length, -1, HEAD_DIM))
    key_heads = rotate(keyval_proj[:, 0].reshape(length, -1, HEAD_DIM))
    value_heads = keyval_proj[:, 1].reshape(length, -1, HEAD_DIM)
    attended = jax.checkpoint(attention)(queries, key_heads, value_heads).reshape(length, -1)
    return (gated_out, attended)


def swiglu(gate, up):
    return jax.nn.silu(gate) * up


def product(left, right):
    return jnp.dot(left, right, preferred_element_type=jnp.float32)


def product_t(left, right):
    return lax.dot_general(left, right, (((1,), (1,)), ((), ())), preferred_element_type=jnp.float32)


def outer_sum(left, right):
    return lax.dot_general(left, right, (((0,), (0,)), ((), ())), preferred_element_type=jnp.float32)


def rows_of(pack, start, stop):
    part = pack[:, start:stop]
    return part.reshape(-1, part.shape[-1])


def per_device(
    stream_in,
    cotangent,
    mixer_gain,
    mamba_in,
    state_in,
    step_in,
    mamba_conv,
    state_conv,
    step_bias,
    decay_log,
    skip_gain,
    query_in,
    keyval_in,
    mamba_out,
    attention_out,
    feed_gain,
    gate_up,
    down_weight,
):
    section, x_hi, z, core, y = place()
    is_first = section == 0
    width = stream_in.shape[2]
    length = 4 * stream_in.shape[1]
    gain_one = mixer_gain.astype(f32)
    gain_two = feed_gain.astype(f32)

    def mine(values, axis):
        size = values.shape[axis] // 2
        return lax.dynamic_slice_in_dim(values, core * size, size, axis)

    def turned(values):
        return mine(values, 1).T

    step_rows = jnp.pad(turned(step_in[0]), ((0, 13), (0, 0)))
    mix = jnp.concatenate(
        [
            turned(mamba_in[0, :, 0]),
            turned(mamba_in[0, :, 1]),
            turned(query_in[0]),
            step_rows,
            mine(mamba_out[0], 0),
            mine(attention_out[0], 0),
        ]
    )
    feed = jnp.concatenate(
        [turned(gate_up[0, :, 0]), turned(gate_up[0, :, 1]), mine(down_weight[0], 0)]
    )
    conv_mine = jnp.pad(mine(mamba_conv[0].astype(f32), 1), ((0, 0), (0, 64)))
    heads_mine = jnp.pad(
        jnp.stack([mine(step_bias[0], 0), mine(decay_log[0], 0), mine(skip_gain[0], 0)]),
        ((0, 9), (0, 253)),
    )
    mix_all, feed_all, small_all = gather_weights(
        mix, feed, jnp.concatenate([conv_mine, heads_mine])
    )
    shared = jnp.concatenate(
        [state_in[0].T, keyval_in[0, :, 0].T, keyval_in[0, :, 1].T]
    )
    conv_x = small_all[:, 0:4, 0:192].transpose(1, 0, 2).reshape(4, 768)
    bias = small_all[:, 4, 0:3].reshape(12)
    decay = small_all[:, 5, 0:3].reshape(12)
    skip = small_all[:, 6, 0:3].reshape(12)
    conv_state_f = state_conv[0].astype(f32)

    w_mamba = jnp.concatenate([rows_of(mix_all, 0, 192), rows_of(mix_all, 192, 384)])
    w_query = rows_of(mix_all, 384, 448)
    w_step = rows_of(mix_all, 448, 451)
    w_mamba_out = rows_of(mix_all, 464, 656)
    w_att_out = rows_of(mix_all, 656, 720)
    w_gate = rows_of(feed_all, 0, 256)
    w_up = rows_of(feed_all, 256, 512)
    w_down = rows_of(feed_all, 512, 768)

    own = to_chips(jnp.where(is_first, stream_in, cotangent)).astype(f32)

    def forward(hidden, ids):
        normed = norm_gather(hidden, gain_one, ids[0])
        mamba_proj = product_t(normed, w_mamba).reshape(length, 2, -1)
        shared_proj = product_t(normed, shared)
        step_proj = product_t(normed, w_step)
        query_proj = product_t(normed, w_query)
        core_values, core_back = jax.vjp(
            mixer_core,
            mamba_proj,
            shared_proj[:, :256],
            step_proj,
            query_proj,
            shared_proj[:, 256:].reshape(length, 2, -1),
            conv_x,
            conv_state_f,
            bias,
            decay,
            skip,
        )
        gated = core_values[0].astype(bf16)
        attended = core_values[1].astype(bf16)
        part = (product(gated, w_mamba_out) + product(attended, w_att_out)).astype(bf16)
        middle, normed_two = middle_step(part, hidden, gain_two, ids[1])
        gate = product_t(normed_two, w_gate)
        up = product_t(normed_two, w_up)
        activated = swiglu(gate, up).astype(bf16)
        part_two = product(activated, w_down).astype(bf16)
        out, received = output_step(part_two, middle, ids[2])
        record = (hidden, normed, core_back, gated, attended, middle, normed_two, gate, up, activated)
        return out, received, record

    def backward(grad_out, record, ids, weights_too):
        hidden, normed, core_back, gated, attended, middle, normed_two, gate, up, activated = record
        feed_grad = cast_gather(grad_out, ids[0])
        activated_grad = product_t(feed_grad, w_down)
        gate_grad, up_grad = jax.vjp(swiglu, gate, up)[1](activated_grad)
        gate_grad = gate_grad.astype(bf16)
        up_grad = up_grad.astype(bf16)
        part = (product(gate_grad, w_gate) + product(up_grad, w_up)).astype(bf16)
        middle_grad, branch_grad, gain_two_grad = middle_back(part, middle, gain_two, grad_out, ids[1])
        core_grads = core_back(
            (product_t(branch_grad, w_mamba_out), product_t(branch_grad, w_att_out))
        )
        mamba_grad = core_grads[0].reshape(length, -1).astype(bf16)
        state_grad = core_grads[1].astype(bf16)
        step_grad = core_grads[2].astype(bf16)
        query_grad = core_grads[3].astype(bf16)
        keyval_grad = core_grads[4].reshape(length, -1).astype(bf16)
        shared_grad = jnp.concatenate([state_grad, keyval_grad], axis=1)
        part_two = (
            product(mamba_grad, w_mamba)
            + product(shared_grad, shared)
            + product(step_grad, w_step)
            + product(query_grad, w_query)
        ).astype(bf16)
        grad_in, received, gain_one_grad = input_back(
            part_two, hidden, gain_one, middle_grad, ids[2]
        )
        if not weights_too:
            return received
        step_slots = jnp.pad(step_grad.reshape(length, 4, 3), ((0, 0), (0, 0), (0, 13)))

        def by_y(values):
            return values.reshape(length, 4, -1)

        left_in = jnp.concatenate(
            [
                by_y(mamba_grad[:, :768]),
                by_y(mamba_grad[:, 768:]),
                by_y(query_grad),
                step_slots,
            ],
            axis=2,
        )
        left_branch = jnp.concatenate([by_y(gated), by_y(attended)], axis=2)
        left_two = jnp.concatenate([by_y(gate_grad), by_y(up_grad)], axis=2)

        def sums(left, right):
            return jnp.einsum("tyr,td->yrd", left, right, preferred_element_type=f32)

        grads = jnp.concatenate(
            [
                sums(left_in, normed),
                sums(left_branch, branch_grad),
                sums(left_two, normed_two),
                sums(by_y(activated), feed_grad),
                sums(by_y(shared_grad), normed),
            ],
            axis=1,
        ).astype(bf16)
        grads = (
            grads.reshape(4, ROWS_ALL, 2, 4, 128).transpose(0, 1, 3, 2, 4).reshape(4, ROWS_ALL, 1024)
        )
        heads = jnp.pad(jnp.concatenate(core_grads[7:10]), (0, 1024 - 36))
        small = jnp.concatenate(
            [
                gain_one_grad,
                gain_two_grad,
                core_grads[6].reshape(1, 1024),
                core_grads[5].reshape(3, 1024),
                heads[None],
                jnp.zeros((1, 1024), f32),
            ]
        )
        return grad_in, grads, small

    _, received, _ = forward(own, (3, 4, 5))
    hidden = jnp.where(is_first, own, received.astype(f32))
    out, _, record = forward(hidden, (6, 7, 8))
    received = backward(own, record, (9, 10, 11), False)
    grad_out = jnp.where(is_first, received.astype(f32), own)
    grad_in, grads, small = backward(grad_out, record, (12, 13, 14), True)
    reduced, shared_sum, small_sum = reduce_grads(grads, small, 15)

    section_output = from_chips(out.astype(bf16), 16).astype(f32)[None]
    input_grad = from_chips(grad_in.astype(bf16), 17).astype(f32)[None]

    lanes = lax.dynamic_slice_in_dim(reduced, core * 64, 64, 2)

    def rows(start, stop):
        return lanes[:, start:stop].reshape(-1, 64)

    def pair(first, second):
        return jnp.stack([rows(*first).T, rows(*second).T], axis=1)[None]

    shared_mine = lax.dynamic_slice_in_dim(shared_sum, core * 64 + y * 16, 16, 2)
    shared_mine = shared_mine.reshape(512, 16).T
    small_both = small_sum[0] + small_sum[1]
    tiny_at = (x_hi * 8 + z * 2 + core) * 4 + y
    gains = lax.dynamic_slice_in_dim(small_both[0:2], tiny_at * 16, 16, 1)
    conv_state_grad = lax.dynamic_slice_in_dim(small_both[2].reshape(4, 256), tiny_at * 4, 4, 1)
    conv_both = lax.dynamic_slice_in_dim(
        small_sum[:, 3:6].reshape(2, 4, 4, 192), y, 1, 2
    )[:, :, 0]
    conv_grad = conv_both.transpose(1, 0, 2).reshape(4, 384)
    heads_both = lax.dynamic_slice_in_dim(
        small_sum[:, 6, :36].reshape(2, 3, 4, 3), y, 1, 2
    )[:, :, 0]
    heads_grad = heads_both.transpose(1, 0, 2).reshape(3, 6)
    return (
        section_output,
        input_grad,
        gains[0][None],
        pair((0, 192), (192, 384)),
        shared_mine[:, :256][None],
        rows(448, 451).T[None],
        conv_grad[None],
        conv_state_grad[None],
        heads_grad[0][None],
        heads_grad[1][None],
        heads_grad[2][None],
        rows(384, 448).T[None],
        shared_mine[:, 256:].reshape(16, 2, 128)[None],
        rows(464, 656)[None],
        rows(656, 720)[None],
        gains[1][None],
        pair((720, 976), (976, 1232)),
        rows(1232, 1488)[None],
    )


def solution(mesh):
    in_specs = (
        P("dp", "tensor", None),
        P("dp", "tensor", None),
        P("section", None),
        P("section", None, None, "tensor"),
        P("section", None, None),
        P("section", None, "tensor"),
        P("section", None, "tensor"),
        P("section", None, None),
        P("section", "tensor"),
        P("section", "tensor"),
        P("section", "tensor"),
        P("section", None, "tensor"),
        P("section", None, None, None),
        P("section", "tensor", None),
        P("section", "tensor", None),
        P("section", None),
        P("section", None, None, "tensor"),
        P("section", "tensor", None),
    )
    out_specs = (
        P("section", "dp", "tensor", None),
        P("section", "dp", "tensor", None),
        P("section", ("dp", "tensor")),
        P("section", "dp", None, "tensor"),
        P("section", ("dp", "tensor"), None),
        P("section", "dp", "tensor"),
        P("section", None, "tensor"),
        P("section", None, ("dp", "tensor")),
        P("section", "tensor"),
        P("section", "tensor"),
        P("section", "tensor"),
        P("section", "dp", "tensor"),
        P("section", ("dp", "tensor"), None, None),
        P("section", "tensor", "dp"),
        P("section", "tensor", "dp"),
        P("section", ("dp", "tensor")),
        P("section", "dp", None, "tensor"),
        P("section", "tensor", "dp"),
    )
    return jax.shard_map(
        per_device, mesh=mesh, in_specs=in_specs, out_specs=out_specs, check_vma=False
    )
```

time: 3260 us -> 957 us (0.29)
  waiting for transfers between devices: 2230 us -> 0 us
  Pallas kernels: 0 us -> 380 us
  blocking collectives: 199 us -> 0 us
  matrix products: 405 us -> 237 us
  other arithmetic: 189 us -> 77.8 us
  local copies, waits for them, and re-layouts: 201 us -> 247 us
    unnamed x41 -> x0, waiting for transfers between devices: 1060 us -> none
    reduce_scatter x15 -> x0, waiting for transfers between devices: 842 us -> none  [the longest x12 374 us: reduce_rows(): return lax.psum_scatter(running, 'tensor', scatter_dimension=0, tiled=True)]
    pallas_call x0 -> x17, Pallas kernels: none -> 380 us  [kernel_call(): pl.pallas_call(body, name=name, out_shape=out_shape, in_specs=[pl.BlockSp...]
    all_gather x12 -> x0, waiting for transfers between devices: 261 us -> none  [spread(): return lax.all_gather(shard, 'tensor', axis=0, tiled=True)]
    dot_general x84 -> x47, matrix products: 356 us -> 180 us  [the longest x6 65.6 us: state_mix(): mixed = jnp.einsum('tsh,shp->thp', mixing, inputs)]
    unnamed x1 -> x0, blocking collectives: 165 us -> none
    ppermute x4 -> x0, waiting for transfers between devices: 61.9 us -> none  [passed_along(): return lax.ppermute(shard, axis, pairs)]
    reshape x1 -> x22, local copies, waits for them, and re-layouts: 0.61 us -> 53 us  [the longest x1 29 us: backward(): grads.reshape(4, ROWS_ALL, 2, 4, 128).transpose(0, 1, 3, 2, 4)]
  transfers between devices with their start and end apart: 38 -> 0, of which waited for: 36 -> 0; matrix products, arithmetic and copies ran while one was open for 6% -> 0% of each run, Pallas kernels for 0% -> 0%
where the time goes in v1:
time: 957 us; the launch traced here: 946 us
  Pallas kernels  380 us (40%)
  local copies, waits for them, and re-layouts  247 us (26%)
  matrix products  237 us (25%)
  other arithmetic  77.8 us (8%)
    pallas_call x17, Pallas kernels, kernel_call(): pl.pallas_call(body, name=name, out_shape=out_shape, in_specs=[pl.BlockSp...  380 us
    dot_general x6, matrix products, state_mix(): mixed = jnp.einsum('tsh,shp->thp', mixing, inputs)  65.6 us
    dot_general x18, matrix products, product(): return jnp.dot(left, right, preferred_element_type=jnp.float32)  57.8 us
    dot_general x17, matrix products, product_t(): lax.dot_general(left, right, (((1,), (1,)), ((), ())), preferred_element_...  53.2 us
    unnamed x361, local copies, waits for them, and re-layouts  48.1 us
    reshape x1, local copies, waits for them, and re-layouts, backward(): grads.reshape(4, ROWS_ALL, 2, 4, 128).transpose(0, 1, 3, 2, 4)  29 us
    dot_general x5, matrix products, sums(): return jnp.einsum('tyr,td->yrd', left, right, preferred_element_type=f32)  23.3 us
    concatenate x4, local copies, waits for them, and re-layouts, backward(): jnp.concatenate([sums(left_in, normed), sums(left_branch, branch_grad), s...  22.7 us

profile of v1, /device:TPU:0, one launch (start us, length us, event | category | flops | bytes accessed | tf_op | source)
XLA Modules:
  0.0 945.5 jit_solution(13093152698594808475)
XLA Ops:
  14.3 11.2 %to_chips.1 = bf16[320,1024]{1,0:T(8,128)(2,1)} custom-call(bf16[2,160,1024]{2,1,0:T(8,128)(2,1)} %broadcast_select_fusion.x_ref), custom_call_target="tpu_custom_call" | custom-call | tf_op jit(solution)/shard_map/to_chips/pallas_call | solution.py:66
  27.7 7.0 norm_gather.2
  43.7 4.7 cast_gather.2
  50.8 4.2 constant_dynamic-slice_fusion.21
  55.6 3.7 copy.240
  77.5 98.7 %gather_weights.1 = (bf16[4,720,1024]{2,1,0:T(8,128)(2,1)}, bf16[4,768,1024]{2,1,0:T(8,128)(2,1)}, f32[4,16,256]{2,1,0:T(8,128)}) custom-call(bf16[720,1024]{1,0:T(8,128)(2,1)} %bitcast_dynamic-update-slice_fusion.4.mix_ref, bf16[768,1024]{1,0:T(8,128)(2,1)} %pad_maximum_fusion.1.feed_ref, f32[16,256]{1,0:T(8,128)} %select_maximum_fusion.2.small_ref), custom_call_target="tpu_custom_call" | custom-call | tf_op jit(solution)/shard_map/gather_weights/pallas_call | solution.py:66
  176.2 5.8 fusion.288
  197.0 4.2 fusion.276
  201.2 5.6 reshape.512
  206.8 8.1 fusion.291
  218.1 5.2 copy.252
  223.3 8.6 fusion.114
  240.2 7.3 fusion.99.part_ref
  247.5 7.7 middle_step.2
  255.2 4.6 fusion.302
  259.8 6.8 convolution_convert_fusion.5.part_ref
  266.5 22.5 %output_step.2 = (f32[320,1024]{1,0:T(8,128)}, bf16[320,1024]{1,0:T(8,128)(2,1)}) custom-call(bf16[640,1024]{1,0:T(8,128)(2,1)} %convolution_convert_fusion.5.part_ref, f32[320,1024]{1,0:T(8,128)} %get-tuple-element.50.middle_ref), custom_call_target="tpu_custom_call" | custom-call | tf_op jit(solution)/shard_map/output_step/pallas_call | solution.py:66
  291.5 4.7 norm_gather.3
  315.5 4.2 fusion.275
  319.7 5.7 reshape.524
  325.4 7.9 fusion.290
  333.3 5.3 copy.261
  341.8 3.6 copy.257
  345.4 9.3 multiply_convert_fusion.4
  370.8 7.6 middle_step.3
  388.8 8.6 middle_back.2
  397.5 3.3 fusion.133
  402.3 4.9 fusion.211
  410.2 16.2 %fusion.17 = (f32[640,12]{0,1:T(8,128)S(1)}, f32[640,12]{0,1:T(8,128)}, f32[640,12]{0,1:T(8,128)}, bf16[640,640]{1,0:T(8,128)(2,1)}) fusion(f32[640,12]{0,1:T(8,128)S(1)} %get-tuple-element.277, f32[640,12]{0,1:T(8,128)S(1)} %bitcast.580, f32[640,640]{1,0:T(8,128)} %fusion.203, pred[640,640]{1,0:T(8,128)(4,1)S(1)} %copy-done.93, ...), kind=kOutput, calls=%fused_computation.23 | convolution fusion | flops 692610560 | bytes 6952960 | tf_op jit(solution)/shard_map/transpose(jvp(tsh,shp->thp))/dot_general | solution.py:822
  426.4 7.7 bitcast_add_fusion.5
  437.9 6.4 reduce-window.34
  454.8 4.0 copy.269
  458.8 6.2 fusion.274
  470.0 3.7 convert_reduce_fusion.1
  487.8 23.2 %input_back.2 = (f32[320,1024]{1,0:T(8,128)}, bf16[320,1024]{1,0:T(8,128)(2,1)}, f32[1,1024]{1,0:T(1,128)}) custom-call(bf16[640,1024]{1,0:T(8,128)(2,1)} %fusion.97.part_ref, f32[320,1024]{1,0:T(8,128)} %convert_select_fusion.1.hidden_ref, f32[1,1024]{1,0:T(1,128)} %convert_element_type.169.gain_ref, f32[320,1024]{1,0:T(8,128)} %get-tuple-element.60.grad_ref), custom_call_target="tpu_custom_call" | custom-call | tf_op jit(solution)/shard_map/input_back/pallas_call | solution.py:66
  513.6 4.6 cast_gather.3
  518.2 6.0 multiply_convert_fusion
  529.7 3.7 fusion.307
  540.8 8.3 middle_back.3
  549.1 22.6 %output_step.3 = (f32[320,1024]{1,0:T(8,128)}, bf16[320,1024]{1,0:T(8,128)(2,1)}) custom-call(bf16[640,1024]{1,0:T(8,128)(2,1)} %convolution_convert_fusion.4.part_ref, f32[320,1024]{1,0:T(8,128)} %get-tuple-element.53.middle_ref), custom_call_target="tpu_custom_call" | custom-call | tf_op jit(solution)/shard_map/output_step/pallas_call | solution.py:66
  573.9 6.0 multiply_reduce_fusion.4
  579.9 11.2 %from_chips.2 = bf16[2,160,1024]{2,1,0:T(8,128)(2,1)} custom-call(bf16[320,1024]{1,0:T(8,128)(2,1)} %convert_element_type.188.x_ref), custom_call_target="tpu_custom_call" | custom-call | tf_op jit(solution)/shard_map/from_chips/pallas_call | solution.py:66
  591.8 7.6 convolution_convert_fusion
  599.4 7.9 concatenate.75
  613.0 4.5 concatenate.73
  621.7 4.9 convolution_convert_fusion.2
  629.6 15.9 %fusion.19 = (f32[640,12]{0,1:T(8,128)S(1)}, f32[640,12]{0,1:T(8,128)S(1)}, f32[640,12]{0,1:T(8,128)}, bf16[640,640]{1,0:T(8,128)(2,1)}) fusion(f32[640,12]{0,1:T(8,128)S(1)} %copy-done.129, f32[640,12]{0,1:T(8,128)S(1)} %bitcast.582, f32[640,640]{1,0:T(8,128)} %fusion.203, pred[640,640]{1,0:T(8,128)(4,1)S(1)} %copy-done.94, f32[12,64,640]{2,1,0:T(8,128)} %bitcast.509, ...), kind=kOutput, calls=%fused_computation.25 | convolution fusion | flops 692610560 | bytes 6952960 | tf_op jit(solution)/shard_map/transpose(jvp(tsh,shp->thp))/dot_general | solution.py:822
  645.5 7.8 bitcast_add_fusion.4
  653.4 3.1 copy.277
  656.6 4.6 multiply_reduce_fusion.7
  661.3 6.6 reduce-window.36
  679.6 3.7 convert_reduce_fusion
  690.2 3.2 fusion.190
  707.0 4.3 fusion.273
  712.9 24.9 %input_back.3 = (f32[320,1024]{1,0:T(8,128)}, bf16[320,1024]{1,0:T(8,128)(2,1)}, f32[1,1024]{1,0:T(1,128)}) custom-call(bf16[640,1024]{1,0:T(8,128)(2,1)} %fusion.96.part_ref, f32[320,1024]{1,0:T(8,128)} %convert_select_fusion.1.hidden_ref, f32[1,1024]{1,0:T(1,128)} %convert_element_type.169.gain_ref, f32[320,1024]{1,0:T(8,128)} %get-tuple-element.67.grad_ref), custom_call_target="tpu_custom_call" | custom-call | tf_op jit(solution)/shard_map/input_back/pallas_call | solution.py:66
  740.0 10.7 %from_chips.3 = bf16[2,160,1024]{2,1,0:T(8,128)(2,1)} custom-call(bf16[320,1024]{1,0:T(8,128)(2,1)} %convert_element_type.212.x_ref), custom_call_target="tpu_custom_call" | custom-call | tf_op jit(solution)/shard_map/from_chips/pallas_call | solution.py:66
  752.5 4.6 convolution_convert_fusion.1
  757.1 8.2 concatenate.71
  766.5 8.1 copy_dynamic-update-slice_fusion.1
  774.6 3.5 copy_dynamic-update-slice_fusion.3
  778.1 6.3 copy_dynamic-update-slice_fusion
  784.4 5.4 copy_dynamic-update-slice_fusion.2
  791.9 29.0 %reshape.560.grads = bf16[4,1616,1024]{2,1,0:T(8,128)(2,1)} reshape(bf16[4,1616,4,2,128]{4,3,2,1,0:T(2,128)(2,1)} %bitcast.471) | data formatting | bytes 26476544 | tf_op jit(solution)/shard_map/reshape | solution.py:1049
  820.9 101.7 %reduce_grads.1 = (f32[2,1616,128]{2,1,0:T(8,128)}, f32[4,128,128]{2,1,0:T(8,128)}, f32[2,8,1024]{2,1,0:T(8,128)}) custom-call(bf16[4,1616,1024]{2,1,0:T(8,128)(2,1)} %reshape.560.grads, f32[8,1024]{1,0:T(8,128)} %concatenate.78.small_ref), custom_call_target="tpu_custom_call" | custom-call | tf_op jit(solution)/shard_map/reduce_grads/pallas_call | solution.py:66
  (612 shorter events, 254.8 us)
Async XLA Ops:
  0.7 11.8 %copy-start = (bf16[1,512,1024]{2,1,0:T(8,128)(2,1)S(1)}, bf16[1,512,1024]{2,1,0:T(8,128)(2,1)}, u32[]{:S(2)}) copy-start(bf16[1,512,1024]{2,1,0:T(8,128)(2,1)} %param.35) | copy-start | bytes 3145732
  0.7 12.7 %copy-start.89 = (bf16[2,160,1024]{2,1,0:T(8,128)(2,1)S(1)}, bf16[2,160,1024]{2,1,0:T(8,128)(2,1)}, u32[]{:S(2)}) copy-start(bf16[2,160,1024]{2,1,0:T(8,128)(2,1)} %param.19) | copy-start | bytes 1966084
  0.7 12.7 %copy-start.88 = (bf16[2,160,1024]{2,1,0:T(8,128)(2,1)S(1)}, bf16[2,160,1024]{2,1,0:T(8,128)(2,1)}, u32[]{:S(2)}) copy-start(bf16[2,160,1024]{2,1,0:T(8,128)(2,1)} %param.18) | copy-start | bytes 1966084
  6.6 35.1 %copy-start.131 = (f32[1,1,256]{2,1,0:T(1,128)}, f32[1,1,256]{2,1,0:T(1,128)S(1)}, u32[]{:S(2)}) copy-start(f32[1,1,256]{2,1,0:T(1,128)S(1)} %get-tuple-element.265) | copy-start | bytes 3076
  6.6 35.1 %copy-start.134 = (f32[1,1,256]{2,1,0:T(1,128)}, f32[1,1,256]{2,1,0:T(1,128)S(1)}, u32[]{:S(2)}) copy-start(f32[1,1,256]{2,1,0:T(1,128)S(1)} %get-tuple-element.266) | copy-start | bytes 3076
  6.6 35.1 %copy-start.137 = (f32[1,1,256]{2,1,0:T(1,128)}, f32[1,1,256]{2,1,0:T(1,128)S(1)}, u32[]{:S(2)}) copy-start(f32[1,1,256]{2,1,0:T(1,128)S(1)} %get-tuple-element.267) | copy-start | bytes 3076
  6.6 35.1 %copy-start.140 = (f32[1,1,256]{2,1,0:T(1,128)}, f32[1,1,256]{2,1,0:T(1,128)S(1)}, u32[]{:S(2)}) copy-start(f32[1,1,256]{2,1,0:T(1,128)S(1)} %get-tuple-element.268) | copy-start | bytes 3076
  8.9 31.1 %copy-start.19 = (f32[640,32]{0,1:T(8,128)}, f32[640,32]{0,1:T(8,128)S(1)}, u32[]{:S(2)}) copy-start(f32[640,32]{0,1:T(8,128)S(1)} %get-tuple-element.271) | copy-start | bytes 245764
  8.9 31.1 %copy-start.22 = (f32[640,32]{0,1:T(8,128)}, f32[640,32]{0,1:T(8,128)S(1)}, u32[]{:S(2)}) copy-start(f32[640,32]{0,1:T(8,128)S(1)} %get-tuple-element.272) | copy-start | bytes 245764
  12.5 12.9 %copy-start.47 = (bf16[1,1024,2,128]{3,2,1,0:T(2,128)(2,1)S(1)}, bf16[1,1024,2,128]{3,2,1,0:T(2,128)(2,1)}, u32[]{:S(2)}) copy-start(bf16[1,1024,2,128]{3,2,1,0:T(2,128)(2,1)} %param.30) | copy-start | bytes 1572868
  26.3 8.4 copy-start.104
  26.3 8.4 copy-start.108
  26.5 8.2 copy-start.154
  42.1 6.2 copy-start.26
  55.6 10.6 %copy-start.11 = (bf16[1,1024,2,512]{3,2,1,0:T(2,128)(2,1)S(1)}, bf16[1,1024,2,512]{3,2,1,0:T(2,128)(2,1)}, u32[]{:S(2)}) copy-start(bf16[1,1024,2,512]{3,2,1,0:T(2,128)(2,1)} %param.34) | copy-start | bytes 6291460
  59.3 5.5 copy-start.112
  59.3 6.3 copy-start.126
  176.2 9.0 copy-start.31
  183.7 39.6 %copy-start.149 = (f32[12]{0:T(128)}, f32[12]{0:T(128)S(1)}, u32[]{:S(2)}) copy-start(f32[12]{0:T(128)S(1)} %mul.1275) | copy-start | bytes 148
  183.9 31.2 %copy-start.117 = (f32[768]{0:T(1024)}, f32[768]{0:T(1024)S(1)}, u32[]{:S(2)}) copy-start(f32[768]{0:T(1024)S(1)} %mul.1243) | copy-start | bytes 9220
  184.0 114.2 %copy-start.143 = (f32[12]{0:T(128)}, f32[12]{0:T(128)S(1)}, u32[]{:S(2)}) copy-start(f32[12]{0:T(128)S(1)} %exp.90) | copy-start | bytes 148
  184.1 31.0 %copy-start.114 = (f32[768]{0:T(1024)}, f32[768]{0:T(1024)S(1)}, u32[]{:S(2)}) copy-start(f32[768]{0:T(1024)S(1)} %mul.1252) | copy-start | bytes 9220
  184.2 30.9 %copy-start.120 = (f32[768]{0:T(1024)}, f32[768]{0:T(1024)S(1)}, u32[]{:S(2)}) copy-start(f32[768]{0:T(1024)S(1)} %mul.1249) | copy-start | bytes 9220
  184.3 30.8 %copy-start.123 = (f32[768]{0:T(1024)}, f32[768]{0:T(1024)S(1)}, u32[]{:S(2)}) copy-start(f32[768]{0:T(1024)S(1)} %mul.1246) | copy-start | bytes 9220
  185.2 111.0 %copy-start.82 = (bf16[12,1024]{1,0:T(8,128)(2,1)}, bf16[12,1024]{1,0:T(8,128)(2,1)S(1)}, u32[]{:S(2)}) copy-start(bf16[12,1024]{1,0:T(8,128)(2,1)S(1)} %reshape.514) | copy-start | bytes 73732
  218.1 5.2 copy-start.61
  223.3 8.7 copy-start.69
  247.5 7.7 copy-start.51
  298.1 128.2 %copy-start.128 = (f32[640,12]{0,1:T(8,128)}, f32[640,12]{0,1:T(8,128)S(1)}, u32[]{:S(2)}) copy-start(f32[640,12]{0,1:T(8,128)S(1)} %get-tuple-element.277) | copy-start | bytes 92164
  307.8 4.9 copy-start.27
  314.0 132.1 %copy-start.32 = (bf16[640,256]{1,0:T(8,128)(2,1)}, bf16[640,256]{1,0:T(8,128)(2,1)S(1)}, u32[]{:S(2)}) copy-start(bf16[640,256]{1,0:T(8,128)(2,1)S(1)} %get-tuple-element.187) | copy-start | bytes 983044
  333.3 5.4 copy-start.5
  341.8 232.1 %copy-start.4 = (f32[640,768]{1,0:T(8,128)}, f32[640,768]{1,0:T(8,128)S(1)}, u32[]{:S(2)}) copy-start(f32[640,768]{1,0:T(8,128)S(1)} %get-tuple-element.190) | copy-start | bytes 5898244
  345.4 9.3 copy-start.15
  370.8 7.6 copy-start.52
  388.8 13.5 %copy-start.57 = (f32[640,768]{1,0:T(8,128)S(1)}, f32[640,768]{1,0:T(8,128)}, u32[]{:S(2)}) copy-start(f32[640,768]{1,0:T(8,128)} %copy.268) | copy-start | bytes 5898244
  410.2 16.2 %copy-start.62 = (f32[640,768]{0,1:T(8,128)S(1)}, f32[640,768]{0,1:T(8,128)}, u32[]{:S(2)}) copy-start(f32[640,768]{0,1:T(8,128)} %copy.265) | copy-start | bytes 5898244
  410.2 16.2 %copy-start.63 = (f32[640,640]{1,0:T(8,128)S(1)}, f32[640,640]{1,0:T(8,128)}, u32[]{:S(2)}) copy-start(f32[640,640]{1,0:T(8,128)} %fusion.203) | copy-start | bytes 4915204
  437.0 10.7 %copy-start.29 = (f32[640,256]{1,0:T(8,128)S(1)}, f32[640,256]{1,0:T(8,128)}, u32[]{:S(2)}) copy-start(f32[640,256]{1,0:T(8,128)} %get-tuple-element.188) | copy-start | bytes 1966084
  458.8 6.2 copy-start.34
  458.8 6.2 copy-start.74
  487.8 23.2 %copy-start.10 = (bf16[320,1024]{1,0:T(8,128)(2,1)S(1)}, bf16[320,1024]{1,0:T(8,128)(2,1)}, u32[]{:S(2)}) copy-start(bf16[320,1024]{1,0:T(8,128)(2,1)} %to_chips.1) | copy-start | bytes 1966084
  511.0 7.2 copy-start.54
  549.1 24.9 %copy-start.18 = (f32[640,1,768]{2,1,0:T(1,128)S(1)}, f32[640,1,768]{2,1,0:T(1,128)}, u32[]{:S(2)}) copy-start(f32[640,1,768]{2,1,0:T(1,128)} %get-tuple-element.205) | copy-start | bytes 5898244
  549.1 24.9 %copy-start.58 = (f32[640,768]{1,0:T(8,128)S(1)}, f32[640,768]{1,0:T(8,128)}, u32[]{:S(2)}) copy-start(f32[640,768]{1,0:T(8,128)} %copy.268) | copy-start | bytes 5898244
  599.4 7.9 copy-start.153
  613.0 5.3 copy-start.43
  613.0 6.0 copy-start.36
  629.6 15.9 %copy-start.60 = (f32[640,768]{0,1:T(8,128)S(1)}, f32[640,768]{0,1:T(8,128)}, u32[]{:S(2)}) copy-start(f32[640,768]{0,1:T(8,128)} %copy.276) | copy-start | bytes 5898244
  629.6 15.9 %copy-start.64 = (f32[640,640]{1,0:T(8,128)S(1)}, f32[640,640]{1,0:T(8,128)}, u32[]{:S(2)}) copy-start(f32[640,640]{1,0:T(8,128)} %fusion.203) | copy-start | bytes 4915204
  629.6 15.9 %copy-start.151 = (f32[12]{0:T(128)S(1)}, f32[12]{0:T(128)}, u32[]{:S(2)}) copy-start(f32[12]{0:T(128)} %copy-done.149) | copy-start | bytes 148
  656.5 11.6 %copy-start.127 = (f32[640,12]{0,1:T(8,128)S(1)}, f32[640,12]{0,1:T(8,128)}, u32[]{:S(2)}) copy-start(f32[640,12]{0,1:T(8,128)} %get-tuple-element.150) | copy-start | bytes 92164
  656.5 11.7 %copy-start.145 = (f32[12]{0:T(128)S(1)}, f32[12]{0:T(128)}, u32[]{:S(2)}) copy-start(f32[12]{0:T(128)} %copy-done.143) | copy-start | bytes 148
  656.5 11.9 %copy-start.148 = (f32[12]{0:T(128)S(1)}, f32[12]{0:T(128)}, u32[]{:S(2)}) copy-start(f32[12]{0:T(128)} %reduce_sum.359) | copy-start | bytes 148
  661.2 8.9 copy-start.33
  661.2 10.5 %copy-start.28 = (f32[640,256]{1,0:T(8,128)S(1)}, f32[640,256]{1,0:T(8,128)}, u32[]{:S(2)}) copy-start(f32[640,256]{1,0:T(8,128)} %copy-done.27) | copy-start | bytes 1966084
  661.2 10.5 %copy-start.30 = (f32[640,256]{1,0:T(8,128)S(1)}, f32[640,256]{1,0:T(8,128)}, u32[]{:S(2)}) copy-start(f32[640,256]{1,0:T(8,128)} %get-tuple-element.188) | copy-start | bytes 1966084
  737.7 13.0 %copy-start.146 = (f32[1,1024]{1,0:T(1,128)S(1)}, f32[1,1024]{1,0:T(1,128)}, u32[]{:S(2)}) copy-start(f32[1,1024]{1,0:T(1,128)} %get-tuple-element.70) | copy-start | bytes 12292
  737.7 13.0 %copy-start.147 = (f32[1,1024]{1,0:T(1,128)S(1)}, f32[1,1024]{1,0:T(1,128)}, u32[]{:S(2)}) copy-start(f32[1,1024]{1,0:T(1,128)} %get-tuple-element.69) | copy-start | bytes 12292
  757.1 8.2 copy-start.37
  766.5 8.1 copy-start.12
  784.4 5.4 copy-start.80
  922.6 12.7 %copy-start.72 = (f32[2,1616,128]{2,1,0:T(8,128)S(1)}, f32[2,1616,128]{2,1,0:T(8,128)}, u32[]{:S(2)}) copy-start(f32[2,1616,128]{2,1,0:T(8,128)} %get-tuple-element.72) | copy-start | bytes 4964356
  936.2 8.8 copy-start.1
  (104 other events, 278.8 us)

commit v2 on v0

v2 whole, which is shorter than its diff:
```python
import functools
import math
import types

import jax
import jax.numpy as jnp
from jax import lax
from jax.experimental import pallas as pl
from jax.experimental.pallas import tpu as pltpu
from jax.sharding import PartitionSpec as P

ROWS_MIX = 720
ROWS_FEED = 768
ROWS_OUT = 704
ROWS_SHARED = 128
ROWS_EXTRA = ROWS_SHARED + 16
ROWS_ALL = ROWS_FEED + ROWS_OUT + ROWS_EXTRA

MESH = pl.DeviceIdType.MESH
DMA = pltpu.SemaphoreType.DMA
bf16 = jnp.bfloat16
f32 = jnp.float32
VMEM = pltpu.VMEM
ANY = pl.ANY
HIGH = lax.Precision.HIGHEST
CHUNK = 128
CHUNKS = 5
LANES = 192
NN = ((1,), (0,))
NT = ((1,), (1,))
TN = ((0,), (0,))

rope_base = 100000000000.0
norm_eps = 1e-05


SECTION, DP, TENSOR = "section", "dp", "tensor"


def place():
    section = lax.axis_index(SECTION)
    dp = lax.axis_index(DP)
    y = lax.axis_index(TENSOR)
    return section, dp // 8, (dp // 2) % 4, dp % 2, y


def at_y(y):
    return {TENSOR: y}


def at_z(x_hi, z, core):
    return {DP: x_hi * 8 + z * 2 + core}


def greet(partners):
    barrier = pltpu.get_barrier_semaphore()
    for partner in partners:
        pl.semaphore_signal(barrier, inc=1, device_id=partner, device_id_type=MESH)
    pl.semaphore_wait(barrier, len(partners))


def remote(src, dst, send_sem, recv_sem, partner):
    return pltpu.make_async_remote_copy(
        src_ref=src,
        dst_ref=dst,
        send_sem=send_sem,
        recv_sem=recv_sem,
        device_id=partner,
        device_id_type=MESH,
    )


class Copies:
    def __init__(self, send, recv):
        self.send, self.recv, self.table, self.gone = send, recv, {}, set()

    def add(self, name, src, dst, partner):
        self.table[name] = (src, dst, len(self.table), partner)

    def of(self, name):
        src, dst, n, partner = self.table[name]
        return remote(src, dst, self.send.at[n], self.recv.at[n], partner)

    def start(self, *names):
        for name in names:
            self.of(name).start()

    def arrive(self, *names):
        for name in names:
            self.of(name).wait_recv()

    def left(self, *names):
        for name in names:
            self.of(name).wait_send()
            self.gone.add(name)

    def leave(self):
        self.left(*(name for name in self.table if name not in self.gone))


def shape(dims, kind):
    return jax.ShapeDtypeStruct(dims, kind)


def kernel_call(body, name, collective, out_shape, args, scratch, in_spaces=None, out_spaces=None):
    in_spaces = in_spaces or [VMEM] * len(args)
    outs = out_shape if isinstance(out_shape, (list, tuple)) else [out_shape]
    out_spaces = out_spaces or [VMEM] * len(outs)
    out_specs = [pl.BlockSpec(memory_space=space) for space in out_spaces]
    return pl.pallas_call(
        body,
        name=name,
        out_shape=out_shape,
        in_specs=[pl.BlockSpec(memory_space=space) for space in in_spaces],
        out_specs=out_specs if isinstance(out_shape, (list, tuple)) else out_specs[0],
        scratch_shapes=scratch,
        compiler_params=pltpu.CompilerParams(
            collective_id=collective, has_side_effects=True, vmem_limit_bytes=56 * 2**20
        ),
    )(*args)


def mm(left, right, dims, precision=None):
    return lax.dot_general(
        left, right, (dims, ((), ())), precision=precision, preferred_element_type=f32
    )


class Swap:
    def __init__(self, send, recv, local):
        _, x_hi, z, core, y = place()
        self.send, self.recv, self.local = send, recv, local
        self.bit = y % 2
        self.own = y // 2 == core
        self.partners = [
            {TENSOR: 2 * core + n, DP: x_hi * 8 + z * 2 + y // 2} for n in (0, 1)
        ]

    def stays(self, n):
        return jnp.logical_and(self.own, self.bit == n)

    def greet(self, others):
        barrier = pltpu.get_barrier_semaphore()
        for partner in others:
            pl.semaphore_signal(barrier, inc=1, device_id=partner, device_id_type=MESH)
        for n in (0, 1):

            @pl.when(jnp.logical_not(self.stays(n)))
            def _():
                pl.semaphore_signal(
                    barrier, inc=1, device_id=self.partners[n], device_id_type=MESH
                )

        @pl.when(self.own)
        def _():
            pl.semaphore_wait(barrier, len(others) + 1)

        @pl.when(jnp.logical_not(self.own))
        def _():
            pl.semaphore_wait(barrier, len(others) + 2)

    def start(self, block, slot, condition=None):
        def also(test):
            return test if condition is None else jnp.logical_and(test, condition)

        for n in (0, 1):

            @pl.when(also(self.stays(n)))
            def _():
                pltpu.make_async_copy(block(n), slot(self.bit), self.local.at[0]).start()

            @pl.when(also(jnp.logical_not(self.stays(n))))
            def _():
                remote(
                    block(n), slot(self.bit), self.send.at[n], self.recv.at[self.bit], self.partners[n]
                ).start()

    def wait(self, block, slot):
        for n in (0, 1):

            @pl.when(self.stays(n))
            def _():
                pltpu.make_async_copy(block(n), slot(n), self.local.at[0]).wait()

            @pl.when(jnp.logical_not(self.stays(n)))
            def _():
                copy = remote(block(n), slot(n), self.send.at[n], self.recv.at[n], self.partners[n])
                copy.wait_send()
                copy.wait_recv()


SWAP_SCRATCH = [DMA((2,)), DMA((2,)), DMA((1,))]


def block_of(ref):
    return lambda n: ref.at[n]


def rows_block(ref):
    rows = ref.shape[0] // 2

    def view(n):
        start = n * rows if isinstance(n, int) else pl.multiple_of(n * rows, rows)
        return ref.at[pl.ds(start, rows)]

    return view


class Gather:
    def __init__(self, src, out, straight, copies, local):
        _, x_hi, z, core, y = place()
        self.right, self.left, self.across = (y + 1) % 4, (y + 3) % 4, (y + 2) % 4
        y_right, y_left = at_y(self.right), at_y(self.left)
        z_right, z_left = at_z(x_hi, (z + 1) % 4, core), at_z(x_hi, (z + 3) % 4, core)
        self.partners = [y_right, y_left, z_right, z_left]
        self.copies, self.local = copies, local
        self.src, self.out, self.y = src, out, y
        rows = (src.shape[0] - straight) // 4
        cut = rows // 32 * 16

        def at(start, count):
            return pl.ds(pl.multiple_of(start, 16), count)

        def ring(name, start, count, first_cut):
            own = src.at[at(start, count)]
            there = out.at[y, at(start, count)]
            copies.add(name + "r", own, there, y_right)
            copies.add(name + "l", own, there, y_left)
            one = out.at[self.left, at(start, first_cut)]
            two = out.at[self.right, at(start + first_cut, count - first_cut)]
            copies.add(name + "rr", one, one, y_right)
            copies.add(name + "ll", two, two, y_left)

        base = straight + z * rows
        ring("h", base, rows, cut)
        ring("s", 0, straight, straight // 32 * 16)
        for name, k in (("zl", self.left), ("zr", self.right), ("za", self.across)):
            own = out.at[k, at(base, rows)]
            copies.add(name + "r", own, own, z_right)
            copies.add(name + "l", own, own, z_left)
            one = out.at[k, at(straight + (z + 3) % 4 * rows, cut)]
            two = out.at[k, at(straight + (z + 1) % 4 * rows + cut, rows - cut)]
            copies.add(name + "rr", one, one, z_right)
            copies.add(name + "ll", two, two, z_left)

    def own(self):
        return pltpu.make_async_copy(self.src, self.out.at[self.y], self.local)

    def one(self):
        self.own().start()
        self.copies.start("hr", "hl")

    def two(self):
        c = self.copies
        c.arrive("hr")
        c.start("hrr", "zlr", "zll")
        c.arrive("hl")
        c.start("hll", "zrr", "zrl")
        c.start("sr", "sl")

    def three(self):
        c = self.copies
        c.arrive("hrr", "hll")
        c.start("zar", "zal")
        c.arrive("zlr")
        c.start("zlrr")
        c.arrive("zll")
        c.start("zlll")
        c.arrive("zrr")
        c.start("zrrr")
        c.arrive("zrl")
        c.start("zrll")

    def four(self):
        c = self.copies
        c.arrive("sr")
        c.start("srr")
        c.arrive("sl")
        c.start("sll")
        c.arrive("zar")
        c.start("zarr")
        c.arrive("zal")
        c.start("zall")

    def end(self):
        self.copies.arrive(
            "zlrr", "zlll", "zrrr", "zrll", "srr", "sll", "zarr", "zall"
        )
        self.copies.leave()
        self.own().wait()


GATHER_SCRATCH = [DMA((20,)), DMA((20,)), DMA((1,))]
MIX_STRAIGHT = 208
FEED_STRAIGHT = 256


def other_core(x_hi, z, core):
    return at_z(x_hi, z, 1 - core)


def inverse_rms(values):
    return lax.rsqrt(jnp.mean(values * values, axis=-1, keepdims=True) + norm_eps)


def my_rows(core, rows):
    return pl.ds(pl.multiple_of(core * rows, rows), rows)


def sigmoid(v):
    return 1.0 / (1.0 + jnp.exp(-v))


def softplus(v):
    return jnp.maximum(v, 0.0) + jnp.log1p(jnp.exp(-jnp.abs(v)))


def softplus_slope(value):
    near = value * (1.0 - 0.5 * value * (1.0 - value * (1.0 / 3.0)))
    return jnp.where(value < 0.01, near, 1.0 - jnp.exp(-value))


def iota(dims, axis):
    return lax.broadcasted_iota(jnp.int32, dims, axis)


def spread_heads(columns, rows):
    lane = iota((rows, LANES), 1)
    return jnp.where(
        lane < 64, columns[:, 0:1], jnp.where(lane < 128, columns[:, 1:2], columns[:, 2:3])
    )


def head_lanes(values, head):
    lane = iota(values.shape, 1)
    return jnp.where(jnp.logical_and(lane >= 64 * head, lane < 64 * head + 64), values, 0.0)


def in_lane(column, lane_at, rows):
    return jnp.where(iota((rows, 16), 1) == lane_at, column, 0.0)


def conv_taps(window, kernel):
    total = window[5 : 5 + CHUNK] * kernel[0:1]
    for k in range(1, 4):
        total = total + window[5 + k : 5 + k + CHUNK] * kernel[k : k + 1]
    return total


def masks_of(rows):
    return iota((rows, rows), 0) >= iota((rows, rows), 1)


def prepare_steps(normed_ref, step_rows, smalls, step_cols, dt_row, cum_row):
    raw = mm(normed_ref[...], jnp.concatenate([step_rows[k] for k in range(4)], axis=0), NT)

    def line(row):
        return jnp.concatenate([smalls[k, row : row + 1, 0:16] for k in range(4)], axis=1)

    dt = softplus(raw + line(4))
    a = -dt * jnp.exp(line(5))
    upto = masks_of(CHUNK).astype(f32)
    fill = jnp.zeros((CHUNK, 64), f32)
    for n in range(CHUNKS):
        at = pl.ds(n * CHUNK, CHUNK)
        dt_n = dt[n * CHUNK : (n + 1) * CHUNK]
        cum = mm(upto, a[n * CHUNK : (n + 1) * CHUNK], NN, HIGH)
        for k in range(4):
            own = slice(16 * k, 16 * k + 8)
            step_cols[k, at] = jnp.concatenate([dt_n[:, own], cum[:, own]], axis=1)
        both = jnp.concatenate([dt_n, cum], axis=1).T
        dt_row[:, at] = both[0:64]
        cum_row[:, at] = both[64:128]


def shared_forward(normed_ref, shared_ref, state_conv_ref, state_pad, b_ref, c_ref, b_turn):
    state_pad[0:8] = jnp.zeros((8, 256), f32)
    state_pad[pl.ds(8, 640)] = mm(normed_ref[...], shared_ref[0:256], NT)
    kernel = state_conv_ref[...]
    for n in range(CHUNKS):
        at = pl.ds(n * CHUNK, CHUNK)
        pre = conv_taps(state_pad[pl.ds(n * CHUNK, CHUNK + 8)], kernel)
        bc = pre * sigmoid(pre)
        b_ref[at] = bc[:, 0:128].astype(bf16)
        c_ref[at] = bc[:, 128:256].astype(bf16)
        b_turn[:, at] = bc[:, 0:128].T.astype(bf16)


def turn_into(out_ref, values):
    for n in range(CHUNKS):
        out_ref[:, pl.ds(n * CHUNK, CHUNK)] = (
            values[n * CHUNK : (n + 1) * CHUNK].astype(f32).T.astype(out_ref.dtype)
        )


def exchanged(rows):
    return jnp.concatenate([rows[32:64], rows[0:32]], axis=0)


def turned_heads(first, second, table_ref):
    return first * table_ref[:, 0:128] + second * table_ref[:, 128:256]


def keys_values(normed_ref, shared_ref, head, table_ref, key_ref, value_ref, value_turn):
    start = pl.multiple_of(head * 64, 64)
    key_rows = shared_ref[pl.ds(256 + start, 64)]
    value_rows = shared_ref[pl.ds(384 + start, 64)]
    rows = jnp.concatenate([value_rows, key_rows, value_rows, exchanged(key_rows)], axis=0)
    out = mm(normed_ref[...], rows, NT)
    key_ref[...] = turned_heads(out[:, 0:128], out[:, 128:256], table_ref).astype(bf16)
    values = jnp.where(iota((640, 128), 1) < 64, out[:, 0:128], 1.0)
    value_ref[...] = values.astype(bf16)
    turn_into(value_turn, values)


def mixer_rows(w):
    query_rows = w[384:448]
    return jnp.concatenate([w[0:192], query_rows, w[192:384], exchanged(query_rows)], axis=0)


QUERY_BLOCKS = ((0, 256), (256, 640))


def scores_of(key_ref, query_ref, first, last):
    scores = mm(key_ref[0:last], query_ref[first:last], NT)
    dims = scores.shape
    return jnp.where(iota(dims, 0) <= iota(dims, 1) + first, scores, -1e30)


def attend(query_ref, key_ref, value_turn, att):
    for first, last in QUERY_BLOCKS:
        scores = scores_of(key_ref, query_ref, first, last)
        top = jnp.max(scores, axis=0, keepdims=True)
        weights = jnp.exp(scores - top).astype(bf16)
        both = mm(value_turn[:, 0:last], weights, NN)
        out = both * (1.0 / both[64:65])
        for n in range(first // CHUNK, last // CHUNK):
            at = n * CHUNK - first
            att[pl.ds(n * CHUNK, CHUNK)] = out[:, at : at + CHUNK].T.astype(bf16)


def store_turned(out_ref, rows, values):
    for k in range(4):
        for x in range(2):
            out_ref[rows, pl.ds((2 * k + x) * 128, 128)] = values[
                :, (4 * x + k) * 128 : (4 * x + k + 1) * 128
            ].astype(bf16)


def silu_slope(pre, s):
    return s * (1.0 + pre * (1.0 - s))


def conv_back(after, kernel):
    total = after[3 : 3 + CHUNK] * kernel[0:1]
    for k in range(1, 4):
        total = total + after[3 - k : 3 - k + CHUNK] * kernel[k : k + 1]
    return total


def column_sum(values):
    return jnp.sum(values, axis=0, keepdims=True)


def attend_back(
    query_ref, key_ref, key_turn, value_ref, value_turn, grad_ref, att_turn, pairs_ref, key_grad, value_grad, table_ref
):
    for first, last in QUERY_BLOCKS:
        query = query_ref[first:last]
        grad = grad_ref[first:last]
        scores = scores_of(key_ref, query_ref, first, last)
        top = jnp.max(scores, axis=0, keepdims=True)
        weights = jnp.exp(scores - top)
        weights = weights * (1.0 / jnp.sum(weights, axis=0, keepdims=True))
        weights_low = weights.astype(bf16)
        att_turn[:, first:last] = mm(value_turn[0:64, 0:last], weights_low, NN).astype(bf16)
        slope = mm(value_ref[0:last], grad, NT)
        inner = jnp.sum(weights * slope, axis=0, keepdims=True)
        slope = (weights * (slope - inner)).astype(bf16)
        key_grad[0:last] += mm(slope, query, NN)
        value_grad[0:last] += mm(weights_low, grad, NN)
        query_grad = mm(key_turn[:, 0:last], slope, NN) * 0.125
        for n in range(first // CHUNK, last // CHUNK):
            at = pl.ds(n * CHUNK, CHUNK)
            turned = query_grad[:, n * CHUNK - first : (n + 1) * CHUNK - first].T
            pairs_ref[at, 192:256] = (turned * table_ref[at, 0:128]).astype(bf16)[:, 64:128]
            pairs_ref[at, 448:512] = (turned * table_ref[at, 128:256]).astype(bf16)[:, 64:128]


def rms_back(values, gain, grad):
    scale = inverse_rms(values)
    weighted = grad * gain
    unit = values * scale
    inner = jnp.mean(weighted * unit, axis=-1, keepdims=True)
    return scale * (weighted - unit * inner), jnp.sum(grad * unit, axis=0, keepdims=True)


REST = ROWS_OUT + ROWS_EXTRA
SMALL_ROWS = 80


def add_into(dst, sources, strip=None):
    if len(dst.shape) == 3:
        for k in range(dst.shape[0]):
            add_into(dst.at[k], [source.at[k] for source in sources], strip)
        return
    rows, width = dst.shape
    if strip is None:
        most = max(16, 65536 // width)
        strip = max(n for n in range(16, min(most, rows) + 1, 16) if rows % n == 0)

    def step(n, carry):
        at = pl.ds(pl.multiple_of(n * strip, 16), strip)
        total = sources[0][at].astype(f32)
        for source in sources[1:]:
            total = total + source[at].astype(f32)
        dst[at] = total.astype(dst.dtype)
        return carry

    lax.fori_loop(0, rows // strip, step, 0)


class RingSum:
    def __init__(self, name, copies, me, right, left, to_right, to_left, block, land, more=()):
        across = (me + 2) % 4
        self.name, self.copies, self.block, self.land = name, copies, block, land
        self.right, self.left, self.me = right, left, me
        copies.add(name + "a", block(across, 0), land(0, 0), to_right)
        copies.add(name + "b", block(across, 1), land(0, 1), to_left)
        copies.add(name + "c", land(0, 0), land(1, 0), to_right)
        copies.add(name + "d", land(0, 1), land(2, 1), to_left)
        copies.add(name + "e", block(right, 1), land(1, 1), to_right)
        copies.add(name + "f", block(left, 0), land(2, 0), to_left)

    def names(self, letters):
        return [self.name + letter for letter in letters]

    def start_far(self):
        self.copies.start(*self.names("ab"))

    def start_near(self):
        self.copies.start(*self.names("ef"))

    def start(self):
        self.start_far()
        self.start_near()

    def pass_on(self, mine_right, mine_left):
        for letter, mine, half, then in (("a", mine_right, 0, "c"), ("b", mine_left, 1, "d")):
            self.copies.arrive(self.name + letter)
            landed = self.land(0, half)
            add_into(landed, (mine, landed))
            self.copies.start(self.name + then)

    def arrive(self):
        self.copies.arrive(*self.names("efcd"))

    def drained(self):
        self.copies.left(*self.names("abef"))


def lanes_of(k, width):
    return pl.ds(pl.multiple_of(k * width, width), width)


def halves(rows, cut):
    return (pl.ds(0, cut), pl.ds(cut, rows - cut))


PAIRS = (pl.ds(0, 2), pl.ds(2, 2))
HALF_FEED = ROWS_FEED // 2
FEED_SUM = dict(
    sum_send=DMA((56,)),
    sum_recv=DMA((56,)),
    near_sem=DMA((6,)),
    land_py=VMEM((3, HALF_FEED, 1024), bf16),
    total_p=VMEM((HALF_FEED, 1024), bf16),
    land_pz=VMEM((3, HALF_FEED, 256), bf16),
    land_qz=VMEM((3, 4, HALF_FEED, 256), bf16),
    total_q=VMEM((4, HALF_FEED, 256), bf16),
    land_qy=VMEM((3, HALF_FEED, 256), bf16),
    feed_both=VMEM((ROWS_FEED, 256), bf16),
    land_x=VMEM((ROWS_FEED, 128), bf16),
    block=VMEM((3, ROWS_OUT, 1024), bf16),
    land_m=VMEM((4, 3, ROWS_OUT, 256), bf16),
    shared_sums=VMEM((4, ROWS_EXTRA, 1024), bf16),
    land_s=VMEM((3, 4, ROWS_EXTRA, 256), bf16),
)


class Sums:
    def __init__(self, r):
        _, x_hi, z, core, y = place()
        self.r, self.y, self.z, self.x_hi = r, y, z, x_hi
        self.y_right, self.y_left = (y + 1) % 4, (y + 3) % 4
        self.z_right, self.z_left = (z + 1) % 4, (z + 3) % 4
        to_y = at_y(self.y_right), at_y(self.y_left)
        to_z = at_z(x_hi, self.z_right, core), at_z(x_hi, self.z_left, core)
        x_other = at_z(1 - x_hi, z, core)
        self.partners = [*to_y, *to_z, x_other]
        self.copies = copies = Copies(r.sum_send, r.sum_recv)
        cut = halves(HALF_FEED, HALF_FEED // 2)
        self.cut = cut
        self.rest = pl.ds(HALF_FEED, HALF_FEED)

        def along_y(name, block, land):
            return RingSum(name, copies, y, self.y_right, self.y_left, *to_y, block, land)

        def along_z(name, block, land):
            return RingSum(name, copies, z, self.z_right, self.z_left, *to_z, block, land)

        self.py = along_y(
            "p", lambda k, n: r.feed.at[k, cut[n]], lambda slot, n: r.land_py.at[slot, cut[n]]
        )
        self.qz = along_z(
            "q",
            lambda k, n: r.feed.at[PAIRS[n], self.rest, lanes_of(k, 256)],
            lambda slot, n: r.land_qz.at[slot, PAIRS[n]],
        )
        self.pz = along_z(
            "u",
            lambda k, n: r.total_p.at[cut[n], lanes_of(k, 256)],
            lambda slot, n: r.land_pz.at[slot, cut[n]],
        )
        self.qy = along_y(
            "v", lambda k, n: r.total_q.at[k, cut[n]], lambda slot, n: r.land_qy.at[slot, cut[n]]
        )
        copies.add("x", r.feed_both.at[:, lanes_of(1 - x_hi, 128)], r.land_x, x_other)
        self.mix_cut = halves(ROWS_OUT, ROWS_OUT // 2)
        self.mix = [
            along_z(
                "abcd"[step],
                lambda k, n, step=step: r.block.at[step % 3, self.mix_cut[n], lanes_of(k, 256)],
                lambda slot, n, step=step: r.land_m.at[step, slot, self.mix_cut[n]],
            )
            for step in range(4)
        ]
        self.shared = along_z(
            "s",
            lambda k, n: r.shared_sums.at[PAIRS[n], :, lanes_of(k, 256)],
            lambda slot, n: r.land_s.at[slot, PAIRS[n]],
        )

    def fetches(self):
        r, feed, cut = self.r, self.r.feed, self.cut
        moves = (
            (feed.at[self.y_right, cut[0]], r.total_p.at[cut[0]]),
            (feed.at[self.y_left, cut[1]], r.total_p.at[cut[1]]),
            (feed.at[self.y, pl.ds(0, HALF_FEED)], r.total_p),
            (feed.at[PAIRS[0], self.rest, lanes_of(self.z_right, 256)], r.total_q.at[PAIRS[0]]),
            (feed.at[PAIRS[1], self.rest, lanes_of(self.z_left, 256)], r.total_q.at[PAIRS[1]]),
            (feed.at[:, self.rest, lanes_of(self.z, 256)], r.total_q),
        )
        return [
            pltpu.make_async_copy(src, dst, r.near_sem.at[n]) for n, (src, dst) in enumerate(moves)
        ]

    def feed_one(self):
        self.py.start_far()
        self.qz.start_far()
        for n in (0, 1, 3, 4):
            self.fetches()[n].start()

    def feed_two(self):
        r = self.r
        for n in (0, 1, 3, 4):
            self.fetches()[n].wait()
        self.py.pass_on(r.total_p.at[self.cut[0]], r.total_p.at[self.cut[1]])
        self.qz.pass_on(r.total_q.at[PAIRS[0]], r.total_q.at[PAIRS[1]])
        self.py.start_near()
        self.qz.start_near()
        for n in (2, 5):
            self.fetches()[n].start()

    def feed_three(self):
        r = self.r
        for n in (2, 5):
            self.fetches()[n].wait()
        self.py.arrive()
        add_into(r.total_p, (r.total_p, r.land_py.at[1], r.land_py.at[2]))
        self.pz.start()
        self.qz.arrive()
        add_into(r.total_q, (r.total_q, r.land_qz.at[1], r.land_qz.at[2]))
        self.qy.start()

    def feed_four(self):
        r, cut = self.r, self.cut
        self.pz.pass_on(
            r.total_p.at[cut[0], lanes_of(self.z_right, 256)],
            r.total_p.at[cut[1], lanes_of(self.z_left, 256)],
        )
        self.qy.pass_on(r.total_q.at[self.y_right, cut[0]], r.total_q.at[self.y_left, cut[1]])

    def feed_five(self):
        r = self.r
        self.pz.arrive()
        add_into(
            r.feed_both.at[pl.ds(0, HALF_FEED)],
            (r.total_p.at[:, lanes_of(self.z, 256)], r.land_pz.at[1], r.land_pz.at[2]),
        )
        self.qy.arrive()
        add_into(
            r.feed_both.at[self.rest], (r.total_q.at[self.y], r.land_qy.at[1], r.land_qy.at[2])
        )
        self.copies.start("x")

    def feed_six(self):
        r = self.r
        self.copies.arrive("x")
        add_into(r.feed_out, (r.feed_both.at[:, lanes_of(self.x_hi, 128)], r.land_x))

    def mix_pass(self, step):
        own = self.r.block.at[step % 3]
        self.mix[step].pass_on(
            own.at[self.mix_cut[0], lanes_of(self.z_right, 256)],
            own.at[self.mix_cut[1], lanes_of(self.z_left, 256)],
        )

    def mix_end(self, step):
        r = self.r
        self.mix[step].arrive()
        own = r.block.at[step % 3, :, lanes_of(self.z, 256)]
        add_into(
            r.sums.at[step, pl.ds(0, ROWS_OUT)], (own, r.land_m.at[step, 1], r.land_m.at[step, 2])
        )
        self.mix[step].drained()

    def shared_pass(self):
        own = self.r.shared_sums
        self.shared.pass_on(
            own.at[PAIRS[0], :, lanes_of(self.z_right, 256)],
            own.at[PAIRS[1], :, lanes_of(self.z_left, 256)],
        )

    def shared_end(self):
        r = self.r
        self.shared.arrive()
        add_into(
            r.sums.at[:, pl.ds(ROWS_OUT, ROWS_EXTRA)],
            (r.shared_sums.at[:, :, lanes_of(self.z, 256)], r.land_s.at[1], r.land_s.at[2]),
        )


def reduce_body(
    feed,
    sums,
    heads_ref,
    state_conv_ref,
    gain_one_ref,
    gain_two_ref,
    home_from,
    out_ref,
    shared_ref,
    small_out,
    home_ref,
    land_y,
    both,
    land_x,
    small_y,
    small_z,
    small_x,
    small_sum,
    send,
    recv,
    *swap_scratch,
):
    _, x_hi, z, core, y = place()
    right, left, across = (y + 1) % 4, (y + 3) % 4, (y + 2) % 4
    y_right, y_left, y_across = at_y(right), at_y(left), at_y(across)
    z_others = [at_z(x_hi, (z + n) % 4, core) for n in (1, 3, 2)]
    x_other = at_z(1 - x_hi, z, core)
    partner = other_core(x_hi, z, core)
    swap = Swap(*swap_scratch)
    copies = Copies(send, recv)
    cut = halves(REST, 432)
    ring = RingSum(
        "r",
        copies,
        y,
        right,
        left,
        y_right,
        y_left,
        lambda k, n: sums.at[k, cut[n]],
        lambda slot, n: land_y.at[slot, cut[n]],
    )
    mine = out_ref.at[core, pl.ds(0, ROWS_FEED)]
    copies.add("k2", mine, mine, partner)
    for n in range(2):
        copies.add(n, both.at[cut[n], lanes_of(1 - x_hi, 128)], land_x.at[cut[n]], x_other)
        mine = out_ref.at[core, pl.ds(ROWS_FEED + 432 * n, cut[n].size)]
        copies.add("k%d" % n, mine, mine, partner)
    for n, to in enumerate((y_right, y_left, y_across)):
        copies.add("sy%d" % n, small_sum.at[0], small_y.at[n], to)
        copies.add("sh%d" % n, shared_ref.at[y], shared_ref.at[y], to)
    for n, to in enumerate(z_others):
        copies.add("sz%d" % n, small_sum.at[1], small_z.at[n], to)
    copies.add("sx", small_sum.at[2], small_x.at[0], x_other)
    copies.add("small", small_out.at[core], small_out.at[core], partner)

    swap.greet([y_right, y_left, y_across, *z_others, x_other, partner])
    ring.start()
    out_ref[core, pl.ds(0, ROWS_FEED)] = feed[...]
    copies.start("k2")
    for k in range(4):
        small_sum[0, pl.ds(16 * k, 16)] = heads_ref[k]
        small_sum[0, 68 + k : 69 + k] = gain_one_ref[:, 256 * k : 256 * k + 256]
        small_sum[0, 72 + k : 73 + k] = gain_two_ref[:, 256 * k : 256 * k + 256]
    small_sum[0, 64:68] = state_conv_ref[...]
    small_sum[0, 76:80] = jnp.zeros((4, 256), f32)
    copies.start("sy0", "sy1", "sy2")
    ring.pass_on(sums.at[right, cut[0]], sums.at[left, cut[1]])
    swap.start(rows_block(home_from), block_of(home_ref))
    copies.arrive("sy0", "sy1", "sy2")
    small_sum[1] = small_sum[0] + small_y[0] + small_y[1] + small_y[2]
    copies.start("sz0", "sz1", "sz2")
    copies.arrive("sz0", "sz1", "sz2")
    small_sum[2] = small_sum[1] + small_z[0] + small_z[1] + small_z[2]
    copies.start("sx")
    copies.arrive("sx")
    small_out[core] = small_sum[2] + small_x[0]
    copies.start("small")
    for n, letters in enumerate(("fc", "ed")):
        copies.arrive(*ring.names(letters))
        add_into(
            both.at[cut[n]], (sums.at[y, cut[n]], land_y.at[1, cut[n]], land_y.at[2, cut[n]])
        )
        copies.start(n)
    for n in range(2):
        copies.arrive(n)
        own = both.at[cut[n], lanes_of(x_hi, 128)]
        add_into(out_ref.at[core, pl.ds(ROWS_FEED + 432 * n, cut[n].size)], (own, land_x.at[cut[n]]))
        copies.start("k%d" % n)
    copies.arrive("k0", "k1", "k2")
    shared_at = pl.ds(ROWS_FEED + ROWS_OUT, ROWS_SHARED)
    shared_ref[y] = out_ref[0, shared_at] + out_ref[1, shared_at]
    copies.start("sh0", "sh1", "sh2")
    swap.wait(rows_block(home_from), block_of(home_ref))
    copies.arrive("small", "sh0", "sh1", "sh2")
    copies.leave()


def reduce_grads(feed, sums, heads, state_conv, gain_one, gain_two, home, collective):
    small = (SMALL_ROWS, 256)
    rows, width = home.shape
    return kernel_call(
        reduce_body,
        "reduce_grads",
        collective,
        [
            shape((2, ROWS_ALL, 128), f32),
            shape((4, ROWS_SHARED, 128), f32),
            shape((2,) + small, f32),
            shape((2, rows // 2, width), bf16),
        ],
        (feed, sums, heads, state_conv, gain_one, gain_two, home),
        [
            VMEM((3, REST, 256), bf16),
            VMEM((REST, 256), bf16),
            VMEM((REST, 128), bf16),
            VMEM((3,) + small, f32),
            VMEM((3,) + small, f32),
            VMEM((1,) + small, f32),
            VMEM((3,) + small, f32),
            DMA((24,)),
            DMA((24,)),
        ]
        + SWAP_SCRATCH,
    )


def whole(dims):
    return pl.BlockSpec(dims, lambda y: (0,) * len(dims), pipeline_mode=pl.Buffered(1))


def by_step(dims):
    return pl.BlockSpec((1,) + tuple(dims[1:]), lambda y: (y,) + (0,) * (len(dims) - 1))


STEP_ROWS = pl.BlockSpec((4, 16, 1024), lambda y: (0, 28, 0))
ANYWHERE = pl.BlockSpec(memory_space=ANY)


def staged(body, name, collective, inputs, outputs, scratch, steps=4):
    names = [*inputs, *outputs, *scratch]

    def kernel(*refs):
        body(types.SimpleNamespace(**dict(zip(names, refs))))

    results = pl.pallas_call(
        kernel,
        name=name,
        grid=(steps,),
        in_specs=[spec or whole(array.shape) for array, spec in inputs.values()],
        out_specs=[spec or whole(dims) for dims, _, spec in outputs.values()],
        out_shape=[shape(dims, kind) for dims, kind, _ in outputs.values()],
        scratch_shapes=list(scratch.values()),
        compiler_params=pltpu.CompilerParams(
            dimension_semantics=("arbitrary",),
            vmem_limit_bytes=60 * 2**20,
            collective_id=collective,
            has_side_effects=collective is not None,
        ),
    )(*[array for array, _ in inputs.values()])
    return types.SimpleNamespace(**dict(zip(outputs, results)))


def hail(partners):
    barrier = pltpu.get_barrier_semaphore()
    for partner in partners:
        pl.semaphore_signal(barrier, inc=1, device_id=partner, device_id_type=MESH)


def hailed(count):
    pl.semaphore_wait(pltpu.get_barrier_semaphore(), count)


PAIR_SCRATCH = dict(
    acc=VMEM((640, 1024), f32),
    part=VMEM((320, 1024), bf16),
    land=VMEM((320, 1024), bf16),
    pair_send=DMA((5,)),
    pair_recv=DMA((5,)),
)
PIECES = ((0, 160), (160, 160))


class Pair:
    def __init__(self, r):
        _, x_hi, z, core, _ = place()
        self.r, self.core = r, core
        self.partner = other_core(x_hi, z, core)
        self.copies = Copies(r.pair_send, r.pair_recv)
        for n, piece in enumerate(PIECES):
            self.copies.add("p%d" % n, r.part.at[pl.ds(*piece)], r.land.at[pl.ds(*piece)], self.partner)

    def rows(self, mine, start=0, count=320):
        side = self.core if mine else 1 - self.core
        return pl.ds(pl.multiple_of(side * 320 + start, 16), count)

    def add_gather(self, full):
        for n, piece in enumerate(PIECES):
            there = full.at[self.rows(True, *piece)]
            self.copies.add("g%d" % n, there, there, self.partner)

    def close(self, last):
        r = self.r
        theirs = self.rows(False)
        r.part[...] = (r.acc[theirs] + last(theirs)).astype(bf16)
        self.copies.start("p0", "p1")
        own = self.rows(True)
        r.acc[own] += last(own)

    def total(self, n):
        self.copies.arrive("p%d" % n)
        start, count = PIECES[n]
        return self.r.acc[self.rows(True, start, count)] + self.r.land[pl.ds(start, count)].astype(f32)


def add_step(y, acc, total):
    @pl.when(y == 0)
    def _():
        acc[...] = total()

    @pl.when(jnp.logical_and(y > 0, y < 3))
    def _():
        acc[...] += total()


def normed_rows(values, gain):
    return (values * inverse_rms(values) * gain).astype(bf16)


MIX_SCRATCH = dict(
    x_pad=VMEM((648, LANES), f32),
    z_part=VMEM((640, LANES), f32),
    step_cols=VMEM((4, 640, 16), f32),
    dt_row=VMEM((64, 640), f32),
    cum_row=VMEM((64, 640), f32),
    query=VMEM((640, 128), bf16),
    gated=VMEM((640, LANES), bf16),
    state_pad=VMEM((648, 256), f32),
    b=VMEM((640, 128), bf16),
    c=VMEM((640, 128), bf16),
    b_turn=VMEM((128, 640), bf16),
    key=VMEM((640, 128), bf16),
    value=VMEM((640, 128), bf16),
    value_turn=VMEM((128, 640), bf16),
    state=VMEM((128, LANES), f32),
)


def mixer_start(y, normed, r):
    @pl.when(y == 0)
    def _():
        shared_forward(normed, r.shared, r.state_conv, r.state_pad, r.b, r.c, r.b_turn)
        prepare_steps(normed, r.step_rows, r.small, r.step_cols, r.dt_row, r.cum_row)
        r.x_pad[0:8] = jnp.zeros((8, LANES), f32)

    @pl.when(y % 2 == 0)
    def _():
        keys_values(normed, r.shared, y // 2, r.table, r.key, r.value, r.value_turn)

    proj = mm(normed[...], mixer_rows(r.w.at[0]), NT)
    r.z_part[...] = proj[:, 0:192]
    r.x_pad[pl.ds(8, 640)] = proj[:, 256:448]
    query = turned_heads(proj[:, 128:256], proj[:, 384:512], r.table)
    r.query[...] = (query * 0.125).astype(bf16)


def scan(y, r):
    small = r.small[y]
    skip = spread_heads(small[6:7, 0:16], 1)
    causal = masks_of(CHUNK)
    kernel = small[0:4, 0:LANES]
    own_rows = pl.ds(pl.multiple_of(16 * y, 16), 16)
    r.state[...] = jnp.zeros((128, LANES), f32)
    for n in range(CHUNKS):
        at = pl.ds(n * CHUNK, CHUNK)
        pre = conv_taps(r.x_pad[pl.ds(n * CHUNK, CHUNK + 8)], kernel)
        u = pre * sigmoid(pre)
        dt = r.step_cols[y, at]
        cum = pltpu.roll(dt, 8, 1)
        dt_r = r.dt_row[own_rows, at]
        cum_r = r.cum_row[own_rows, at]
        c_chunk = r.c[at]
        inter = mm(c_chunk, r.b[at], NT)
        mixing = []
        inputs = []
        for h in range(3):
            gap = cum[:, h : h + 1] - cum_r[h : h + 1]
            decay = jnp.exp(jnp.where(causal, gap, -1e30))
            mixing.append((inter * decay * dt_r[h : h + 1]).astype(bf16))
            inputs.append(head_lanes(u, h).astype(bf16))
        inside = mm(jnp.concatenate(mixing, axis=1), jnp.concatenate(inputs, axis=0), NN)
        old = r.state[...]
        low = old.astype(bf16)
        if hasattr(r, "states"):
            r.states[0, n] = low
        before = mm(c_chunk, low, NN) * spread_heads(jnp.exp(cum), CHUNK)
        out = inside + before + skip * u
        z = r.z_part[at]
        r.gated[at] = (out * (z * sigmoid(z))).astype(bf16)
        end = cum[CHUNK - 1 : CHUNK]
        feed = spread_heads(dt * jnp.exp(end - cum), CHUNK) * u
        r.state[...] = old * spread_heads(jnp.exp(end), 1) + mm(r.b_turn[:, at], feed.astype(bf16), NN)


def middle_end(pair, hidden, r):
    for n, (start, count) in enumerate(PIECES):
        piece = pl.ds(start, count)
        middle = hidden[piece].astype(f32) + pair.total(n)
        r.middle[piece] = middle
        r.full[pair.rows(True, start, count)] = normed_rows(middle, r.gain_two[...])
        pair.copies.start("g%d" % n)
    pair.copies.arrive("g0", "g1")
    pair.copies.leave()
    r.normed_two[...] = r.full[...]


def mix_steps(y, pair, normed, hidden, r):
    mixer_start(y, normed, r)
    attend(r.query, r.key, r.value_turn, r.att)
    scan(y, r)
    w = r.w.at[0]

    def share(rows):
        return mm(r.gated[rows], w[464:656], NN) + mm(r.att[rows, 0:64], w[656:720], NN)

    add_step(y, r.acc, lambda: share(pl.ds(0, 640)))

    @pl.when(y == 3)
    def _():
        pair.close(share)
        middle_end(pair, hidden, r)


def mix_first_body(r):
    y = pl.program_id(0)
    pair = Pair(r)
    pair.add_gather(r.full)
    gather = Gather(r.feed, r.feed_all, FEED_STRAIGHT, Copies(r.send, r.recv), r.local.at[0])

    @pl.when(y == 0)
    def _():
        greet(gather.partners + [pair.partner])
        gather.one()

    for n, stage in enumerate((gather.two, gather.three, gather.four)):

        @pl.when(y == n + 1)
        def _():
            stage()

    mix_steps(y, pair, r.normed, r.hidden, r)

    @pl.when(y == 3)
    def _():
        gather.end()


def mix_second_body(r):
    y = pl.program_id(0)
    section = lax.axis_index(SECTION)
    pair = Pair(r)
    pair.add_gather(r.full)
    mine = r.normed_full.at[pair.rows(True)]
    pair.copies.add("n", mine, mine, pair.partner)

    @pl.when(y == 0)
    def _():
        hail([pair.partner])

        @pl.when(section == 0)
        def _():
            r.hidden[...] = r.own[...]

        @pl.when(section == 1)
        def _():
            r.hidden[...] = r.received[...]

        r.normed_full[pair.rows(True)] = normed_rows(r.hidden[...].astype(f32), r.gain_one[...])
        hailed(1)
        pair.copies.start("n")
        pair.copies.arrive("n")

    mix_steps(y, pair, r.normed_full, r.hidden, r)

    @pl.when(y == 3)
    def _():
        r.normed[...] = r.normed_full[...]


def mixer_inputs(w_mix, small, shared, state_conv, table):
    return dict(
        w=(w_mix, by_step(w_mix.shape)),
        step_rows=(w_mix, STEP_ROWS),
        small=(small, None),
        shared=(shared, None),
        state_conv=(state_conv, None),
        table=(table, None),
    )


MIDDLE_OUT = dict(middle=((320, 1024), f32, None), normed_two=((640, 1024), bf16, None))
FULL = dict(full=VMEM((640, 1024), bf16))


def mix_first(normed, hidden, mixer, gain_two, feed, collective):
    return staged(
        mix_first_body,
        "mix_first",
        collective,
        dict(normed=(normed, None), hidden=(hidden, None), gain_two=(gain_two, None), feed=(feed, None))
        | mixer_inputs(*mixer),
        MIDDLE_OUT | dict(feed_all=((4,) + feed.shape, bf16, ANYWHERE)),
        PAIR_SCRATCH
        | MIX_SCRATCH
        | FULL
        | dict(att=VMEM((640, 128), bf16), send=DMA((20,)), recv=DMA((20,)), local=DMA((1,))),
    )


def mix_second(own, received, mixer, gain_one, gain_two, collective):
    return staged(
        mix_second_body,
        "mix_second",
        collective,
        dict(
            own=(own, None),
            received=(received, None),
            gain_one=(gain_one, None),
            gain_two=(gain_two, None),
        )
        | mixer_inputs(*mixer),
        MIDDLE_OUT
        | dict(
            normed=((640, 1024), bf16, None),
            hidden=((320, 1024), bf16, None),
            states=((4, CHUNKS, 128, LANES), bf16, by_step((4, CHUNKS, 128, LANES))),
        ),
        PAIR_SCRATCH
        | MIX_SCRATCH
        | FULL
        | dict(att=VMEM((640, 128), bf16), normed_full=VMEM((640, 1024), bf16)),
    )


def feed_body(r, further):
    y = pl.program_id(0)
    section = lax.axis_index(SECTION)
    pair = Pair(r)
    beyond = {SECTION: 1 - section}
    if further:
        for n, piece in enumerate(PIECES):
            piece = pl.ds(*piece)
            pair.copies.add("s%d" % n, r.low.at[piece], r.beyond.at[piece], beyond)

    @pl.when(y == 0)
    def _():
        hail([pair.partner] + ([beyond] if further else []))

    w = r.w.at[0]
    both = mm(r.normed_two[...], w[0:512], NT)
    gate, up = both[:, 0:256], both[:, 256:512]
    r.active[...] = (gate * sigmoid(gate) * up).astype(bf16)

    def share(rows):
        return mm(r.active[rows], w[512:768], NN)

    add_step(y, r.acc, lambda: share(pl.ds(0, 640)))

    @pl.when(y == 3)
    def _():
        hailed(2 if further else 1)
        pair.close(share)
        for n, piece in enumerate(PIECES):
            piece = pl.ds(*piece)
            low = (r.middle[piece] + pair.total(n)).astype(bf16)
            if further:
                r.low[piece] = low
                pair.copies.start("s%d" % n)
            else:
                r.out[piece] = low
        if further:
            pair.copies.arrive("s0", "s1")
            r.out[...] = r.beyond[...]
        pair.copies.leave()


def feed_layer(normed_two, w_feed, middle, collective, further):
    more = dict(low=VMEM((320, 1024), bf16), beyond=VMEM((320, 1024), bf16)) if further else {}
    return staged(
        functools.partial(feed_body, further=further),
        "feed_first" if further else "feed_second",
        collective,
        dict(normed_two=(normed_two, None), middle=(middle, None), w=(w_feed, by_step(w_feed.shape))),
        dict(out=((320, 1024), bf16, None)),
        PAIR_SCRATCH | dict(active=VMEM((640, 256), bf16)) | more,
    ).out


def feed_back_body(r):
    y = pl.program_id(0)
    weights_too = hasattr(r, "sums")
    section = lax.axis_index(SECTION)
    pair = Pair(r)
    pair.add_gather(r.full)
    mine = r.grad_full.at[pair.rows(True)]
    pair.copies.add("n", mine, mine, pair.partner)

    @pl.when(y == 0)
    def _():
        hail([pair.partner])

        @pl.when(section == 0)
        def _():
            r.grad_full[pair.rows(True)] = r.received[...]

        @pl.when(section == 1)
        def _():
            r.grad_full[pair.rows(True)] = r.own[...]

        hailed(1)
        pair.copies.start("n")
        pair.copies.arrive("n")

    w = r.w.at[0]
    both = mm(r.normed_two[...], w[0:512], NT)
    gate, up = both[:, 0:256], both[:, 256:512]
    act_grad = mm(r.grad_full[...], w[512:768], NT)
    s = sigmoid(gate)
    silu = gate * s
    r.gate_grad[:, 0:256] = (act_grad * up * silu_slope(gate, s)).astype(bf16)
    r.gate_grad[:, 256:512] = (act_grad * silu).astype(bf16)
    if weights_too:
        out = r.sums.at[0]
        store_turned(out, pl.ds(512, 256), mm((silu * up).astype(bf16), r.grad_full[...], TN))
        store_turned(out, pl.ds(0, 512), mm(r.gate_grad[...], r.normed_two[...], TN))

    def share(rows):
        return mm(r.gate_grad[rows], w[0:512], NN)

    add_step(y, r.acc, lambda: share(pl.ds(0, 640)))

    @pl.when(y == 3)
    def _():
        pair.close(share)
        gain_sum = jnp.zeros((1, 1024), f32)
        for n, (start, count) in enumerate(PIECES):
            piece = pl.ds(start, count)
            back, gain_grad = rms_back(r.middle[piece], r.gain_two[...], pair.total(n))
            gain_sum = gain_sum + gain_grad
            rows = pair.rows(True, start, count)
            total = r.grad_full[rows].astype(f32) + back
            r.middle_grad[piece] = total
            r.full[rows] = total.astype(bf16)
            pair.copies.start("g%d" % n)
        if weights_too:
            r.gain_grad[...] = gain_sum
        pair.copies.arrive("g0", "g1")
        pair.copies.leave()
        r.branch_grad[...] = r.full[...]


def feed_back(own, received, normed_two, middle, w_feed, gain_two, collective, weights_too):
    more = {}
    if weights_too:
        more = dict(
            sums=((4, ROWS_FEED, 1024), bf16, by_step((4, ROWS_FEED, 1024))),
            gain_grad=((1, 1024), f32, None),
        )
    return staged(
        feed_back_body,
        "feed_back_sums" if weights_too else "feed_back",
        collective,
        dict(
            own=(own, None),
            received=(received, None),
            normed_two=(normed_two, None),
            middle=(middle, None),
            gain_two=(gain_two, None),
            w=(w_feed, by_step(w_feed.shape)),
        ),
        dict(middle_grad=((320, 1024), f32, None), branch_grad=((640, 1024), bf16, None)) | more,
        PAIR_SCRATCH | FULL | dict(grad_full=VMEM((640, 1024), bf16), gate_grad=VMEM((640, 512), bf16)),
    )


MIX_BACK_SCRATCH = dict(
    att_turn=VMEM((64, 640), bf16),
    c_turn=VMEM((128, 640), bf16),
    key_turn=VMEM((128, 640), bf16),
    gated_grad=VMEM((640, LANES), f32),
    att_grad=VMEM((640, 128), bf16),
    proj_grad=VMEM((640, 512), bf16),
    key_grad=VMEM((640, 128), f32),
    value_grad=VMEM((640, 128), f32),
    keyval_grad=VMEM((640, 256), bf16),
    pre_grad=VMEM((648, LANES), f32),
    line_grad=VMEM((128, 640), f32),
    step_slopes=VMEM((4, 640, 16), f32),
    end_grad=VMEM((4, 8, 16), f32),
    step_grad=VMEM((640, 64), bf16),
    inter_grad=VMEM((CHUNKS, CHUNK, CHUNK), f32),
    b_grad=VMEM((640, 128), f32),
    c_grad=VMEM((640, 128), f32),
    bc_pre_grad=VMEM((648, 256), f32),
    bc_grad=VMEM((640, 256), bf16),
)


def scan_back(y, r, weights_too):
    small = r.small[y]
    kernel = small[0:4, 0:LANES]
    skip = spread_heads(small[6:7, 0:16], 1)
    own_rows = pl.ds(pl.multiple_of(16 * y, 16), 16)
    r.state[...] = jnp.zeros((128, LANES), f32)
    skip_sum = jnp.zeros((1, LANES), f32)
    kernel_sum = [jnp.zeros((1, LANES), f32) for _ in range(4)]
    causal = masks_of(CHUNK)
    follows = iota((CHUNK, CHUNK), 0) <= iota((CHUNK, CHUNK), 1)
    for n in range(CHUNKS - 1, -1, -1):
        at = pl.ds(n * CHUNK, CHUNK)
        window = r.x_pad[pl.ds(n * CHUNK, CHUNK + 8)]
        pre = conv_taps(window, kernel)
        s = sigmoid(pre)
        u = pre * s
        dt = r.step_cols[y, at]
        cum = pltpu.roll(dt, 8, 1)
        dt_r = r.dt_row[own_rows, at]
        cum_r = r.cum_row[own_rows, at]
        b_chunk = r.b[at]
        c_chunk = r.c[at]
        inter = mm(c_chunk, b_chunk, NT)
        inter_t = mm(b_chunk, c_chunk, NT)
        end = cum[CHUNK - 1 : CHUNK]
        start_state = r.states[0, n]
        reach = spread_heads(jnp.exp(cum), CHUNK)
        before = mm(c_chunk, start_state, NN) * reach
        z = r.z_part[at]
        sz = sigmoid(z)
        silu_z = z * sz
        out_grad = r.gated_grad[at]
        y_grad = out_grad * silu_z
        u_low = u.astype(bf16)
        mixing = []
        mixing_t = []
        inputs = []
        grads = []
        dt_grad = jnp.zeros((CHUNK, 16), f32)
        cum_grad = jnp.zeros((CHUNK, 16), f32)
        lines_dt = []
        lines_cum = []
        inter_total = r.inter_grad[n]
        for h in range(3):
            gap = cum[:, h : h + 1] - cum_r[h : h + 1]
            decay = jnp.exp(jnp.where(causal, gap, -1e30))
            gap_t = cum_r[h : h + 1] - cum[:, h : h + 1]
            decay_t = jnp.exp(jnp.where(follows, gap_t, -1e30))
            weight = decay * dt_r[h : h + 1]
            mixing.append((inter * weight).astype(bf16))
            mixing_t.append((inter_t * decay_t * dt[:, h : h + 1]).astype(bf16))
            inputs.append(head_lanes(u, h).astype(bf16))
            own = head_lanes(y_grad, h).astype(bf16)
            grads.append(own)
            mix_grad = mm(own, u_low, NT)
            inter_total = inter_total + mix_grad * weight
            per = mix_grad * inter * decay
            column = column_sum(per)
            lines_dt.append(column)
            lines_cum.append(-dt_r[h : h + 1] * column)
            row_sum = jnp.sum(per * dt_r[h : h + 1], axis=1, keepdims=True)
            cum_grad = cum_grad + in_lane(row_sum, 8 + h, CHUNK)
        r.inter_grad[n] = inter_total
        inside = mm(jnp.concatenate(mixing, axis=1), jnp.concatenate(inputs, axis=0), NN)
        out = inside + before + skip * u
        r.gated[at] = (out * silu_z).astype(bf16)
        r.proj_grad[at, 0:192] = (out_grad * out * silu_slope(z, sz)).astype(bf16)
        u_grad = mm(jnp.concatenate(mixing_t, axis=1), jnp.concatenate(grads, axis=0), NN)
        u_grad = u_grad + skip * y_grad
        if weights_too:
            skip_sum = skip_sum + column_sum(y_grad * u)
        reached = (y_grad * reach).astype(bf16)
        later = r.state[...]
        later_low = later.astype(bf16)
        left = jnp.exp(end - cum)
        fed = dt * left
        fed_wide = spread_heads(fed, CHUNK)
        r.c_grad[at] += mm(reached, start_state, NT)
        r.b_grad[at] += mm((fed_wide * u).astype(bf16), later_low, NT)
        from_state = mm(b_chunk, later_low, NN)
        u_grad = u_grad + fed_wide * from_state
        before_grad = y_grad * before
        fed_grad = u * from_state
        state_share = column_sum(later * start_state.astype(f32)) * spread_heads(jnp.exp(end), 1)
        end_grad = jnp.zeros((1, 16), f32)
        for h in range(3):
            cum_grad = cum_grad + in_lane(
                jnp.sum(head_lanes(before_grad, h), axis=1, keepdims=True), 8 + h, CHUNK
            )
            fed_h = jnp.sum(head_lanes(fed_grad, h), axis=1, keepdims=True)
            dt_grad = dt_grad + in_lane(fed_h * left[:, h : h + 1], h, CHUNK)
            moved = fed_h * fed[:, h : h + 1]
            cum_grad = cum_grad - in_lane(moved, 8 + h, CHUNK)
            share = jnp.sum(head_lanes(state_share, h), axis=1, keepdims=True)
            end_grad = end_grad + in_lane(column_sum(moved) + share, h, 1)
        r.state[...] = later * spread_heads(jnp.exp(end), 1) + mm(r.c_turn[:, at], reached, NN)
        rest = jnp.zeros((5, CHUNK), f32)
        first = pl.ds(pl.multiple_of(16 * y, 16), 8)
        second = pl.ds(pl.multiple_of(64 + 16 * y, 16), 8)
        r.line_grad[first, at] = jnp.concatenate(lines_dt + [rest], axis=0)
        r.line_grad[second, at] = jnp.concatenate(lines_cum + [rest], axis=0)
        r.step_slopes[y, at] = dt_grad + cum_grad
        r.end_grad[y, n : n + 1] = end_grad
        own_pre = u_grad * silu_slope(pre, s)
        r.pre_grad[at] = own_pre
        after = r.pre_grad[pl.ds(n * CHUNK, CHUNK + 8)]
        r.proj_grad[at, 256:448] = conv_back(after, kernel).astype(bf16)
        if weights_too:
            for k in range(4):
                kernel_sum[k] = kernel_sum[k] + column_sum(own_pre * window[5 + k : 5 + k + CHUNK])
    if weights_too:
        skip_row = jnp.zeros((1, 16), f32)
        for h in range(3):
            skip_row = skip_row + in_lane(
                jnp.sum(head_lanes(skip_sum, h), axis=1, keepdims=True), h, 1
            )
        grads = r.small_grad.at[y]
        grads[...] = jnp.zeros((16, 256), f32)
        for k in range(4):
            grads[k : k + 1, 0:LANES] = kernel_sum[k]
        grads[6:7, 0:16] = skip_row


def steps_back(r, weights_too):
    def wide(ref, at):
        return jnp.concatenate([ref[k, at] for k in range(4)], axis=1)

    rate = jnp.exp(jnp.concatenate([r.small[k, 5:6, 0:16] for k in range(4)], axis=1))
    follows = (iota((CHUNK, CHUNK), 0) <= iota((CHUNK, CHUNK), 1)).astype(f32)
    bias_sum = jnp.zeros((1, 64), f32)
    decay_sum = jnp.zeros((1, 64), f32)
    for n in range(CHUNKS):
        at = pl.ds(n * CHUNK, CHUNK)
        turned = r.line_grad[:, at].T
        dt = wide(r.step_cols, at)
        slopes = [r.step_slopes[k, at] for k in range(4)]
        low = iota((CHUNK, 16), 1) < 8
        dt_own = [jnp.where(low, own, 0.0) for own in slopes]
        cum_own = [jnp.where(low, pltpu.roll(own, 8, 1), 0.0) for own in slopes]
        cum_grad = jnp.concatenate(cum_own, axis=1) + turned[:, 64:128]
        a_grad = mm(follows, cum_grad, NN, HIGH) + wide(r.end_grad, pl.ds(n, 1))
        dt_grad = jnp.concatenate(dt_own, axis=1) + turned[:, 0:64] - rate * a_grad
        raw_grad = dt_grad * softplus_slope(dt)
        r.step_grad[at] = raw_grad.astype(bf16)
        bias_sum = bias_sum + column_sum(raw_grad)
        decay_sum = decay_sum - column_sum(a_grad * dt) * rate
    if weights_too:
        for k in range(4):
            r.small_grad[k, 4:5, 0:16] = bias_sum[:, 16 * k : 16 * k + 16]
            r.small_grad[k, 5:6, 0:16] = decay_sum[:, 16 * k : 16 * k + 16]


def shared_back(r, weights_too):
    sums = [jnp.zeros((1, 256), f32) for _ in range(4)]
    kernel = r.state_conv[...]
    for n in range(CHUNKS - 1, -1, -1):
        at = pl.ds(n * CHUNK, CHUNK)
        inter_low = r.inter_grad[n].astype(bf16)
        grad_b = r.b_grad[at] + mm(inter_low, r.c[at], TN)
        grad_c = r.c_grad[at] + mm(inter_low, r.b[at], NN)
        window = r.state_pad[pl.ds(n * CHUNK, CHUNK + 8)]
        pre = conv_taps(window, kernel)
        own_pre = jnp.concatenate([grad_b, grad_c], axis=1) * silu_slope(pre, sigmoid(pre))
        r.bc_pre_grad[at] = own_pre
        after = r.bc_pre_grad[pl.ds(n * CHUNK, CHUNK + 8)]
        r.bc_grad[at] = conv_back(after, kernel).astype(bf16)
        if weights_too:
            for k in range(4):
                sums[k] = sums[k] + column_sum(own_pre * window[5 + k : 5 + k + CHUNK])
    if weights_too:
        for k in range(4):
            r.state_conv_grad[k : k + 1] = sums[k]


def mix_back_body(r):
    y = pl.program_id(0)
    weights_too = hasattr(r, "sums")
    section = lax.axis_index(SECTION)
    pair = Pair(r)
    beyond = {SECTION: 1 - section}
    if weights_too:
        sums = Sums(r)

        @pl.when(y == 0)
        def _():
            greet(sums.partners + [pair.partner])
            sums.feed_one()

        @pl.when(y == 1)
        def _():
            sums.feed_two()
            sums.mix[0].start()

        @pl.when(y == 2)
        def _():
            sums.feed_three()
            sums.mix_pass(0)
            sums.mix[1].start()

        @pl.when(y == 3)
        def _():
            sums.feed_four()
            sums.mix_end(0)
            sums.mix_pass(1)
            sums.mix[2].start()

    else:
        swap = Swap(r.swap_send, r.swap_recv, r.swap_local)
        for n, piece in enumerate(PIECES):
            piece = pl.ds(*piece)
            pair.copies.add("s%d" % n, r.low.at[piece], r.beyond.at[piece], beyond)

        @pl.when(y == 0)
        def _():
            swap.greet([pair.partner, beyond])
            swap.start(rows_block(r.result), block_of(r.home_land))

    mixer_start(y, r.normed, r)

    @pl.when(y == 0)
    def _():
        turn_into(r.c_turn, r.c[...])
        r.pre_grad[pl.ds(640, 8)] = jnp.zeros((8, LANES), f32)
        r.bc_pre_grad[pl.ds(640, 8)] = jnp.zeros((8, 256), f32)
        r.inter_grad[...] = jnp.zeros((CHUNKS, CHUNK, CHUNK), f32)
        r.b_grad[...] = jnp.zeros((640, 128), f32)
        r.c_grad[...] = jnp.zeros((640, 128), f32)
        r.line_grad[...] = jnp.zeros((128, 640), f32)

    @pl.when(y % 2 == 0)
    def _():
        turn_into(r.key_turn, r.key[...])
        r.key_grad[...] = jnp.zeros((640, 128), f32)
        r.value_grad[...] = jnp.zeros((640, 128), f32)

    w = r.w.at[0]
    nothing = jnp.zeros((64, 1024), bf16)
    branch_rows = jnp.concatenate([w[464:656], nothing, w[656:720], nothing], axis=0)
    branch = mm(r.branch_grad[...], branch_rows, NT)
    r.gated_grad[...] = branch[:, 0:192]
    r.att_grad[...] = branch[:, 256:384].astype(bf16)
    attend_back(
        r.query,
        r.key,
        r.key_turn,
        r.value,
        r.value_turn,
        r.att_grad,
        r.att_turn,
        r.proj_grad,
        r.key_grad,
        r.value_grad,
        r.table,
    )
    scan_back(y, r, weights_too)

    def share(at):
        return mm(r.proj_grad[at], mixer_rows(r.w.at[0]), NN)

    add_step(y, r.acc, lambda: share(pl.ds(0, 640)))
    for head in range(2):

        @pl.when(y == 2 * head + 1)
        def _():
            own = r.key_grad[...]
            first = jnp.where(
                iota((640, 128), 1) < 64, r.value_grad[...], own * r.table[:, 0:128]
            )
            second = own * r.table[:, 128:256]
            r.keyval_grad[...] = jnp.concatenate([first, second], axis=1).astype(bf16)

    def keyval_rows(head):
        key_rows = r.shared[pl.ds(256 + 64 * head, 64)]
        value_rows = r.shared[pl.ds(384 + 64 * head, 64)]
        return jnp.concatenate([value_rows, key_rows, value_rows, exchanged(key_rows)], axis=0)

    @pl.when(y == 1)
    def _():
        r.acc[...] += mm(r.keyval_grad[...], keyval_rows(0), NN)

    @pl.when(y == 3)
    def _():
        shared_back(r, weights_too)
        steps_back(r, weights_too)

    if weights_too:
        out = r.block.at[y % 3]
        normed = r.normed[...]
        grad = r.branch_grad[...]
        own = mm(r.proj_grad[...], normed, TN)
        store_turned(out, pl.ds(0, 192), own[0:192])
        store_turned(out, pl.ds(192, 192), own[256:448])
        store_turned(out, pl.ds(384, 64), own[192:256] + exchanged(own[448:512]))
        store_turned(out, pl.ds(448, 192), mm(r.gated[...], grad, TN))
        store_turned(out, pl.ds(640, 64), mm(r.att_turn[...], grad, NN))
        for head in range(2):

            @pl.when(y == 2 * head + 1)
            def _():
                own = mm(r.keyval_grad[...], normed, TN)
                at = pl.ds(64 * head, 64)
                store_turned(r.shared_sums.at[2], at, own[64:128] + exchanged(own[192:256]))
                store_turned(r.shared_sums.at[3], at, own[0:64])

        @pl.when(y == 3)
        def _():
            both = mm(r.bc_grad[...], normed, TN)
            store_turned(r.shared_sums.at[0], pl.ds(0, 128), both[0:128])
            store_turned(r.shared_sums.at[1], pl.ds(0, 128), both[128:256])
            steps = mm(r.step_grad[...], normed, TN)
            for k in range(4):
                store_turned(r.shared_sums.at[k], pl.ds(128, 16), steps[16 * k : 16 * k + 16])
            sums.mix[3].start()
            sums.shared.start()

    @pl.when(y == 3)
    def _():
        step_weights = jnp.concatenate([r.step_rows[k] for k in range(4)], axis=0)

        def last(at):
            return (
                share(at)
                + mm(r.keyval_grad[at], keyval_rows(1), NN)
                + mm(r.bc_grad[at], r.shared[0:256], NN)
                + mm(r.step_grad[at], step_weights, NN)
            )

        pair.close(last)
        if weights_too:
            sums.feed_five()
            sums.mix_end(1)
            sums.mix_pass(2)
            sums.mix_pass(3)
            sums.shared_pass()
        gain_sum = jnp.zeros((1, 1024), f32)
        for n, (start, count) in enumerate(PIECES):
            piece = pl.ds(start, count)
            hidden = r.hidden[piece].astype(f32)
            back, gain_grad = rms_back(hidden, r.gain_one[...], pair.total(n))
            low = (r.middle_grad[piece] + back).astype(bf16)
            gain_sum = gain_sum + gain_grad
            if weights_too:
                r.grad_in[piece] = low
            else:
                r.low[piece] = low
                pair.copies.start("s%d" % n)
        if weights_too:
            r.gain_grad[...] = gain_sum
            sums.feed_six()
            sums.mix_end(2)
            sums.mix_end(3)
            sums.shared_end()
            sums.copies.leave()
        else:
            swap.wait(rows_block(r.result), block_of(r.home_land))
            r.home[...] = r.home_land[...]
            pair.copies.arrive("s0", "s1")
            r.received[...] = r.beyond[...]
        pair.copies.leave()


def mix_back(forward, branch_grad, middle_grad, mixer, gain_one, collective, result=None, feed=None):
    inputs = dict(
        normed=(forward.normed, None),
        hidden=(forward.hidden, None),
        states=(forward.states, by_step(forward.states.shape)),
        branch_grad=(branch_grad, None),
        middle_grad=(middle_grad, None),
        gain_one=(gain_one, None),
    ) | mixer_inputs(*mixer)
    scratch = PAIR_SCRATCH | MIX_SCRATCH | MIX_BACK_SCRATCH
    if feed is None:
        inputs |= dict(result=(result, None))
        outputs = dict(received=((320, 1024), bf16, None), home=((2, 160, 1024), bf16, None))
        scratch = scratch | dict(
            low=VMEM((320, 1024), bf16),
            beyond=VMEM((320, 1024), bf16),
            home_land=VMEM((2, 160, 1024), bf16),
            swap_send=DMA((2,)),
            swap_recv=DMA((2,)),
            swap_local=DMA((1,)),
        )
    else:
        inputs |= dict(feed=(feed, ANYWHERE))
        outputs = dict(
            grad_in=((320, 1024), bf16, None),
            gain_grad=((1, 1024), f32, None),
            sums=((4, ROWS_OUT + ROWS_EXTRA, 256), bf16, None),
            small_grad=((4, 16, 256), f32, None),
            state_conv_grad=((4, 256), f32, None),
            feed_out=((ROWS_FEED, 128), f32, None),
        )
        scratch = scratch | FEED_SUM
    return staged(
        mix_back_body,
        "mix_back" if feed is None else "mix_back_sums",
        collective,
        inputs,
        outputs,
        scratch,
    )


def pick(rows, columns, start):
    return (iota((rows, columns), 1) == iota((rows, columns), 0) + start).astype(bf16)


def write_turn_table(table_ref):
    lane = iota((640, 128), 1)
    pair = (lane % 32).astype(f32)
    frequency = jnp.exp(pair * (-2.0 / 64.0 * math.log(rope_base)))
    angle = iota((640, 128), 0).astype(f32) * frequency
    kept = lane >= 64
    sine = jnp.sin(angle)
    table_ref[:, 0:128] = jnp.where(kept, jnp.cos(angle), 0.0)
    table_ref[:, 128:256] = jnp.where(kept, jnp.where(lane < 96, -sine, sine), 0.0)


def start_body(r):
    section, x_hi, z, core, y = place()
    gather = Gather(r.mix, r.mix_all, MIX_STRAIGHT, Copies(r.send, r.recv), r.local.at[0])
    swap = Swap(r.swap_send, r.swap_recv, r.swap_local)
    small = Copies(r.small_send, r.small_recv)
    for n, k in enumerate((gather.right, gather.left, gather.across)):
        small.add(n, r.small, r.small_land.at[y], at_y(k))
    partner = other_core(x_hi, z, core)
    mine = r.normed_full.at[my_rows(core, 320)]
    small.add(3, mine, mine, partner)

    def turned(values, rows, start):
        return mm(pick(rows, values.shape[1], start), values, NT).astype(bf16)

    swap.greet(gather.partners + [at_y(gather.across), partner])
    swap.start(block_of(r.stream), rows_block(r.own_land), section == 0)
    swap.start(block_of(r.cotangent), rows_block(r.own_land), section == 1)
    r.mix[464:656] = r.mamba_out[pl.ds(pl.multiple_of(core * 192, 192), 192)]
    r.mix[656:720] = r.att_out[pl.ds(pl.multiple_of(core * 64, 64), 64)]
    r.mix[0:192] = turned(r.mamba[:, 0:384], 192, core * 192)
    r.mix[192:384] = turned(r.mamba[:, 384:768], 192, core * 192)
    r.mix[384:448] = turned(r.query[...], 64, core * 64)
    wanted = jnp.logical_and(
        iota((16, 128), 1) == iota((16, 128), 0) + core * 3, iota((16, 128), 0) < 3
    )
    r.mix[448:464] = mm(wanted.astype(bf16), r.step[...], NT).astype(bf16)
    gather.one()
    small.start(0, 1, 2)
    r.small_land[y] = r.small[...]
    r.shared[0:256] = turned(r.state[...], 256, 0)
    r.shared[256:512] = turned(r.keyval[...], 256, 0)
    gather.two()
    swap.wait(block_of(r.stream), rows_block(r.own_land))
    r.own[...] = r.own_land[...]
    r.normed_full[my_rows(core, 320)] = normed_rows(r.own[...].astype(f32), r.gain_one[...])
    small.start(3)
    r.feed[0:256] = turned(r.gate_up[:, 0:512], 256, core * 256)
    r.feed[256:512] = turned(r.gate_up[:, 512:1024], 256, core * 256)
    r.feed[512:768] = r.down[pl.ds(pl.multiple_of(core * 256, 256), 256)]
    gather.three()
    write_turn_table(r.table)
    gather.four()
    small.arrive(0, 1, 2, 3)
    small.leave()
    r.small_all[...] = r.small_land[...]
    r.normed[...] = r.normed_full[...]
    gather.end()


def start(inputs, collective):
    rows = 320
    return staged(
        start_body,
        "start",
        collective,
        {name: (array, None) for name, array in inputs.items()},
        dict(
            mix_all=((4, ROWS_MIX, 1024), bf16, ANYWHERE),
            feed=((ROWS_FEED, 1024), bf16, None),
            shared=((512, 1024), bf16, None),
            small_all=((4, 16, 256), f32, None),
            own=((rows, 1024), bf16, None),
            normed=((2 * rows, 1024), bf16, None),
            table=((640, 256), f32, None),
        ),
        dict(
            mix=VMEM((ROWS_MIX, 1024), bf16),
            small_land=VMEM((4, 16, 256), f32),
            own_land=VMEM((rows, 1024), bf16),
            normed_full=VMEM((2 * rows, 1024), bf16),
            send=DMA((20,)),
            recv=DMA((20,)),
            local=DMA((1,)),
            small_send=DMA((4,)),
            small_recv=DMA((4,)),
            swap_send=DMA((2,)),
            swap_recv=DMA((2,)),
            swap_local=DMA((1,)),
        ),
        steps=1,
    )


def chosen(rows, start, width=128):
    return (iota((rows, width), 1) == iota((rows, width), 0) + start).astype(f32)


def finish_body(r):
    _, x_hi, z, core, y = place()
    own = chosen(64, core * 64)
    f = ROWS_FEED

    def across(side, start, stop):
        return mm(own, r.sums[side, start:stop], NT, HIGH)

    def along(side, start, stop):
        return mm(r.sums[side, start:stop], own, NT, HIGH)

    for c in range(2):
        for n in range(2):
            r.mamba_in[:, n, 192 * c : 192 * c + 192] = across(c, f + 192 * n, f + 192 * n + 192)
            r.gate_up[:, n, 256 * c : 256 * c + 256] = across(c, 256 * n, 256 * n + 256)
        r.query_in[:, 64 * c : 64 * c + 64] = across(c, f + 384, f + 448)
        r.step_in[:, 3 * c : 3 * c + 3] = across(c, f + 832, f + 848)[:, 0:3]
        r.mamba_out[192 * c : 192 * c + 192] = along(c, f + 448, f + 640)
        r.attention_out[64 * c : 64 * c + 64] = along(c, f + 640, f + 704)
        r.down_weight[256 * c : 256 * c + 256] = along(c, 512, 768)
        heads = r.small[c, pl.ds(pl.multiple_of(16 * y, 16), 16)]
        r.mamba_conv[:, 192 * c : 192 * c + 192] = heads[0:4, 0:192]
        r.step_bias[:, 3 * c : 3 * c + 3] = heads[4:5, 0:3]
        r.decay_log[:, 3 * c : 3 * c + 3] = heads[5:6, 0:3]
        r.skip_gain[:, 3 * c : 3 * c + 3] = heads[6:7, 0:3]
    few = chosen(16, core * 64 + y * 16)
    shared = [mm(few, r.shared_sums[k], NT, HIGH) for k in range(4)]
    for k in range(2):
        r.state_in[:, 128 * k : 128 * k + 128] = shared[k]
        r.keyval_in[:, k] = shared[2 + k]
    tiny = (x_hi * 8 + z * 2 + core) * 4 + y
    kernel = r.small[0, 64:68] + r.small[1, 64:68]
    r.state_conv[...] = mm(kernel, chosen(4, tiny * 4, 256), NT, HIGH)
    lanes = chosen(16, tiny % 16 * 16, 256)
    for out, start in ((r.mixer_gain, 68), (r.feed_gain, 72)):
        both = r.small[0, start : start + 4] + r.small[1, start : start + 4]
        row = jnp.sum(jnp.where(iota((4, 256), 0) == tiny // 16, both, 0.0), axis=0, keepdims=True)
        out[...] = mm(row, lanes, NT, HIGH)
    r.section_output[...] = r.result[...].astype(f32)
    r.input_grad[...] = r.grad[...].astype(f32)


def finish(sums, shared_sums, small, result, grad):
    inputs = dict(sums=sums, shared_sums=shared_sums, small=small, result=result, grad=grad)
    outputs = dict(
        section_output=(2, 160, 1024),
        input_grad=(2, 160, 1024),
        mixer_gain=(1, 16),
        mamba_in=(64, 2, 384),
        state_in=(16, 256),
        step_in=(64, 6),
        mamba_conv=(4, 384),
        state_conv=(4, 4),
        step_bias=(1, 6),
        decay_log=(1, 6),
        skip_gain=(1, 6),
        query_in=(64, 128),
        keyval_in=(16, 2, 128),
        mamba_out=(384, 64),
        attention_out=(128, 64),
        feed_gain=(1, 16),
        gate_up=(64, 2, 512),
        down_weight=(512, 64),
    )
    return staged(
        finish_body,
        "finish",
        None,
        {name: (array, None) for name, array in inputs.items()},
        {name: (dims, f32, None) for name, dims in outputs.items()},
        {},
        steps=1,
    )


def per_device(
    stream_in,
    cotangent,
    mixer_gain,
    mamba_in,
    state_in,
    step_in,
    mamba_conv,
    state_conv,
    step_bias,
    decay_log,
    skip_gain,
    query_in,
    keyval_in,
    mamba_out,
    attention_out,
    feed_gain,
    gate_up,
    down_weight,
):
    core = lax.axis_index(DP) % 2
    gain_one = mixer_gain.astype(f32)
    gain_two = feed_gain.astype(f32)

    def mine(values, axis):
        size = values.shape[axis] // 2
        return lax.dynamic_slice_in_dim(values, core * size, size, axis)

    conv_mine = jnp.pad(mine(mamba_conv[0].astype(f32), 1), ((0, 0), (0, 64)))
    heads_mine = jnp.stack([mine(step_bias[0], 0), mine(decay_log[0], 0), mine(skip_gain[0], 0)])
    small_mine = jnp.concatenate(
        [
            conv_mine,
            jnp.pad(heads_mine, ((0, 1), (0, 253))),
            jnp.pad(heads_mine.T, ((0, 5), (0, 253))),
        ]
    )
    begun = start(
        dict(
            mamba=mamba_in[0].reshape(1024, 768),
            query=query_in[0],
            step=jnp.pad(step_in[0], ((0, 0), (0, 122))),
            mamba_out=mamba_out[0],
            att_out=attention_out[0],
            gate_up=gate_up[0].reshape(1024, 1024),
            down=down_weight[0],
            state=state_in[0],
            keyval=keyval_in[0].reshape(1024, 256),
            small=small_mine,
            stream=stream_in,
            cotangent=cotangent,
            gain_one=gain_one,
        ),
        1,
    )
    own = begun.own
    mixer = (begun.mix_all, begun.small_all, begun.shared, state_conv[0].astype(f32), begun.table)

    first = mix_first(begun.normed, own, mixer, gain_two, begun.feed, 4)
    w_feed = first.feed_all
    received = feed_layer(first.normed_two, w_feed, first.middle, 5, True)
    forward = mix_second(own, received, mixer, gain_one, gain_two, 6)
    result = feed_layer(forward.normed_two, w_feed, forward.middle, 7, False)
    back = feed_back(own, own, forward.normed_two, forward.middle, w_feed, gain_two, 8, False)
    moved = mix_back(forward, back.branch_grad, back.middle_grad, mixer, gain_one, 9, result=result)
    back = feed_back(own, moved.received, forward.normed_two, forward.middle, w_feed, gain_two, 10, True)
    ends = mix_back(forward, back.branch_grad, back.middle_grad, mixer, gain_one, 11, feed=back.sums)
    reduced, shared_sum, small_sum, input_grad = reduce_grads(
        ends.feed_out,
        ends.sums,
        ends.small_grad,
        ends.state_conv_grad,
        ends.gain_grad,
        back.gain_grad,
        ends.grad_in,
        12,
    )
    done = finish(reduced, shared_sum, small_sum, moved.home, input_grad)
    return tuple(value.reshape(1, *value.shape[value.shape[0] == 1 :]) for value in vars(done).values())


def solution(mesh):
    in_specs = (
        P(DP, TENSOR, None),
        P(DP, TENSOR, None),
        P(SECTION, None),
        P(SECTION, None, None, TENSOR),
        P(SECTION, None, None),
        P(SECTION, None, TENSOR),
        P(SECTION, None, TENSOR),
        P(SECTION, None, None),
        P(SECTION, TENSOR),
        P(SECTION, TENSOR),
        P(SECTION, TENSOR),
        P(SECTION, None, TENSOR),
        P(SECTION, None, None, None),
        P(SECTION, TENSOR, None),
        P(SECTION, TENSOR, None),
        P(SECTION, None),
        P(SECTION, None, None, TENSOR),
        P(SECTION, TENSOR, None),
    )
    out_specs = (
        P(SECTION, DP, TENSOR, None),
        P(SECTION, DP, TENSOR, None),
        P(SECTION, (DP, TENSOR)),
        P(SECTION, DP, None, TENSOR),
        P(SECTION, (DP, TENSOR), None),
        P(SECTION, DP, TENSOR),
        P(SECTION, None, TENSOR),
        P(SECTION, None, (DP, TENSOR)),
        P(SECTION, TENSOR),
        P(SECTION, TENSOR),
        P(SECTION, TENSOR),
        P(SECTION, DP, TENSOR),
        P(SECTION, (DP, TENSOR), None, None),
        P(SECTION, TENSOR, DP),
        P(SECTION, TENSOR, DP),
        P(SECTION, (DP, TENSOR)),
        P(SECTION, DP, None, TENSOR),
        P(SECTION, TENSOR, DP),
    )
    return jax.shard_map(
        per_device, mesh=mesh, in_specs=in_specs, out_specs=out_specs, check_vma=False
    )
```

time: 3260 us -> 461 us (0.14)
  waiting for transfers between devices: 2230 us -> 0 us
  Pallas kernels: 0 us -> 433 us
  matrix products: 405 us -> 0 us
  blocking collectives: 199 us -> 0 us
  local copies, waits for them, and re-layouts: 201 us -> 15.8 us
  other arithmetic: 189 us -> 5.37 us
    unnamed x41 -> x0, waiting for transfers between devices: 1060 us -> none
    reduce_scatter x15 -> x0, waiting for transfers between devices: 842 us -> none  [the longest x12 374 us: reduce_rows(): return lax.psum_scatter(running, 'tensor', scatter_dimension=0, tiled=True)]
    pallas_call x0 -> x11, Pallas kernels: none -> 433 us  [the longest x10 390 us: staged(): pl.pallas_call(kernel, name=name, grid=(steps,), in_specs=[spec or whole(...]
    dot_general x111 -> x0, matrix products: 405 us -> none  [the longest x9 134 us: state_mix(): jnp.einsum('tsh,shp->thp', mixing, inputs, precision=lax.Precision.HIGHEST)]
    all_gather x12 -> x0, waiting for transfers between devices: 261 us -> none  [spread(): return lax.all_gather(shard, 'tensor', axis=0, tiled=True)]
    unnamed x1 -> x0, blocking collectives: 165 us -> none
    unnamed x686 -> x18, local copies, waits for them, and re-layouts: 79.7 us -> 14.3 us
    ppermute x4 -> x0, waiting for transfers between devices: 61.9 us -> none  [passed_along(): return lax.ppermute(shard, axis, pairs)]
  transfers between devices with their start and end apart: 38 -> 0, of which waited for: 36 -> 0; matrix products, arithmetic and copies ran while one was open for 6% -> 0% of each run, Pallas kernels for 0% -> 0%
where the time goes in v2:
time: 461 us; the launch traced here: 455 us
  Pallas kernels  433 us (94%)
  local copies, waits for them, and re-layouts  15.8 us (3%)
  other arithmetic  5.37 us (1%)
    pallas_call x10, Pallas kernels, staged(): pl.pallas_call(kernel, name=name, grid=(steps,), in_specs=[spec or whole(...  390 us
    pallas_call x1, Pallas kernels, kernel_call(): pl.pallas_call(body, name=name, out_shape=out_shape, in_specs=[pl.BlockSp...  43.2 us
    unnamed x18, local copies, waits for them, and re-layouts  14.3 us

profile of v2, /device:TPU:0, one launch (start us, length us, event | category | flops | bytes accessed | tf_op | source)
XLA Modules:
  0.0 455.1 jit_solution(7240853512560012281)
XLA Ops:
  0.7 0.0 copy-start
  0.7 0.0 copy-start.2
  0.7 0.6 copy-done
  1.3 0.1 constant_dynamic-slice_fusion.2
  1.4 0.7 constant_dynamic-slice_fusion
  2.1 0.1 copy.47
  2.2 0.1 copy.45
  2.3 0.1 copy.46
  2.4 0.1 fusion.1
  2.5 0.1 pad_maximum_fusion
  2.6 0.1 copy.48
  2.7 0.8 convert_bitcast_fusion
  3.4 1.3 convert_element_type.24.refs_12_.refs_2_.refs_5_
  4.7 1.3 bitcast_convert_fusion.refs_8_.refs_10_
  6.0 1.3 convert_element_type.25.refs_2_.refs_3_.refs_4_
  7.3 0.6 select_maximum_fusion.refs_9_
  7.9 0.9 copy.36
  8.8 0.8 pad.16.refs_2_
  9.6 1.9 copy.53
  11.5 0.0 copy-done.2
  11.5 0.0 copy-start.1
  11.5 1.5 copy.49
  13.0 0.7 copy-done.1
  13.7 1.9 copy.50
  15.6 51.4 %start.1 = (bf16[4,720,1024]{2,1,0:T(8,128)(2,1)}, bf16[768,1024]{1,0:T(8,128)(2,1)}, bf16[512,1024]{1,0:T(8,128)(2,1)}, f32[4,16,256]{2,1,0:T(8,128)}, bf16[320...) custom-call(bf16[1024,768]{1,0:T(8,128)(2,1)} %bitcast.38, bf16[1024,128]{1,0:T(8,128)(2,1)} %bitcast.47, ...), custom_call_target="tpu_custom_call" | custom-call | tf_op jit(solution)/shard_map/start/pallas_call | solution.py:890
  67.0 42.8 %mix_first.1 = (f32[320,1024]{1,0:T(8,128)}, bf16[640,1024]{1,0:T(8,128)(2,1)}, bf16[4,768,1024]{2,1,0:T(8,128)(2,1)}) custom-call(bf16[640,1024]{1,0:T(8,128)(2,1)} %get-tuple-element.70.refs_0_, bf16[320,1024]{1,0:T(8,128)(2,1)} %get-tuple-element.69.refs_1_.refs_0_, f32[1,1024]{1,0:T(1,128)} %convert_element_type.25.refs_2_.refs_3_.refs_4_, ...), custom_call_target="tpu_custom_call" | custom-call | tf_op jit(solution)/shard_map/mix_first/pallas_call | solution.py:890
  109.8 26.9 %feed_first.1.refs_1_ = bf16[320,1024]{1,0:T(8,128)(2,1)} custom-call(bf16[640,1024]{1,0:T(8,128)(2,1)} %get-tuple-element.76.refs_0_, f32[320,1024]{1,0:T(8,128)} %get-tuple-element.77.refs_1_, bf16[4,768,1024]{2,1,0:T(8,128)(2,1)} %get-tuple-element.78.refs_2_.refs_5_), custom_call_target="tpu_custom_call" | custom-call | tf_op jit(solution)/shard_map/feed_first/pallas_call | solution.py:890
  136.8 29.1 %mix_second.1 = (f32[320,1024]{1,0:T(8,128)}, bf16[640,1024]{1,0:T(8,128)(2,1)}, bf16[640,1024]{1,0:T(8,128)(2,1)}, bf16[320,1024]{1,0:T(8,128)(2,1)}, bf16[4,5,128,192]{3,2,1,0:T(8,128)(2,1)}) custom-call(bf16[320,1024]{1,0:T(8,128)(2,1)} %get-tuple-element.69.refs_1_.refs_0_, bf16[320,1024]{1,0:T(8,128)(2,1)} %feed_first.1.refs_1_, ...), custom_call_target="tpu_custom_call" | custom-call | tf_op jit(solution)/shard_map/mix_second/pallas_call | solution.py:890
  165.9 10.7 %feed_second.1.refs_12_ = bf16[320,1024]{1,0:T(8,128)(2,1)} custom-call(bf16[640,1024]{1,0:T(8,128)(2,1)} %get-tuple-element.82.refs_2_.refs_0_, f32[320,1024]{1,0:T(8,128)} %get-tuple-element.83.refs_3_.refs_1_, bf16[4,768,1024]{2,1,0:T(8,128)(2,1)} %get-tuple-element.78.refs_2_.refs_5_), custom_call_target="tpu_custom_call" | custom-call | tf_op jit(solution)/shard_map/feed_second/pallas_call | solution.py:890
  176.6 18.6 %feed_back.1 = (f32[320,1024]{1,0:T(8,128)}, bf16[640,1024]{1,0:T(8,128)(2,1)}) custom-call(bf16[320,1024]{1,0:T(8,128)(2,1)} %get-tuple-element.69.refs_1_.refs_0_, bf16[320,1024]{1,0:T(8,128)(2,1)} %get-tuple-element.69.refs_1_.refs_0_, bf16[640,1024]{1,0:T(8,128)(2,1)} %get-tuple-element.82.refs_2_.refs_0_, ...), custom_call_target="tpu_custom_call" | custom-call | tf_op jit(solution)/shard_map/feed_back/pallas_call | solution.py:890
  195.2 70.9 %mix_back.1 = (bf16[320,1024]{1,0:T(8,128)(2,1)}, bf16[2,160,1024]{2,1,0:T(8,128)(2,1)}) custom-call(bf16[640,1024]{1,0:T(8,128)(2,1)} %get-tuple-element.79.refs_0_, bf16[320,1024]{1,0:T(8,128)(2,1)} %get-tuple-element.80.refs_1_, bf16[4,5,128,192]{3,2,1,0:T(8,128)(2,1)} %get-tuple-element.81.refs_2_, bf16[640,1024]{1,0:T(8,128)(2,1)} %get-tuple-element.84.refs_3_, ...), custom_call_target="tpu_custom_call" | custom-call | tf_op jit(solution)/shard_map/mix_back/pallas_call | solution.py:890
  266.2 24.9 %feed_back_sums.1 = (f32[320,1024]{1,0:T(8,128)}, bf16[640,1024]{1,0:T(8,128)(2,1)}, bf16[4,768,1024]{2,1,0:T(8,128)(2,1)}, f32[1,1024]{1,0:T(1,128)}) custom-call(bf16[320,1024]{1,0:T(8,128)(2,1)} %get-tuple-element.69.refs_1_.refs_0_, bf16[320,1024]{1,0:T(8,128)(2,1)} %get-tuple-element.86.refs_1_, bf16[640,1024]{1,0:T(8,128)(2,1)} %get-tuple-element.82.refs_2_.refs_0_, ...), custom_call_target="tpu_custom_call" | custom-call | tf_op jit(solution)/shard_map/feed_back_sums/pallas_call | solution.py:890
  291.1 108.2 %mix_back_sums.1 = (bf16[320,1024]{1,0:T(8,128)(2,1)}, f32[1,1024]{1,0:T(1,128)}, bf16[4,848,256]{2,1,0:T(8,128)(2,1)}, f32[4,16,256]{2,1,0:T(8,128)}, f32[4,256]{1,0:T(4,128)}, /*index=5*/f32[768,128]{1,0:T(8,128)}) custom-call(bf16[640,1024]{1,0:T(8,128)(2,1)} %get-tuple-element.79.refs_0_, bf16[320,1024]{1,0:T(8,128)(2,1)} %get-tuple-element.80.refs_1_, ...), custom_call_target="tpu_custom_call" | custom-call | tf_op jit(solution)/shard_map/mix_back_sums/pallas_call | solution.py:890
  399.3 43.2 %reduce_grads.1 = (f32[2,1616,128]{2,1,0:T(8,128)}, f32[4,128,128]{2,1,0:T(8,128)}, f32[2,80,256]{2,1,0:T(8,128)}, bf16[2,160,1024]{2,1,0:T(8,128)(2,1)}) custom-call(f32[768,128]{1,0:T(8,128)} %get-tuple-element.90.feed, bf16[4,848,256]{2,1,0:T(8,128)(2,1)} %get-tuple-element.91.sums, f32[4,16,256]{2,1,0:T(8,128)} %get-tuple-element.92.heads_ref, ...), custom_call_target="tpu_custom_call" | custom-call | tf_op jit(solution)/shard_map/reduce_grads/pallas_call | solution.py:110
  442.6 5.9 %finish.1 = (f32[2,160,1024]{2,1,0:T(8,128)}, f32[2,160,1024]{2,1,0:T(8,128)}, f32[1,16]{1,0:T(1,128)}, f32[64,2,384]{2,1,0:T(2,128)}, f32[16,256]{1,0:T(8,128)}...) custom-call(f32[2,1616,128]{2,1,0:T(8,128)} %get-tuple-element.97.re, ...), custom_call_target="tpu_custom_call" | custom-call | tf_op jit(solution)/shard_map/finish/pallas_call | solution.py:890
  448.5 1.4 copy.41
  449.9 1.5 copy.43
  451.5 1.7 copy.42
  453.1 1.7 copy.44
Async XLA Ops:
  0.7 0.7 copy-start
  0.7 10.8 %copy-start.2 = (bf16[1,1024,2,384]{3,2,1,0:T(2,128)(2,1)S(1)}, bf16[1,1024,2,384]{3,2,1,0:T(2,128)(2,1)}, u32[]{:S(2)}) copy-start(bf16[1,1024,2,384]{3,2,1,0:T(2,128)(2,1)} %param.21) | copy-start | bytes 4718596
  11.5 2.2 copy-start.1
